TPU v7x, 32 devices: a whole 2x2x4 slice. The times are simulated.
32 devices in a mesh: kv: 4 (over y, x), seq: 8 (over z, core).
Axes of the slice: x: 2, y: 2, z: 4, core: 2. Of those that a mesh axis runs over, the one named last changes fastest.
Arguments:
- page_cache: bfloat16 [512, 2, 8, 128, 128], P('seq', None, 'kv'), may hold values from -9 to 64
- keep_list: int32 [512, 128], P('seq'), may hold values from 0 to 1, as said below
- fold_weight: float32 [512, 128], P('seq'), may hold values from 0.1 to 10
- page_table: int32 [64, 8], replicated, may hold values from 0 to 511, as said below
- lengths: int32 [64], replicated, may hold values from 1 to 1024, 40960 in all
- queries: bfloat16 [64, 16, 128], P('seq', 'kv'), may hold values from -6 to 40
- fresh_entries: bfloat16 [64, 2, 8, 128], P('seq', None, 'kv'), may hold values from -6 to 6
- out_weight: bfloat16 [2048, 2048], P('kv'), may hold values from -0.125 to 0.125
Outputs:
- packed_cache: bfloat16 [512, 2, 8, 128, 128], P('seq', None, 'kv')
- packed_mass: bfloat16 [512, 128], P('seq')
- attended: bfloat16 [64, 2048], P('seq', 'kv')
- projected: bfloat16 [64, 2048], P('seq', 'kv')
Inputs may be any that keep to these rules, and one draw needn't show every extreme that they name: `page_table`: every physical page appears exactly once. Of the 64 pages of the requests held by one index of seq, exactly 8 lie on each index of seq. `keep_list`: every page keeps at least one and drops at least one of its 128 slots.
All inputs are finite; a program needn't handle non-finite values.
Results may differ from a plain program's by a relative error of at most 0.015.
Values may be sent and summed in bfloat16 or wider, within the bound.
No kernel may reach another device: no remote copies, remote signals or barrier semaphores. Data moves between devices by JAX's collectives and lax.ppermute only.
A program may use at most 128 MiB of HBM per device.

v0:
```python
import jax
import jax.numpy as jnp
from jax import lax
from jax.sharding import PartitionSpec as P

negative_floor = -1e30


def compact_pages(page_cache, keep_list, fold_weight, valid_count):
    slot_count = keep_list.shape[1]
    slot_index = jnp.arange(slot_count, dtype=jnp.int32)
    valid = slot_index[None, :] < valid_count[:, None]
    kept_mask = jnp.logical_and(valid, keep_list > 0)
    dropped = jnp.logical_and(valid, keep_list == 0)
    kept_flag = kept_mask.astype(jnp.int32)
    position = jnp.cumsum(kept_flag, axis=1) - kept_flag
    total_kept = jnp.sum(kept_flag, axis=1)
    selector = jnp.logical_and(
        position[:, None, :] == slot_index[None, :, None], kept_mask[:, None, :]
    ).astype(jnp.bfloat16)
    moved = jnp.einsum(
        "pst,pchtd->pchsd", selector, page_cache, preferred_element_type=jnp.float32
    ).astype(jnp.bfloat16)
    dropped_weight = jnp.where(dropped, fold_weight, 0.0)
    weight_sum = jnp.sum(dropped_weight, axis=1)
    folded = jnp.einsum(
        "pt,pchtd->pchd",
        dropped_weight,
        page_cache.astype(jnp.float32),
        precision=lax.Precision.HIGHEST,
    )
    folded = (folded / jnp.maximum(weight_sum, 1.0)[:, None, None, None]).astype(jnp.bfloat16)
    at_fold = slot_index[None, :] == total_kept[:, None]
    packed = jnp.where(at_fold[:, None, None, :, None], folded[:, :, :, None, :], moved)
    page_mass = jnp.where(
        slot_index[None, :] < total_kept[:, None], 1.0, jnp.where(at_fold, weight_sum[:, None], 0.0)
    ).astype(jnp.bfloat16)
    return (packed, page_mass)


def page_partials(query_pages, pages, page_mass, score_scale):
    scores = (
        jnp.einsum("phgd,phtd->phgt", query_pages, pages[:, 0], preferred_element_type=jnp.float32)
        * score_scale
    )
    live_mask = (page_mass > 0)[:, None, None, :]
    page_top = jnp.max(jnp.where(live_mask, scores, negative_floor), axis=-1)
    weights = jnp.where(
        live_mask,
        page_mass.astype(jnp.float32)[:, None, None, :] * jnp.exp(scores - page_top[..., None]),
        0.0,
    )
    page_total = jnp.sum(weights, axis=-1)
    page_part = jnp.einsum(
        "phgt,phtd->phgd",
        weights.astype(jnp.bfloat16),
        pages[:, 1],
        preferred_element_type=jnp.float32,
    )
    return (page_top, page_total, page_part)


def per_device(
    page_cache, keep_list, fold_weight, page_table, lengths, queries, fresh_entries, out_weight
):
    seq_count = lax.axis_size("seq")
    seq_rank = lax.axis_index("seq")
    pages_dev = page_cache.shape[0]
    peer_pages = pages_dev // seq_count
    req_dev = queries.shape[0]
    max_pages = page_table.shape[1]
    slot_count = keep_list.shape[1]
    kv_local = page_cache.shape[2]
    head_size = queries.shape[2]
    groups = queries.shape[1] // kv_local
    score_scale = head_size ** (-0.5)
    table_flat = page_table.reshape(-1)
    all_pages = table_flat.shape[0]
    holder = (table_flat // pages_dev).reshape(seq_count, pages_dev)
    earlier = jnp.arange(pages_dev)[None, :] < jnp.arange(pages_dev)[:, None]
    within = jnp.sum(
        jnp.logical_and(holder[:, :, None] == holder[:, None, :], earlier[None]), axis=2
    )
    slot_rows = (holder * peer_pages + within).reshape(-1)
    within_flat = within.reshape(-1)
    logical = (
        jnp.zeros((all_pages,), jnp.int32)
        .at[table_flat]
        .set(jnp.arange(all_pages, dtype=jnp.int32))
    )
    mine_logical = lax.dynamic_slice_in_dim(logical, seq_rank * pages_dev, pages_dev)
    owner = mine_logical // pages_dev
    send_row = owner * peer_pages + within_flat[mine_logical]
    send_order = jnp.argsort(send_row)
    request = mine_logical // max_pages
    valid_count = jnp.clip(lengths[request] - mine_logical % max_pages * slot_count, 0, slot_count)
    packed, page_mass = compact_pages(page_cache, keep_list, fold_weight, valid_count)
    own_rows = lax.dynamic_slice_in_dim(slot_rows, seq_rank * pages_dev, pages_dev)
    query_groups = queries.reshape(req_dev, kv_local, groups, head_size)
    query_pages = jnp.broadcast_to(
        query_groups[:, None], (req_dev, max_pages, kv_local, groups, head_size)
    ).reshape(pages_dev, kv_local, groups, head_size)
    moved, moved_mass = (
        lax.all_to_all(packed[send_order], "seq", split_axis=0, concat_axis=0, tiled=True),
        lax.all_to_all(page_mass[send_order], "seq", split_axis=0, concat_axis=0, tiled=True),
    )
    page_top, page_total, page_part = page_partials(
        query_pages, moved[own_rows], moved_mass[own_rows], score_scale
    )
    page_top = page_top.reshape(req_dev, max_pages, kv_local, groups)
    page_total = page_total.reshape(req_dev, max_pages, kv_local, groups)
    page_part = page_part.reshape(req_dev, max_pages, kv_local, groups, head_size)
    own_score = (
        jnp.einsum(
            "rhgd,rhd->rhg", query_groups, fresh_entries[:, 0], preferred_element_type=jnp.float32
        )
        * score_scale
    )
    best_score = jnp.maximum(jnp.max(page_top, axis=1), own_score)
    factor = jnp.exp(page_top - best_score[:, None])
    own_factor = jnp.exp(own_score - best_score)
    denominator = jnp.sum(factor * page_total, axis=1) + own_factor
    fresh_value = fresh_entries[:, 1].astype(jnp.float32)
    numerator = (
        jnp.sum(factor[..., None] * page_part, axis=1)
        + own_factor[..., None] * fresh_value[:, :, None, :]
    )
    attended = (
        (numerator / denominator[..., None])
        .astype(jnp.bfloat16)
        .reshape(req_dev, kv_local * groups * head_size)
    )
    partial_value = jnp.dot(attended, out_weight, preferred_element_type=jnp.float32)
    projected = lax.psum_scatter(
        partial_value.astype(jnp.bfloat16), "kv", scatter_dimension=1, tiled=True
    )
    return (packed, page_mass, attended, projected)


def solution(mesh):
    placed = (
        P("seq", None, "kv", None, None),
        P("seq", None),
        P("seq", None),
        P(),
        P(),
        P("seq", "kv", None),
        P("seq", None, "kv", None),
        P("kv", None),
    )
    return jax.shard_map(
        per_device,
        mesh=mesh,
        in_specs=placed,
        out_specs=(
            P("seq", None, "kv", None, None),
            P("seq", None),
            P("seq", "kv"),
            P("seq", "kv"),
        ),
        check_vma=False,
    )
```

profile of v0, /device:TPU:0, one launch (start us, length us, event | category | flops | bytes accessed | tf_op | source)
XLA Modules:
  0.0 283.5 jit_solution(18272947098219555300)
XLA Ops:
  7.2 0.9 copy.22
  8.3 2.4 scatter_custom_fusion
  10.9 0.3 convert_reduce_fusion
  11.3 0.8 gather_fusion.1
  12.1 1.4 gather_fusion
  13.5 0.8 fusion.28
  14.4 0.3 reduce_window_sum.11
  14.7 1.0 fusion.30
  15.6 2.0 sort.17
  17.9 1.2 gather_fusion.2
  19.1 6.3 %all-to-all-start = ((bf16[8,8,128]{2,1,0:T(8,128)(2,1)}), bf16[8,8,128]{2,1,0:T(8,128)(2,1)S(1)}, u32[]{:S(2)}, u32[]{:S(2)}) async-start(bf16[8,8,128]{2,1,0:T(8,128)(2,1)} %bitcast.8), calls=%async_computation | async-start | bytes 32768 | tf_op jit(solution)/shard_map/all_to_all | solution.py:105
  25.6 6.5 %fusion.32 = f32[64,1,2,2,128]{4,1,3,2,0:T(1,128)S(1)} fusion(f32[64,128,1,1,1]{1,2,4,3,0:T(1,128)S(1)} %bitcast.62, bf16[64,2,2,128,128]{4,3,2,1,0:T(8,128)(2,1)} %param.8), kind=kOutput, calls=%fused_computation.93 | convolution fusion | flops 50331648 | bytes 8552448 | tf_op jit(solution)/shard_map/pt,pchtd->pchd/dot_general | solution.py:26
  32.1 0.1 divide_convert_fusion
  32.3 4.8 %select_bitcast_fusion = bf16[64,2,2,128,128]{4,3,2,1,0:T(8,128)(2,1)} fusion(pred[64,128]{1,0:T(8,128)(4,1)S(1)} %iota_compare_fusion.4, bf16[64,2,2,128,128]{4,3,2,1,0:T(8,128)(2,1)S(1)} %copy-done.1, bf16[64,2,2,128]{3,2,1,0:T(2,128)(2,1)S(1)} %divide_convert_fusion, s32[64,128]{1,0:T(8,128)S(1)} %get-tuple-element.18, ...), kind=kOutput, calls=%fused_computation.7 | convolution fusion | flops 1084227584 | bytes 16891904 | tf_op jit(solution)/shard_map/pst,pchtd->pchsd/dot_general | solution.py:21
  37.0 8.9 %gather_fusion.4 = bf16[64,2,2,128,128]{4,3,2,1,0:T(8,128)(2,1)} fusion(bf16[64,2,2,128,128]{4,3,2,1,0:T(8,128)(2,1)} %select_bitcast_fusion, s32[1024]{0:T(1024)S(1)} %pad_clamp_fusion.1), kind=kCustom, calls=%fused_computation.4 | custom fusion | bytes 16777472 | tf_op jit(solution)/shard_map/gather | solution.py:104
  46.0 5.2 %all-to-all-start.1 = ((bf16[64,2,2,128,128]{4,3,2,1,0:T(8,128)(2,1)}), bf16[64,2,2,128,128]{4,3,2,1,0:T(8,128)(2,1)}, u32[]{:S(2)}, u32[]{:S(2)}) async-start(bf16[64,2,2,128,128]{4,3,2,1,0:T(8,128)(2,1)} %gather_fusion.4), calls=%async_computation.1 | async-start | bytes 16777216 | tf_op jit(solution)/shard_map/all_to_all | solution.py:104
  51.6 0.7 gather_fusion.3
  52.3 182.9 %all-to-all-done.1 = bf16[64,2,2,128,128]{4,3,2,1,0:T(8,128)(2,1)} async-done(((bf16[64,2,2,128,128]{4,3,2,1,0:T(8,128)(2,1)}), bf16[64,2,2,128,128]{4,3,2,1,0:T(8,128)(2,1)}, u32[]{:S(2)}, u32[]{:S(2)}) %all-to-all-start.1) | async-done | bytes 8388640 | tf_op jit(solution)/shard_map/all_to_all | solution.py:104
  235.2 8.9 %gather_fusion.5 = bf16[64,2,2,128,128]{4,3,2,1,0:T(8,128)(2,1)} fusion(bf16[64,2,2,128,128]{4,3,2,1,0:T(8,128)(2,1)} %all-to-all-done.1, s32[1024]{0:T(1024)S(1)} %pad_clamp_fusion), kind=kCustom, calls=%fused_computation.5 | custom fusion | bytes 16777472 | tf_op jit(solution)/shard_map/gather | solution.py:108
  244.1 4.6 %select_reduce_fusion = (f32[64,2,2]{2,1,0:T(2,128)S(1)}, f32[64,2,128,2]{2,3,1,0:T(2,128)S(1)}) fusion(pred[64,128]{1,0:T(8,128)(4,1)S(1)} %broadcast_compare_fusion, bf16[64,2,2,128]{3,2,1,0:T(2,128)(2,1)S(1)} %bitcast.63, bf16[64,2,2,128,128]{4,3,2,1,0:T(8,128)(2,1)} %gather_fusion.5), kind=kOutput, calls=%fused_computation.24 | convolution fusion | flops 8486656 | bytes 4400128 | tf_op jit(solution)/shard_map/phgd,phtd->phgt/dot_general | solution.py:43
  248.8 0.4 bitcast_reduce_fusion
  249.4 3.5 %multiply_reduce_fusion = f32[8,2,2,128]{3,2,1,0:T(2,128)S(1)} fusion(f32[8,8,2,2]{3,2,1,0:T(2,128)S(1)} %get-tuple-element.9, bf16[64,2,2,128,128]{4,3,2,1,0:T(8,128)(2,1)} %gather_fusion.5, f32[64,2,128,2]{2,3,1,0:T(2,128)S(1)} %get-tuple-element.23, f32[64,2,2]{2,1,0:T(2,128)S(1)} %get-tuple-element.22, f32[64,128]{1,0:T(8,128)S(1)} %convert_element_type.53, ...), kind=kOutput, calls=%fused_computation.22 | convolution fusion | flops 8581120 | bytes 4384768 | tf_op jit(solution)/shard_map/phgt,phtd->phgd/dot_general | solution.py:54
  253.0 1.0 convolution_convert_fusion
  254.0 22.6 %reduce-scatter.2.cloned.1.call-done = bf16[8,512]{1,0:T(8,128)(2,1)} async-done(((bf16[8,2048]{1,0:T(8,128)(2,1)}), bf16[8,512]{1,0:T(8,128)(2,1)}) %reduce-scatter.2.cloned.1.call-update) | async-done | bytes 8208 | tf_op jit(solution)/shard_map/reduce_scatter | solution.py:134
  (49 shorter events, 1.4 us)
Async XLA Ops:
  7.2 245.8 %copy-start = (bf16[512,2048]{1,0:T(8,128)(2,1)S(1)}, bf16[512,2048]{1,0:T(8,128)(2,1)}, u32[]{:S(2)}) copy-start(bf16[512,2048]{1,0:T(8,128)(2,1)} %param.15) | copy-start | bytes 6291460
  17.9 19.1 %copy-start.2 = (bf16[64,128]{1,0:T(8,128)(2,1)}, bf16[64,128]{1,0:T(8,128)(2,1)S(1)}, u32[]{:S(2)}) copy-start(bf16[64,128]{1,0:T(8,128)(2,1)S(1)} %select_convert_fusion) | copy-start | bytes 49156
  19.1 26.8 %all-to-all-start = ((bf16[8,8,128]{2,1,0:T(8,128)(2,1)}), bf16[8,8,128]{2,1,0:T(8,128)(2,1)S(1)}, u32[]{:S(2)}, u32[]{:S(2)}) async-start(bf16[8,8,128]{2,1,0:T(8,128)(2,1)} %bitcast.8), calls=%async_computation | async-start | bytes 32768 | tf_op jit(solution)/shard_map/all_to_all | solution.py:105
  25.5 6.8 %copy-start.1 = (bf16[64,2,2,128,128]{4,3,2,1,0:T(8,128)(2,1)S(1)}, bf16[64,2,2,128,128]{4,3,2,1,0:T(8,128)(2,1)}, u32[]{:S(2)}) copy-start(bf16[64,2,2,128,128]{4,3,2,1,0:T(8,128)(2,1)} %param.8) | copy-start | bytes 25165828
  45.9 5.5 %copy-start.5 = (bf16[8,2,2,128]{3,2,1,0:T(2,128)(2,1)S(1)}, bf16[8,2,2,128]{3,2,1,0:T(2,128)(2,1)}, u32[]{:S(2)}) copy-start(bf16[8,2,2,128]{3,2,1,0:T(2,128)(2,1)} %param.14) | copy-start | bytes 24580
  45.9 5.5 %copy-start.4 = (bf16[8,4,128]{2,1,0:T(4,128)(2,1)S(1)}, bf16[8,4,128]{2,1,0:T(4,128)(2,1)}, u32[]{:S(2)}) copy-start(bf16[8,4,128]{2,1,0:T(4,128)(2,1)} %param.13) | copy-start | bytes 24580
  46.0 189.2 %all-to-all-start.1 = ((bf16[64,2,2,128,128]{4,3,2,1,0:T(8,128)(2,1)}), bf16[64,2,2,128,128]{4,3,2,1,0:T(8,128)(2,1)}, u32[]{:S(2)}, u32[]{:S(2)}) async-start(bf16[64,2,2,128,128]{4,3,2,1,0:T(8,128)(2,1)} %gather_fusion.4), calls=%async_computation.1 | async-start | bytes 16777216 | tf_op jit(solution)/shard_map/all_to_all | solution.py:104
  51.2 225.5 %reduce-scatter.2.cloned.1.call-start = ((), (), s32[]{:S(2)}) async-start(), calls=%async_computation.3 | async-start | bytes 40960 | tf_op jit(solution)/shard_map/reduce_scatter | solution.py:134
  253.0 23.7 %copy-start.3 = (bf16[8,512]{1,0:T(8,128)(2,1)}, bf16[8,512]{1,0:T(8,128)(2,1)S(1)}, u32[]{:S(2)}) copy-start(bf16[8,512]{1,0:T(8,128)(2,1)S(1)} %convert_element_type.58) | copy-start | bytes 24580
Sparse Core Ops, SparseCore 0:
  254.1 22.4 reduce-scatter.1
where the time goes:
time: 284 us
  waiting for transfers between devices  206 us (73%)
  local copies, waits for them, and re-layouts  25.7 us (9%)
  matrix products  20.5 us (7%)
  between operations  14.3 us (5%)
  starting transfers between devices  11.6 us (4%)
  other arithmetic  5.84 us (2%)
    all_to_all x1, waiting for transfers between devices, per_device(): lax.all_to_all(packed[send_order], 'seq', split_axis=0, concat_axis=0, ti...  183 us
    reduce_scatter x1, waiting for transfers between devices, per_device(): lax.psum_scatter(partial_value.astype(jnp.bfloat16), 'kv', scatter_dimens...  22.6 us
    gather x1, local copies, waits for them, and re-layouts, per_device(): packed[send_order]  8.9 us
    gather x1, local copies, waits for them, and re-layouts, per_device(): moved[own_rows]  8.9 us
    dot_general x1, matrix products, compact_pages(): jnp.einsum('pt,pchtd->pchd', dropped_weight, page_cache.astype(jnp.float3...  6.53 us
    all_to_all x1, starting transfers between devices, per_device(): lax.all_to_all(page_mass[send_order], 'seq', split_axis=0, concat_axis=0,...  6.33 us
  transfers between devices with their start and end apart: 3, of which 2 were waited for; matrix products, arithmetic and copies ran while one was open for 8% of the time, Pallas kernels for 0%

commit v1 on v0

v1 whole, which is shorter than its diff:
```python
import functools

import jax
import jax.numpy as jnp
from jax import lax
from jax.experimental import pallas as pl
from jax.experimental.pallas import tpu as pltpu
from jax.sharding import PartitionSpec as P

negative_floor = -1e30
f32 = jnp.float32
bf16 = jnp.bfloat16
i32 = jnp.int32


def iota(shape, dim):
    return lax.broadcasted_iota(i32, shape, dim)


def dot(a, b, contract=(1, 0)):
    return lax.dot_general(
        a, b, (((contract[0],), (contract[1],)), ((), ())), preferred_element_type=f32
    )


def pieces(x):
    high = x.astype(bf16)
    rest = x - high.astype(f32)
    middle = rest.astype(bf16)
    low = (rest - middle.astype(f32)).astype(bf16)
    return high, middle, low


def ones_where(mask):
    return jnp.where(mask, 1.0, 0.0).astype(bf16)


def compact_kernel(
    heads, req_dev, base_ref, table_ref, lengths_ref, keep_ref, weight_ref, pages_ref,
    packed_ref, mass_ref, kept_ref, fold_mass_ref, folded_ref, request_ref, slot_ref,
    position_ref, count_ref, share_ref,
):
    step = pl.program_id(0)
    group = pages_ref.shape[0]
    pages_dev, slots = keep_ref.shape
    reqs, max_pages = table_ref.shape

    @pl.when(step == 0)
    def _():
        base = base_ref[0]
        diagonal = iota((reqs, reqs), 0) == iota((reqs, reqs), 1)
        lengths = jnp.sum(
            jnp.where(diagonal, jnp.broadcast_to(lengths_ref[...], (reqs, reqs)), 0),
            axis=1, keepdims=True,
        )
        page_id = iota((reqs, pages_dev), 1) + base
        valid = jnp.zeros((reqs, pages_dev), i32)
        owns = jnp.zeros((reqs, pages_dev), i32)
        for j in range(max_pages):
            match = table_ref[:, j : j + 1] == page_id
            left = jnp.clip(lengths - j * slots, 0, slots)
            valid = valid + jnp.where(match, left, 0)
            owns = owns + jnp.where(match, 1, 0)
        valid_count = dot(valid.astype(f32).astype(bf16), jnp.ones((reqs, slots), bf16), (0, 0))
        owns_f = owns.astype(f32)
        owns_b = owns_f.astype(bf16)
        request = dot(owns_b, iota((reqs, slots), 0).astype(f32).astype(bf16), (0, 0))
        slot_index = iota((pages_dev, slots), 1).astype(f32)
        in_page = slot_index < valid_count
        kept = jnp.logical_and(in_page, keep_ref[...] > 0)
        dropped = jnp.logical_and(in_page, keep_ref[...] == 0)
        kept_f = jnp.where(kept, 1.0, 0.0)
        before = ones_where(iota((slots, slots), 0) < iota((slots, slots), 1))
        position = dot(kept_f.astype(bf16), before)
        count = jnp.sum(kept_f, axis=1, keepdims=True)
        dropped_weight = jnp.where(dropped, weight_ref[...], 0.0)
        weight_sum = jnp.sum(dropped_weight, axis=1, keepdims=True)
        mass = jnp.where(
            slot_index < count, 1.0, jnp.where(slot_index == count, weight_sum, 0.0)
        ).astype(bf16)
        mass_ref[...] = mass
        kept_ref[...] = kept_f
        fold_mass_ref[...] = jnp.broadcast_to(
            weight_sum.astype(bf16).astype(f32), (pages_dev, slots)
        )
        position_ref[...] = jnp.where(kept, position, -1.0)
        count_ref[...] = jnp.broadcast_to(count, (pages_dev, slots))
        share = pieces(dropped_weight / jnp.maximum(weight_sum, 1.0))
        for n in range(3):
            share_ref[n] = share[n].astype(f32)
        rows = pages_dev * heads
        spread = ones_where(iota((rows, pages_dev), 0) // heads == iota((rows, pages_dev), 1))
        request_ref[...] = dot(spread, request.astype(bf16))
        owner_of = (iota((reqs, slots), 0) // req_dev).astype(f32)
        owner_col = dot(owns_b, owner_of.astype(bf16), (0, 0))[:, :pages_dev]
        owner_row = jnp.sum(owns_f * owner_of[:, :pages_dev], axis=0, keepdims=True)
        earlier = jnp.logical_and(
            owner_col == owner_row, iota((pages_dev, pages_dev), 0) < iota((pages_dev, pages_dev), 1)
        )
        rank = jnp.sum(jnp.where(earlier, 1.0, 0.0), axis=0, keepdims=True)
        per_owner = pages_dev // (reqs // req_dev)
        slot = jnp.broadcast_to(owner_row * per_owner + rank, (8, pages_dev)).astype(bf16)
        slot_ref[...] = dot(slot, spread, (1, 1))

    row = iota((slots, slots), 0).astype(f32)
    tile_row = iota((16, slots), 0)
    for i in range(group):
        page = step * group + i
        selector = ones_where(row == position_ref[pl.ds(page, 1), :])
        shares = jnp.zeros((16, slots), f32)
        for n in range(3):
            shares = jnp.where(tile_row == n, share_ref[n, pl.ds(page, 1), :], shares)
        left = jnp.concatenate([selector, shares.astype(bf16)], axis=0)
        at_fold = row == count_ref[pl.ds(page, 1), :]
        for c in range(2):
            kv_local = pages_ref.shape[2]
            right = jnp.concatenate([pages_ref[i, c, g] for g in range(kv_local)], axis=1)
            result = dot(left, right)
            folded = jnp.sum(result[slots : slots + 8], axis=0, keepdims=True)
            folded = folded.astype(bf16).astype(f32)
            for g in range(kv_local):
                part = slice(g * 128, (g + 1) * 128)
                folded_ref[c, g, pl.ds(page, 1), :] = folded[:, part]
                packed_ref[i, c, g] = jnp.where(
                    at_fold, folded[:, part], result[:slots, part]
                ).astype(bf16)


def compact(base, page_table, lengths, keep_list, fold_weight, page_cache, heads, req_dev, group):
    pages_dev, _, kv_local, slots, head_size = page_cache.shape
    rows = pages_dev * heads
    whole = lambda *shape: pl.BlockSpec(shape, lambda s: (0,) * len(shape))
    paged = pl.BlockSpec((group, 2, kv_local, slots, head_size), lambda s: (s, 0, 0, 0, 0))
    small = (pages_dev, slots)
    fold = (2, kv_local, pages_dev, head_size)
    return pl.pallas_call(
        functools.partial(compact_kernel, heads, req_dev),
        grid=(pages_dev // group,),
        in_specs=[
            pl.BlockSpec(memory_space=pltpu.SMEM),
            whole(*page_table.shape),
            whole(1, lengths.shape[0]),
            whole(*small),
            whole(*small),
            paged,
        ],
        out_specs=[
            paged, whole(*small), whole(*small), whole(*small), whole(*fold),
            whole(rows, slots), whole(8, rows),
        ],
        out_shape=[
            jax.ShapeDtypeStruct(page_cache.shape, bf16),
            jax.ShapeDtypeStruct(small, bf16),
            jax.ShapeDtypeStruct(small, f32),
            jax.ShapeDtypeStruct(small, f32),
            jax.ShapeDtypeStruct(fold, f32),
            jax.ShapeDtypeStruct((rows, slots), f32),
            jax.ShapeDtypeStruct((8, rows), f32),
        ],
        scratch_shapes=[
            pltpu.VMEM(small, f32),
            pltpu.VMEM(small, f32),
            pltpu.VMEM((3,) + small, f32),
        ],
        compiler_params=pltpu.CompilerParams(vmem_limit_bytes=40 << 20),
        cost_estimate=pl.CostEstimate(
            flops=2 * pages_dev * slots * slots * 2 * kv_local * head_size,
            bytes_accessed=4 * page_cache.size, transcendentals=0,
        ),
        name="compact",
    )(base, page_table, lengths.reshape(1, -1), keep_list, fold_weight, page_cache)


def attend_kernel(
    heads, score_scale, chunk, query_ref, kept_ref, fold_mass_ref, folded_ref, request_ref, slot_ref,
    pages_ref, out_ref, keys, values, scores, parts, key_sem, value_sem,
):
    pages_dev, slots = kept_ref.shape
    kv_local = folded_ref.shape[1]
    groups = heads // kv_local
    rows = pages_dev * heads
    copies = []
    for c, (buffer, sem) in enumerate(((keys, key_sem), (values, value_sem))):
        for n in range(pages_dev // chunk):
            span = pl.ds(n * chunk, chunk)
            copies.append(
                pltpu.make_async_copy(pages_ref.at[span, c], buffer.at[span], sem.at[n])
            )
    for copy in copies:
        copy.start()
    key_copies, value_copies = copies[: len(copies) // 2], copies[len(copies) // 2 :]

    all_rows = query_ref.shape[0]
    target = request_ref[...] * heads + (iota((rows, slots), 0) % heads).astype(f32)
    query = jnp.zeros((rows, 128), f32)
    for n in range(all_rows // slots):
        pick = ones_where(target == (iota((rows, slots), 1) + n * slots).astype(f32))
        query = query + dot(pick, query_ref[n * slots : (n + 1) * slots])
    query_b = query.astype(bf16)

    tile = 16
    tile_pages = tile // heads
    row = iota((tile, 128), 0)
    row_page = row // heads
    row_group = (row % heads) // groups

    def choose(results):
        chosen = None
        for i in range(tile_pages):
            for g in range(kv_local):
                piece = results[i][:, g * 128 : (g + 1) * 128]
                if chosen is None:
                    chosen = piece
                else:
                    here = jnp.logical_and(row_page == i, row_group == g)
                    chosen = jnp.where(here, piece, chosen)
        return chosen

    for n in range(pages_dev // chunk):
        key_copies[n].wait()
        for m in range(chunk // tile_pages):
            first = n * chunk + m * tile_pages
            at = first * heads
            left = query_b[at : at + tile]
            results = [
                dot(left, keys[first + i].reshape(kv_local * slots, 128), (1, 1))
                for i in range(tile_pages)
            ]
            scores[at : at + tile, :] = choose(results)

    spread = ones_where(iota((rows, pages_dev), 0) // heads == iota((rows, pages_dev), 1))
    group_of = (iota((rows, pages_dev), 0) % heads) // groups
    kept = dot(spread, kept_ref[...].astype(bf16)) > 0.5
    fold_mass = dot(spread, fold_mass_ref[...].astype(bf16))[:, :1]
    fold_key = jnp.zeros((rows, 128), f32)
    fold_value = jnp.zeros((rows, 128), f32)
    for g in range(kv_local):
        spread_g = jnp.where(group_of == g, spread.astype(f32), 0.0).astype(bf16)
        fold_key = fold_key + dot(spread_g, folded_ref[0, g].astype(bf16))
        fold_value = fold_value + dot(spread_g, folded_ref[1, g].astype(bf16))
    fold_score = jnp.sum(query * fold_key, axis=1, keepdims=True) * score_scale
    fold_live = fold_mass > 0
    score = jnp.where(kept, scores[...] * score_scale, negative_floor)
    top = jnp.maximum(
        jnp.max(score, axis=1, keepdims=True), jnp.where(fold_live, fold_score, negative_floor)
    )
    weight = jnp.where(kept, jnp.exp(score - top), 0.0)
    fold_weight = jnp.where(fold_live, fold_mass * jnp.exp(fold_score - top), 0.0)
    total = jnp.sum(weight, axis=1, keepdims=True) + fold_weight
    weight_b = weight.astype(bf16)

    for n in range(pages_dev // chunk):
        value_copies[n].wait()
        for m in range(chunk // tile_pages):
            first = n * chunk + m * tile_pages
            at = first * heads
            left = weight_b[at : at + tile]
            results = [
                dot(left, jnp.concatenate([values[first + i, g] for g in range(kv_local)], axis=1))
                for i in range(tile_pages)
            ]
            parts[at : at + tile, :] = choose(results)

    part = parts[...] + fold_weight.astype(bf16).astype(f32) * fold_value
    lane = iota((rows, 128), 1)
    stats = jnp.where(lane == 6, request_ref[...], 0.0)
    for n, piece in enumerate(pieces(top) + pieces(total)):
        stats = jnp.where(lane == n, piece.astype(f32), stats)
    send = jnp.concatenate([part.astype(bf16), stats.astype(bf16)], axis=1)
    place = slot_ref[:1] * heads + (iota((1, rows), 1) % heads).astype(f32)
    move = ones_where(iota((rows, rows), 0).astype(f32) == place)
    out_ref[...] = dot(move, send).astype(bf16)


def attend(queries, kept, fold_mass, folded, request, slot, page_cache, score_scale, heads):
    pages_dev, _, kv_local, slots, head_size = page_cache.shape
    rows = pages_dev * heads
    chunk = 8
    vmem = pl.BlockSpec(memory_space=pltpu.VMEM)
    return pl.pallas_call(
        functools.partial(attend_kernel, heads, score_scale, chunk),
        in_specs=[vmem] * 6 + [pl.BlockSpec(memory_space=pl.ANY)],
        out_specs=vmem,
        out_shape=jax.ShapeDtypeStruct((rows, 2 * head_size), bf16),
        scratch_shapes=[
            pltpu.VMEM((pages_dev, kv_local, slots, head_size), bf16),
            pltpu.VMEM((pages_dev, kv_local, slots, head_size), bf16),
            pltpu.VMEM((rows, slots), f32),
            pltpu.VMEM((rows, head_size), f32),
            pltpu.SemaphoreType.DMA((pages_dev // chunk,)),
            pltpu.SemaphoreType.DMA((pages_dev // chunk,)),
        ],
        compiler_params=pltpu.CompilerParams(vmem_limit_bytes=40 << 20),
        cost_estimate=pl.CostEstimate(
            flops=4 * rows * slots * head_size * 16, bytes_accessed=2 * page_cache.size,
            transcendentals=rows * slots,
        ),
        name="attend",
    )(queries, kept, fold_mass, folded, request, slot, page_cache)


def combine_kernel(
    heads, req_dev, score_scale, kv_count, first_ref, rank_ref, got_ref, query_ref, fresh_key_ref,
    fresh_value_ref, weight_ref, attended_ref, *out_refs
):
    rows = got_ref.shape[0]
    cols = heads * req_dev
    width = weight_ref.shape[1] // kv_count
    stats = got_ref[:, 128:].astype(f32)
    top = stats[:, 0:1] + stats[:, 1:2] + stats[:, 2:3]
    request = stats[:, 6:7] - first_ref[0].astype(f32)
    row_head = (iota((rows, cols), 0) % heads).astype(f32)
    col = iota((rows, cols), 1)
    match = jnp.logical_and(
        request == (col % req_dev).astype(f32), row_head == (col // req_dev).astype(f32)
    )
    own = jnp.sum(
        query_ref[...].astype(f32) * fresh_key_ref[...].astype(f32), axis=1, keepdims=True
    ) * score_scale
    diagonal = iota((cols, cols), 0) == iota((cols, cols), 1)
    own_row = jnp.sum(jnp.where(diagonal, own, 0.0), axis=0, keepdims=True)
    best = jnp.maximum(
        jnp.max(jnp.where(match, top, negative_floor), axis=0, keepdims=True), own_row
    )
    best_col = jnp.sum(jnp.where(diagonal, best, 0.0), axis=1, keepdims=True)
    factor = jnp.where(match, jnp.exp(top - best), 0.0)
    high, middle, low = pieces(factor)
    got = got_ref[...]
    sums = dot(high, got, (0, 0)) + dot(middle, got, (0, 0)) + dot(low, got, (0, 0))
    own_factor = jnp.exp(own - best_col)
    denominator = sums[:, 131:132] + sums[:, 132:133] + sums[:, 133:134] + own_factor
    numerator = sums[:, :128] + own_factor * fresh_value_ref[...].astype(f32)
    attended = numerator / denominator
    attended = jnp.concatenate(
        [attended[h * req_dev : (h + 1) * req_dev] for h in range(heads)], axis=1
    ).astype(bf16)
    attended_ref[...] = attended
    rank = rank_ref[0]
    for k in range(kv_count):
        other = lax.rem(rank + k, kv_count)
        at = pl.multiple_of(other * width, width)
        out_refs[k][...] = dot(attended, weight_ref[:, pl.ds(at, width)]).astype(bf16)


def combine(first, rank, got, query, fresh_key, fresh_value, out_weight, score_scale, heads, kv_count):
    req_dev = query.shape[0] // heads
    vmem = pl.BlockSpec(memory_space=pltpu.VMEM)
    smem = pl.BlockSpec(memory_space=pltpu.SMEM)
    width = out_weight.shape[1] // kv_count
    return pl.pallas_call(
        functools.partial(combine_kernel, heads, req_dev, score_scale, kv_count),
        in_specs=[smem, smem] + [vmem] * 5,
        out_specs=[vmem] * (1 + kv_count),
        out_shape=[jax.ShapeDtypeStruct((req_dev, out_weight.shape[0]), bf16)]
        + [jax.ShapeDtypeStruct((req_dev, width), bf16)] * kv_count,
        compiler_params=pltpu.CompilerParams(vmem_limit_bytes=40 << 20),
        cost_estimate=pl.CostEstimate(
            flops=2 * req_dev * out_weight.size, bytes_accessed=2 * out_weight.size, transcendentals=0
        ),
        name="combine",
    )(first, rank, got, query, fresh_key, fresh_value, out_weight)


def per_device(
    page_cache, keep_list, fold_weight, page_table, lengths, queries, fresh_entries, out_weight
):
    seq_count = lax.axis_size("seq")
    kv_count = lax.axis_size("kv")
    seq_rank = lax.axis_index("seq").astype(i32).reshape(1)
    kv_rank = lax.axis_index("kv").astype(i32).reshape(1)
    pages_dev, _, kv_local, slots, head_size = page_cache.shape
    req_dev, heads, _ = queries.shape
    groups = heads // kv_local
    score_scale = head_size ** (-0.5)

    rows = queries.reshape(req_dev * heads, head_size)
    query_all = lax.all_to_all(
        jnp.broadcast_to(rows[None], (seq_count,) + rows.shape), "seq",
        split_axis=0, concat_axis=0, tiled=True,
    ).reshape(seq_count * req_dev * heads, head_size)
    packed, mass, kept, fold_mass, folded, request, slot = compact(
        seq_rank * pages_dev, page_table, lengths, keep_list, fold_weight, page_cache,
        heads, req_dev, 4,
    )
    send = attend(
        query_all, kept, fold_mass, folded, request, slot, page_cache, score_scale, heads
    )
    got = lax.all_to_all(
        send.reshape(seq_count, -1, send.shape[1]), "seq", split_axis=0, concat_axis=0, tiled=True
    ).reshape(send.shape)
    by_head = lambda x: x.transpose(1, 0, 2).reshape(heads * req_dev, head_size)
    fresh = jnp.repeat(fresh_entries, groups, axis=2)
    attended, *shares = combine(
        seq_rank * req_dev, kv_rank, got, by_head(queries), by_head(fresh[:, 0]),
        by_head(fresh[:, 1]), out_weight, score_scale, heads, kv_count,
    )
    total = shares[0].astype(f32)
    for k in range(1, kv_count):
        moved = lax.ppermute(shares[k], "kv", [(i, (i + k) % kv_count) for i in range(kv_count)])
        total = total + moved.astype(f32)
    return packed, mass, attended, total.astype(bf16)


def solution(mesh):
    placed = (
        P("seq", None, "kv", None, None),
        P("seq", None),
        P("seq", None),
        P(),
        P(),
        P("seq", "kv", None),
        P("seq", None, "kv", None),
        P("kv", None),
    )
    return jax.shard_map(
        per_device,
        mesh=mesh,
        in_specs=placed,
        out_specs=(
            P("seq", None, "kv", None, None),
            P("seq", None),
            P("seq", "kv"),
            P("seq", "kv"),
        ),
        check_vma=False,
    )
```

time: 284 us -> 55.7 us (0.20)
  waiting for transfers between devices: 206 us -> 10.7 us
  matrix products: 20.5 us -> 0 us
  Pallas kernels: 0 us -> 17.1 us
  local copies, waits for them, and re-layouts: 25.7 us -> 11.1 us
  between operations: 14.3 us -> 0.69 us
  other arithmetic: 5.84 us -> 0.61 us
  starting transfers between devices: 11.6 us -> 15 us
    all_to_all x2, waiting for transfers between devices: 183 us -> 6.72 us  [the longest x1 6.72 us: per_device(): lax.all_to_all(send.reshape(seq_count, -1, send.shape[1]), 'seq', split_a...]
    reduce_scatter x1 -> x0, waiting for transfers between devices: 22.6 us -> none  [per_device(): lax.psum_scatter(partial_value.astype(jnp.bfloat16), 'kv', scatter_dimens...]
    gather x6 -> x0, local copies, waits for them, and re-layouts: 21.9 us -> none  [the longest x1 8.9 us: per_device(): packed[send_order]]
    dot_general x6 -> x0, matrix products: 20.5 us -> none  [the longest x1 6.53 us: compact_pages(): jnp.einsum('pt,pchtd->pchd', dropped_weight, page_cache.astype(jnp.float3...]
    pallas_call x0 -> x3, Pallas kernels: none -> 17.1 us  [the longest x1 9.94 us: compact(): pl.pallas_call(functools.partial(compact_kernel, heads, req_dev), grid=(p...]
    unnamed x13 -> x18, local copies, waits for them, and re-layouts: 0.95 us -> 9.72 us
    ppermute x0 -> x3, waiting for transfers between devices: none -> 3.96 us  [per_device(): lax.ppermute(shares[k], 'kv', [(i, (i + k) % kv_count) for i in range(kv_...]
    ppermute x0 -> x3, starting transfers between devices: none -> 3.54 us  [per_device(): lax.ppermute(shares[k], 'kv', [(i, (i + k) % kv_count) for i in range(kv_...]
  transfers between devices with their start and end apart: 3 -> 5, of which waited for: 2 -> 4; matrix products, arithmetic and copies ran while one was open for 8% -> 1% of each run, Pallas kernels for 0% -> 18%
where the time goes in v1:
time: 55.7 us; the launch traced here: 55.1 us
  Pallas kernels  17.1 us (31%)
  starting transfers between devices  15 us (27%)
  local copies, waits for them, and re-layouts  11.1 us (20%)
  waiting for transfers between devices  10.7 us (19%)
  between operations  0.69 us (1%)
  other arithmetic  0.61 us (1%)
    pallas_call x1, Pallas kernels, compact(): pl.pallas_call(functools.partial(compact_kernel, heads, req_dev), grid=(p...  9.94 us
    unnamed x18, local copies, waits for them, and re-layouts  9.72 us
    all_to_all x1, waiting for transfers between devices, per_device(): lax.all_to_all(send.reshape(seq_count, -1, send.shape[1]), 'seq', split_a...  6.72 us
    all_to_all x1, starting transfers between devices, per_device(): lax.all_to_all(jnp.broadcast_to(rows[None], (seq_count,) + rows.shape), '...  6.33 us
    pallas_call x1, Pallas kernels, attend(): pl.pallas_call(functools.partial(attend_kernel, heads, score_scale, chunk...  5.67 us
    all_to_all x1, starting transfers between devices, per_device(): lax.all_to_all(send.reshape(seq_count, -1, send.shape[1]), 'seq', split_a...  5.11 us
    ppermute x3, waiting for transfers between devices, per_device(): lax.ppermute(shares[k], 'kv', [(i, (i + k) % kv_count) for i in range(kv_...  3.96 us
    ppermute x3, starting transfers between devices, per_device(): lax.ppermute(shares[k], 'kv', [(i, (i + k) % kv_count) for i in range(kv_...  3.54 us
  transfers between devices with their start and end apart: 5, of which 4 were waited for; matrix products, arithmetic and copies ran while one was open for 1% of the time, Pallas kernels for 18%

profile of v1, /device:TPU:0, one launch (start us, length us, event | category | flops | bytes accessed | tf_op | source)
XLA Modules:
  0.0 55.1 jit_solution(16492718942382002330)
XLA Ops:
  0.6 1.3 %broadcast_in_dim.11 = bf16[8,32,128]{2,1,0:T(8,128)(2,1)} broadcast(bf16[32,128]{1,0:T(8,128)(2,1)} %bitcast.30), dimensions={1,2} | broadcast | bytes 73728 | tf_op jit(solution)/shard_map/broadcast_in_dim | solution.py:378
  2.0 6.3 %all-to-all-start = ((bf16[8,32,128]{2,1,0:T(8,128)(2,1)}), bf16[8,32,128]{2,1,0:T(8,128)(2,1)S(1)}, u32[]{:S(2)}, u32[]{:S(2)}) async-start(bf16[8,32,128]{2,1,0:T(8,128)(2,1)} %broadcast_in_dim.11), calls=%async_computation | async-start | bytes 131072 | tf_op jit(solution)/shard_map/all_to_all | solution.py:377
  8.3 0.8 %copy.12.table_ref = s32[64,8]{1,0:T(8,128)S(1)} copy(s32[64,8]{0,1:T(8,128)} %param.11) | data formatting | bytes 4096 | tf_op args[3]
  9.1 3.4 %copy-done = bf16[64,2,2,128,128]{4,3,2,1,0:T(8,128)(2,1)S(1)} copy-done((bf16[64,2,2,128,128]{4,3,2,1,0:T(8,128)(2,1)S(1)}, bf16[64,2,2,128,128]{4,3,2,1,0:T(8,128)(2,1)}, u32[]{:S(2)}) %copy-start) | copy-done | bytes 8388632
  12.4 0.8 %copy-done.3 = s32[64,128]{1,0:T(8,128)S(1)} copy-done((s32[64,128]{1,0:T(8,128)S(1)}, s32[64,128]{1,0:T(8,128)}, u32[]{:S(2)}) %copy-start.3) | copy-done | bytes 32792
  13.2 0.8 %copy-done.4 = f32[64,128]{1,0:T(8,128)S(1)} copy-done((f32[64,128]{1,0:T(8,128)S(1)}, f32[64,128]{1,0:T(8,128)}, u32[]{:S(2)}) %copy-start.4) | copy-done | bytes 32792
  14.0 0.7 %copy-done.5 = s32[64]{0:T(128)S(1)} copy-done((s32[64]{0:T(128)S(1)}, s32[64]{0:T(128)}, u32[]{:S(2)}) %copy-start.5) | copy-done | bytes 280
  14.6 9.9 %compact.1 = (bf16[64,2,2,128,128]{4,3,2,1,0:T(8,128)(2,1)}, bf16[64,128]{1,0:T(8,128)(2,1)}, f32[64,128]{1,0:T(8,128)S(1)}, f32[64,128]{1,0:T(8,128)S(1)}, f32[...) custom-call(s32[1]{0:T(128)} %bitcast.base_ref, s32[64,8]{1,0:T(8,128)S(1)} %copy.12.table_ref, ...), custom_call_target="tpu_custom_call" | custom-call | flops 1073741824 | bytes 16777216 | tf_op jit(solution)/shard_map/compact/pallas_call | solution.py:136
  24.6 0.0 all-to-all-done
  24.6 3.4 %copy-done.1 = bf16[64,2,2,128,128]{4,3,2,1,0:T(8,128)(2,1)S(1)} copy-done((bf16[64,2,2,128,128]{4,3,2,1,0:T(8,128)(2,1)S(1)}, bf16[64,2,2,128,128]{4,3,2,1,0:T(8,128)(2,1)}, u32[]{:S(2)}) %copy-start.1) | copy-done | bytes 8388632
  28.0 5.7 %attend.1 = bf16[256,256]{1,0:T(8,128)(2,1)} custom-call(bf16[256,128]{1,0:T(8,128)(2,1)S(1)} %bitcast.26, f32[64,128]{1,0:T(8,128)S(1)} %get-tuple-element.18.kept_ref, f32[64,128]{1,0:T(8,128)S(1)} %get-tuple-element.19.fold_mass_ref, f32[2,2,64,128]{3,2,1,0:T(8,128)S(1)} %get-tuple-element.20.folded_ref, f32[256,128]{1,0:T(8,128)S(1)} %get-tuple-element.21.request_ref, ...), custom_call_target="tpu_custom_call" | custom-call | flops 268435456 | bytes 8388608 | tf_op jit(solution)/shard_map/attend/pallas_call | solution.py:280
  33.6 5.1 %all-to-all-start.1 = ((bf16[8,32,256]{2,1,0:T(8,128)(2,1)}), bf16[8,32,256]{2,1,0:T(8,128)(2,1)S(1)}, u32[]{:S(2)}, u32[]{:S(2)}) async-start(bf16[8,32,256]{2,1,0:T(8,128)(2,1)} %bitcast.6), calls=%async_computation.1 | async-start | bytes 262144 | tf_op jit(solution)/shard_map/all_to_all | solution.py:388
  38.7 0.0 copy-done.6
  38.8 0.0 copy-done.7
  38.8 6.7 %all-to-all-done.1 = bf16[8,32,256]{2,1,0:T(8,128)(2,1)S(1)} async-done(((bf16[8,32,256]{2,1,0:T(8,128)(2,1)}), bf16[8,32,256]{2,1,0:T(8,128)(2,1)S(1)}, u32[]{:S(2)}, u32[]{:S(2)}) %all-to-all-start.1) | async-done | bytes 131104 | tf_op jit(solution)/shard_map/all_to_all | solution.py:388
  45.5 0.0 copy-done.2
  45.5 1.5 %combine.1 = (bf16[8,512]{1,0:T(8,128)(2,1)}, bf16[8,512]{1,0:T(8,128)(2,1)S(1)}, bf16[8,512]{1,0:T(8,128)(2,1)S(1)}, bf16[8,512]{1,0:T(8,128)(2,1)S(1)}, bf16[8,512]{1,0:T(8,128)(2,1)S(1)}) custom-call(s32[1]{0:T(128)} %bitcast.2.first_ref, s32[1]{0:T(128)} %bitcast.3.rank_ref, bf16[256,256]{1,0:T(8,128)(2,1)S(1)} %bitcast.25, ...), custom_call_target="tpu_custom_call" | custom-call | flops 16777216 | bytes 2097152 | tf_op jit(solution)/shard_map/combine/pallas_call | solution.py:350
  47.0 2.4 %collective-permute-start.2 = (bf16[8,512]{1,0:T(8,128)(2,1)S(1)}, bf16[8,512]{1,0:T(8,128)(2,1)S(1)}, u32[]{:S(2)}, u32[]{:S(2)}) collective-permute-start(bf16[8,512]{1,0:T(8,128)(2,1)S(1)} %get-tuple-element.27), channel_id=1, source_target_pairs={{0,24},{8,0},{16,8},{24,16},{1,25},{9,1},{17,9},{25,17},{2,26},{10... | collective-permute-start | bytes 24584 | tf_op jit(solution)/shard_map/ppermute | solution.py:399
  49.5 0.5 collective-permute-start.1
  50.0 0.6 %collective-permute-start = (bf16[8,512]{1,0:T(8,128)(2,1)S(1)}, bf16[8,512]{1,0:T(8,128)(2,1)S(1)}, u32[]{:S(2)}, u32[]{:S(2)}) collective-permute-start(bf16[8,512]{1,0:T(8,128)(2,1)S(1)} %get-tuple-element.25), channel_id=1, source_target_pairs={{0,8},{8,16},{16,24},{24,0},{1,9},{9,17},{17,25},{25,1},{2,10},{10... | collective-permute-start | bytes 24584 | tf_op jit(solution)/shard_map/ppermute | solution.py:399
  50.6 0.3 collective-permute-done.2
  50.8 2.3 %collective-permute-done.1 = bf16[8,512]{1,0:T(8,128)(2,1)S(1)} collective-permute-done((bf16[8,512]{1,0:T(8,128)(2,1)S(1)}, bf16[8,512]{1,0:T(8,128)(2,1)S(1)}, u32[]{:S(2)}, u32[]{:S(2)}) %collective-permute-start.1) | collective-permute-done | bytes 8224 | tf_op jit(solution)/shard_map/ppermute | solution.py:399
  53.1 1.4 %collective-permute-done = bf16[8,512]{1,0:T(8,128)(2,1)S(1)} collective-permute-done((bf16[8,512]{1,0:T(8,128)(2,1)S(1)}, bf16[8,512]{1,0:T(8,128)(2,1)S(1)}, u32[]{:S(2)}, u32[]{:S(2)}) %collective-permute-start) | collective-permute-done | bytes 8224 | tf_op jit(solution)/shard_map/ppermute | solution.py:399
  54.5 0.6 %add_convert_fusion = bf16[8,512]{1,0:T(8,128)(2,1)} fusion(bf16[8,512]{1,0:T(8,128)(2,1)S(1)} %collective-permute-done.2, bf16[8,512]{1,0:T(8,128)(2,1)S(1)} %collective-permute-done.1, bf16[8,512]{1,0:T(8,128)(2,1)S(1)} %collective-permute-done, bf16[8,512]{1,0:T(8,128)(2,1)S(1)} %get-tuple-element.24), kind=kLoop, calls=%fused_computation | loop fusion | flops 32768 | bytes 40960 | tf_op jit(solution)/shard_map/convert_element_type | solution.py:401
  (12 shorter events, 0.0 us)
Async XLA Ops:
  2.0 22.6 %all-to-all-start = ((bf16[8,32,128]{2,1,0:T(8,128)(2,1)}), bf16[8,32,128]{2,1,0:T(8,128)(2,1)S(1)}, u32[]{:S(2)}, u32[]{:S(2)}) async-start(bf16[8,32,128]{2,1,0:T(8,128)(2,1)} %broadcast_in_dim.11), calls=%async_computation | async-start | bytes 131072 | tf_op jit(solution)/shard_map/all_to_all | solution.py:377
  9.1 3.4 %copy-start = (bf16[64,2,2,128,128]{4,3,2,1,0:T(8,128)(2,1)S(1)}, bf16[64,2,2,128,128]{4,3,2,1,0:T(8,128)(2,1)}, u32[]{:S(2)}) copy-start(bf16[64,2,2,128,128]{4,3,2,1,0:T(8,128)(2,1)} %pages_ref.3) | copy-start | bytes 25165828
  12.4 0.8 %copy-start.3 = (s32[64,128]{1,0:T(8,128)S(1)}, s32[64,128]{1,0:T(8,128)}, u32[]{:S(2)}) copy-start(s32[64,128]{1,0:T(8,128)} %keep_ref.1) | copy-start | bytes 98308
  13.2 0.8 %copy-start.4 = (f32[64,128]{1,0:T(8,128)S(1)}, f32[64,128]{1,0:T(8,128)}, u32[]{:S(2)}) copy-start(f32[64,128]{1,0:T(8,128)} %weight_ref.2) | copy-start | bytes 98308
  14.0 0.7 %copy-start.5 = (s32[64]{0:T(128)S(1)}, s32[64]{0:T(128)}, u32[]{:S(2)}) copy-start(s32[64]{0:T(128)} %param.12) | copy-start | bytes 772
  14.6 24.1 %copy-start.6 = (bf16[8,4,128]{2,1,0:T(4,128)(2,1)S(1)}, bf16[8,4,128]{2,1,0:T(4,128)(2,1)}, u32[]{:S(2)}) copy-start(bf16[8,4,128]{2,1,0:T(4,128)(2,1)} %param.13) | copy-start | bytes 24580
  14.6 24.1 %copy-start.7 = (bf16[8,2,2,128]{3,2,1,0:T(2,128)(2,1)S(1)}, bf16[8,2,2,128]{3,2,1,0:T(2,128)(2,1)}, u32[]{:S(2)}) copy-start(bf16[8,2,2,128]{3,2,1,0:T(2,128)(2,1)} %param.14) | copy-start | bytes 24580
  14.6 30.9 %copy-start.2 = (bf16[512,2048]{1,0:T(8,128)(2,1)S(1)}, bf16[512,2048]{1,0:T(8,128)(2,1)}, u32[]{:S(2)}) copy-start(bf16[512,2048]{1,0:T(8,128)(2,1)} %weight_ref.3) | copy-start | bytes 6291460
  24.6 3.4 %copy-start.1 = (bf16[64,2,2,128,128]{4,3,2,1,0:T(8,128)(2,1)S(1)}, bf16[64,2,2,128,128]{4,3,2,1,0:T(8,128)(2,1)}, u32[]{:S(2)}) copy-start(bf16[64,2,2,128,128]{4,3,2,1,0:T(8,128)(2,1)} %pages_ref.3) | copy-start | bytes 25165828
  33.6 11.9 %all-to-all-start.1 = ((bf16[8,32,256]{2,1,0:T(8,128)(2,1)}), bf16[8,32,256]{2,1,0:T(8,128)(2,1)S(1)}, u32[]{:S(2)}, u32[]{:S(2)}) async-start(bf16[8,32,256]{2,1,0:T(8,128)(2,1)} %bitcast.6), calls=%async_computation.1 | async-start | bytes 262144 | tf_op jit(solution)/shard_map/all_to_all | solution.py:388
  47.0 3.8 %collective-permute-start.2 = (bf16[8,512]{1,0:T(8,128)(2,1)S(1)}, bf16[8,512]{1,0:T(8,128)(2,1)S(1)}, u32[]{:S(2)}, u32[]{:S(2)}) collective-permute-start(bf16[8,512]{1,0:T(8,128)(2,1)S(1)} %get-tuple-element.27), channel_id=1, source_target_pairs={{0,24},{8,0},{16,8},{24,16},{1,25},{9,1},{17,9},{25,17},{2,26},{10... | collective-permute-start | bytes 24584 | tf_op jit(solution)/shard_map/ppermute | solution.py:399
  49.5 3.7 %collective-permute-start.1 = (bf16[8,512]{1,0:T(8,128)(2,1)S(1)}, bf16[8,512]{1,0:T(8,128)(2,1)S(1)}, u32[]{:S(2)}, u32[]{:S(2)}) collective-permute-start(bf16[8,512]{1,0:T(8,128)(2,1)S(1)} %get-tuple-element.26), channel_id=1, source_target_pairs={{0,16},{8,24},{16,0},{24,8},{1,17},{9,25},{17,1},{25,9},{2,18},{10... | collective-permute-start | bytes 24584 | tf_op jit(solution)/shard_map/ppermute | solution.py:399
  50.0 4.5 %collective-permute-start = (bf16[8,512]{1,0:T(8,128)(2,1)S(1)}, bf16[8,512]{1,0:T(8,128)(2,1)S(1)}, u32[]{:S(2)}, u32[]{:S(2)}) collective-permute-start(bf16[8,512]{1,0:T(8,128)(2,1)S(1)} %get-tuple-element.25), channel_id=1, source_target_pairs={{0,8},{8,16},{16,24},{24,0},{1,9},{9,17},{17,25},{25,1},{2,10},{10... | collective-permute-start | bytes 24584 | tf_op jit(solution)/shard_map/ppermute | solution.py:399

commit v2 on v1

v2 whole, which is shorter than its diff:
```python
import functools

import jax
import jax.numpy as jnp
from jax import lax
from jax.experimental import pallas as pl
from jax.experimental.pallas import tpu as pltpu
from jax.sharding import PartitionSpec as P

negative_floor = -1e30
f32 = jnp.float32
bf16 = jnp.bfloat16
i32 = jnp.int32


def iota(shape, dim):
    return lax.broadcasted_iota(i32, shape, dim)


def dot(a, b, contract=(1, 0)):
    return lax.dot_general(
        a, b, (((contract[0],), (contract[1],)), ((), ())), preferred_element_type=f32
    )


def pieces(x):
    high = x.astype(bf16)
    rest = x - high.astype(f32)
    middle = rest.astype(bf16)
    low = (rest - middle.astype(f32)).astype(bf16)
    return high, middle, low


def ones_where(mask):
    return jnp.where(mask, 1.0, 0.0).astype(bf16)


def spread_rows(pages_dev, heads):
    rows = pages_dev * heads
    return ones_where(iota((rows, pages_dev), 0) // heads == iota((rows, pages_dev), 1))


def select_left(page, position, count_ref, slots):
    row = iota((slots, slots), 0).astype(f32)
    selector = ones_where(row == position[pl.ds(page, 1), :])
    return selector, row == count_ref[pl.ds(page, 1), :]


def share_rows(page, share):
    row = iota((16, share.shape[2]), 0)
    rows = jnp.zeros((16, share.shape[2]), f32)
    for n in range(3):
        rows = jnp.where(row == n, share[n, pl.ds(page, 1), :], rows)
    return rows.astype(bf16)


def rounded_fold(rows):
    return jnp.sum(rows, axis=0, keepdims=True).astype(bf16).astype(f32)


def side_by_side(ref, page):
    return jnp.concatenate([ref[page, g] for g in range(ref.shape[1])], axis=1)


def prepare_kernel(
    heads, req_dev, chunk, rank_ref, table_hbm, lengths_hbm, keep_hbm, weight_hbm, query_hbm,
    pages_hbm, keys, query_ref, mass_ref, kept_ref, fold_mass_ref, position_ref, count_ref, share_ref,
    folded_ref, target_ref, slot_ref,
    table_ref, lengths_ref, keep_ref, weight_ref, small_sem, in_sem,
):
    pages_dev, slots = keep_ref.shape
    max_pages, reqs = table_ref.shape
    kv_local = keys.shape[1]
    chunks = pages_dev // chunk
    small = [
        pltpu.make_async_copy(a, b, small_sem.at[n])
        for n, (a, b) in enumerate(
            ((table_hbm, table_ref), (lengths_hbm, lengths_ref), (keep_hbm, keep_ref),
             (weight_hbm, weight_ref), (query_hbm, query_ref))
        )
    ]
    for copy in small:
        copy.start()
    loads = [
        pltpu.make_async_copy(
            pages_hbm.at[pl.ds(n * chunk, chunk), 0], keys.at[pl.ds(n * chunk, chunk)], in_sem.at[n]
        )
        for n in range(chunks)
    ]
    for copy in loads:
        copy.start()
    for copy in small:
        copy.wait()

    rank = rank_ref[0]
    page_id = iota((pages_dev, reqs), 0) + rank * pages_dev
    req_id = iota((pages_dev, reqs), 1)
    valid = jnp.zeros((pages_dev, reqs), i32)
    request = jnp.zeros((pages_dev, reqs), i32)
    for j in range(max_pages):
        match = table_ref[j : j + 1, :] == page_id
        left = jnp.clip(lengths_ref[...] - j * slots, 0, slots)
        valid = valid + jnp.where(match, left, 0)
        request = request + jnp.where(match, req_id, 0)
    valid = jnp.sum(valid, axis=1, keepdims=True)
    request = jnp.sum(request, axis=1, keepdims=True)
    slot_index = iota((pages_dev, slots), 1)
    in_page = slot_index < valid
    kept = jnp.logical_and(in_page, keep_ref[...] > 0)
    dropped = jnp.logical_and(in_page, keep_ref[...] == 0)
    kept_f = jnp.where(kept, 1.0, 0.0)
    before = ones_where(iota((slots, slots), 0) < iota((slots, slots), 1))
    position = dot(kept_f.astype(bf16), before)
    count = jnp.sum(kept_f, axis=1, keepdims=True)
    dropped_weight = jnp.where(dropped, weight_ref[...], 0.0)
    weight_sum = jnp.sum(dropped_weight, axis=1, keepdims=True)
    slot_f = slot_index.astype(f32)
    mass_ref[...] = jnp.where(
        slot_f < count, 1.0, jnp.where(slot_f == count, weight_sum, 0.0)
    ).astype(bf16)
    kept_ref[...] = kept_f
    fold_mass_ref[...] = jnp.broadcast_to(weight_sum.astype(bf16).astype(f32), (pages_dev, slots))
    position_ref[...] = jnp.where(kept, position, -1.0)
    count_ref[...] = jnp.broadcast_to(count, (pages_dev, slots))
    share = pieces(dropped_weight / jnp.maximum(weight_sum, 1.0))
    for n in range(3):
        share_ref[n] = share[n].astype(f32)

    owner = request // req_dev
    chip, core = owner // 2, owner % 2
    from_chip = jnp.bitwise_xor(chip, rank // 2)
    from_core = jnp.where(core == rank % 2, 0, 1)
    at_hand = (from_core * (reqs // req_dev // 2) + from_chip) * req_dev + request % req_dev
    at_hand = jnp.broadcast_to(at_hand, (pages_dev, slots)).astype(f32)
    spread = spread_rows(pages_dev, heads)
    rows = pages_dev * heads
    target_ref[...] = dot(spread, at_hand.astype(bf16)).astype(i32) * heads + iota((rows, slots), 0) % heads
    owner_col = jnp.broadcast_to(owner, (pages_dev, pages_dev))
    page_row, page_col = iota((pages_dev, pages_dev), 0), iota((pages_dev, pages_dev), 1)
    owner_row = jnp.sum(jnp.where(page_row == page_col, owner_col, 0), axis=0, keepdims=True)
    earlier = jnp.logical_and(owner_col == owner_row, page_row < page_col)
    order = jnp.sum(jnp.where(earlier, 1, 0), axis=0, keepdims=True)
    slot = owner_row * (pages_dev // (reqs // req_dev)) + order
    slot = jnp.broadcast_to(slot, (8, pages_dev)).astype(f32).astype(bf16)
    slot_ref[...] = dot(slot, spread, (1, 1))

    for n in range(chunks):
        loads[n].wait()
        for page in range(n * chunk, (n + 1) * chunk):
            result = dot(share_rows(page, share_ref), side_by_side(keys, page))
            folded = rounded_fold(result[:8])
            for g in range(kv_local):
                folded_ref[g, page : page + 1, :] = folded[:, g * 128 : (g + 1) * 128]


def prepare(rank, page_table, lengths, keep_list, fold_weight, queries, page_cache, heads, req_dev, chunk=16):
    pages_dev, _, kv_local, slots, head_size = page_cache.shape
    reqs, max_pages = page_table.shape
    rows = pages_dev * heads
    chunks = pages_dev // chunk
    hbm = pl.BlockSpec(memory_space=pltpu.HBM)
    vmem = pl.BlockSpec(memory_space=pltpu.VMEM)
    small = (pages_dev, slots)
    return pl.pallas_call(
        functools.partial(prepare_kernel, heads, req_dev, chunk),
        in_specs=[pl.BlockSpec(memory_space=pltpu.SMEM)] + [hbm] * 6,
        out_specs=[vmem] * 11,
        out_shape=[
            pltpu.VMEM((pages_dev, kv_local, slots, head_size), bf16),
            pltpu.VMEM(queries.shape, bf16),
            jax.ShapeDtypeStruct(small, bf16),
            jax.ShapeDtypeStruct(small, f32),
            jax.ShapeDtypeStruct(small, f32),
            jax.ShapeDtypeStruct(small, f32),
            jax.ShapeDtypeStruct(small, f32),
            jax.ShapeDtypeStruct((3,) + small, f32),
            jax.ShapeDtypeStruct((kv_local, pages_dev, head_size), f32),
            jax.ShapeDtypeStruct((rows, slots), i32),
            jax.ShapeDtypeStruct((8, rows), f32),
        ],
        scratch_shapes=[
            pltpu.VMEM((max_pages, reqs), i32),
            pltpu.VMEM((1, reqs), i32),
            pltpu.VMEM(small, i32),
            pltpu.VMEM(small, f32),
            pltpu.SemaphoreType.DMA((5,)),
            pltpu.SemaphoreType.DMA((chunks,)),
        ],
        compiler_params=pltpu.CompilerParams(vmem_limit_bytes=24 << 20),
        name="prepare",
    )(
        rank, *(
            pltpu.with_memory_space_constraint(x, pltpu.HBM)
            for x in (
                page_table.T, lengths.reshape(1, -1), keep_list, fold_weight, queries, page_cache
            )
        )
    )


def pack_kernel(half, chunk, *refs):
    pages_hbm, position_ref, count_ref, folded_ref = refs[:4]
    packed_hbm, raw, staged, in_sem, out_sem = refs[-5:]
    pages_dev, slots = position_ref.shape
    kv_local = raw.shape[1]
    spans = [pl.ds(n * chunk, chunk) for n in range(pages_dev // chunk)]
    loads = [
        pltpu.make_async_copy(pages_hbm.at[span, half], raw.at[span], in_sem.at[n])
        for n, span in enumerate(spans)
    ]
    stores = [
        pltpu.make_async_copy(staged.at[span], packed_hbm.at[span, half], out_sem.at[n])
        for n, span in enumerate(spans)
    ]
    for copy in loads:
        copy.start()
    for n in range(pages_dev // chunk):
        loads[n].wait()
        for page in range(n * chunk, (n + 1) * chunk):
            selector, at_fold = select_left(page, position_ref, count_ref, slots)
            result = dot(selector, side_by_side(raw, page))
            for g in range(kv_local):
                staged[page, g] = jnp.where(
                    at_fold, folded_ref[g, pl.ds(page, 1), :], result[:, g * 128 : (g + 1) * 128]
                ).astype(bf16)
        stores[n].start()
    for copy in stores:
        copy.wait()


def pack(half, page_cache, position, count, folded, packed=None, chunk=8):
    pages_dev, _, kv_local, slots, head_size = page_cache.shape
    hbm = pl.BlockSpec(memory_space=pltpu.HBM)
    vmem = pl.BlockSpec(memory_space=pltpu.VMEM)
    there = [] if packed is None else [packed]
    buffer = pltpu.VMEM((pages_dev, kv_local, slots, head_size), bf16)
    chunks = pltpu.SemaphoreType.DMA((pages_dev // chunk,))
    in_hbm = lambda x: pltpu.with_memory_space_constraint(x, pltpu.HBM)
    return pl.pallas_call(
        functools.partial(pack_kernel, half, chunk),
        in_specs=[hbm] + [vmem] * 3 + [hbm] * len(there),
        out_specs=hbm,
        out_shape=jax.ShapeDtypeStruct(page_cache.shape, bf16),
        input_output_aliases={4: 0} if there else {},
        scratch_shapes=[buffer, buffer, chunks, chunks],
        compiler_params=pltpu.CompilerParams(vmem_limit_bytes=24 << 20),
        name=("pack_keys", "pack_values")[half],
    )(in_hbm(page_cache), position, count, folded, *map(in_hbm, there))


def attend_kernel(
    heads, req_dev, score_scale, chunk, near_ref, far_ref, keys, kept_ref, fold_mass_ref, share_ref,
    fold_key_ref, target_ref, slot_ref, pages_hbm, out_ref, fold_value_ref, scores, parts, values,
    value_sem,
):
    pages_dev, slots = kept_ref.shape
    kv_local = keys.shape[1]
    loads = [
        pltpu.make_async_copy(
            pages_hbm.at[pl.ds(n * chunk, chunk), 1], values.at[pl.ds(n * chunk, chunk)],
            value_sem.at[n],
        )
        for n in range(pages_dev // chunk)
    ]
    for copy in loads:
        copy.start()
    groups = heads // kv_local
    rows = pages_dev * heads
    spread = spread_rows(pages_dev, heads)

    half = near_ref.shape[0]
    query = jnp.zeros((rows, 128), f32)
    for n, ref in enumerate((near_ref, far_ref)):
        for m in range(half // slots):
            first = n * half + m * slots
            pick = ones_where(target_ref[...] == iota((rows, slots), 1) + first)
            query = query + dot(pick, ref[m * slots : (m + 1) * slots])
    query_b = query.astype(bf16)

    tile = 16
    tile_pages = tile // heads
    row = iota((tile, 128), 0)
    row_page = row // heads
    row_group = (row % heads) // groups

    def choose(results):
        chosen = results[0][:tile, :128]
        for i in range(tile_pages):
            for g in range(kv_local):
                if i + g > 0:
                    here = jnp.logical_and(row_page == i, row_group == g)
                    chosen = jnp.where(here, results[i][:tile, g * 128 : (g + 1) * 128], chosen)
        return chosen

    for first in range(0, pages_dev, tile_pages):
        at = first * heads
        left = query_b[at : at + tile]
        results = [
            dot(left, keys[first + i].reshape(kv_local * slots, 128), (1, 1))
            for i in range(tile_pages)
        ]
        scores[at : at + tile, :] = choose(results)

    group_of = (iota((rows, pages_dev), 0) % heads) // groups
    spread_g = [
        jnp.where(group_of == g, spread.astype(f32), 0.0).astype(bf16) for g in range(kv_local)
    ]

    def spread_fold(ref):
        return sum(dot(spread_g[g], ref[g].astype(bf16)) for g in range(kv_local))

    kept = dot(spread, kept_ref[...].astype(bf16)) > 0.5
    fold_mass = dot(spread, fold_mass_ref[...].astype(bf16))[:, :1]
    fold_score = jnp.sum(query * spread_fold(fold_key_ref), axis=1, keepdims=True) * score_scale
    fold_live = fold_mass > 0
    score = jnp.where(kept, scores[...] * score_scale, negative_floor)
    top = jnp.maximum(
        jnp.max(score, axis=1, keepdims=True), jnp.where(fold_live, fold_score, negative_floor)
    )
    weight = jnp.where(kept, jnp.exp(score - top), 0.0)
    fold_weight = jnp.where(fold_live, fold_mass * jnp.exp(fold_score - top), 0.0)
    total = jnp.sum(weight, axis=1, keepdims=True) + fold_weight
    weight_b = weight.astype(bf16)

    for first in range(0, pages_dev, tile_pages):
        if first % chunk == 0:
            loads[first // chunk].wait()
        at = first * heads
        results = []
        for i in range(tile_pages):
            left = jnp.concatenate(
                [weight_b[at : at + tile], share_rows(first + i, share_ref)], axis=0
            )
            result = dot(left, side_by_side(values, first + i))
            results.append(result)
            folded = rounded_fold(result[tile : tile + 8])
            for g in range(kv_local):
                fold_value_ref[g, first + i : first + i + 1, :] = folded[:, g * 128 : (g + 1) * 128]
        parts[at : at + tile, :] = choose(results)

    part = parts[...] + fold_weight.astype(bf16).astype(f32) * spread_fold(fold_value_ref)
    lane = iota((rows, 128), 1)
    local = (target_ref[...] // heads % req_dev).astype(f32)
    stats = jnp.where(lane == 6, local, 0.0)
    for n, piece in enumerate(pieces(top) + pieces(total)):
        stats = jnp.where(lane == n, piece.astype(f32), stats)
    send = jnp.concatenate([part.astype(bf16), stats.astype(bf16)], axis=1)
    place = slot_ref[:1] * heads + (iota((1, rows), 1) % heads).astype(f32)
    move = ones_where(iota((rows, rows), 0).astype(f32) == place)
    out_ref[...] = dot(move, send).astype(bf16)


def attend(
    near, far, keys, kept, fold_mass, share, fold_key, target, slot, page_cache, score_scale, heads,
    req_dev, chunk=16
):
    pages_dev, _, kv_local, slots, head_size = page_cache.shape
    rows = pages_dev * heads
    vmem = pl.BlockSpec(memory_space=pltpu.VMEM)
    return pl.pallas_call(
        functools.partial(attend_kernel, heads, req_dev, score_scale, chunk),
        in_specs=[vmem] * 9 + [pl.BlockSpec(memory_space=pltpu.HBM)],
        out_specs=[vmem] * 2,
        out_shape=[
            jax.ShapeDtypeStruct((rows, 2 * head_size), bf16),
            jax.ShapeDtypeStruct((kv_local, pages_dev, head_size), f32),
        ],
        scratch_shapes=[
            pltpu.VMEM((rows, slots), f32),
            pltpu.VMEM((rows, head_size), f32),
            pltpu.VMEM((pages_dev, kv_local, slots, head_size), bf16),
            pltpu.SemaphoreType.DMA((pages_dev // chunk,)),
        ],
        compiler_params=pltpu.CompilerParams(vmem_limit_bytes=24 << 20),
        name="attend",
    )(
        near, far, keys, kept, fold_mass, share, fold_key, target, slot,
        pltpu.with_memory_space_constraint(page_cache, pltpu.HBM),
    )


def combine_kernel(
    heads, req_dev, score_scale, kv_count, rank_ref, got_ref, query_ref, fresh_key_ref,
    fresh_value_ref, weight_ref, attended_ref, *out_refs
):
    rows = got_ref.shape[0]
    cols = heads * req_dev
    width = weight_ref.shape[1] // kv_count
    stats = got_ref[:, 128:].astype(f32)
    top = stats[:, 0:1] + stats[:, 1:2] + stats[:, 2:3]
    request = stats[:, 6:7]
    row_head = (iota((rows, cols), 0) % heads).astype(f32)
    col = iota((rows, cols), 1)
    match = jnp.logical_and(
        request == (col % req_dev).astype(f32), row_head == (col // req_dev).astype(f32)
    )
    own = jnp.sum(
        query_ref[...].astype(f32) * fresh_key_ref[...].astype(f32), axis=1, keepdims=True
    ) * score_scale
    diagonal = iota((cols, cols), 0) == iota((cols, cols), 1)
    own_row = jnp.sum(jnp.where(diagonal, own, 0.0), axis=0, keepdims=True)
    best = jnp.maximum(
        jnp.max(jnp.where(match, top, negative_floor), axis=0, keepdims=True), own_row
    )
    best_col = jnp.sum(jnp.where(diagonal, best, 0.0), axis=1, keepdims=True)
    factor = jnp.where(match, jnp.exp(top - best), 0.0)
    high, middle, low = pieces(factor)
    got = got_ref[...]
    sums = dot(high, got, (0, 0)) + dot(middle, got, (0, 0)) + dot(low, got, (0, 0))
    own_factor = jnp.exp(own - best_col)
    denominator = sums[:, 131:132] + sums[:, 132:133] + sums[:, 133:134] + own_factor
    numerator = sums[:, :128] + own_factor * fresh_value_ref[...].astype(f32)
    attended = numerator / denominator
    attended = jnp.concatenate(
        [attended[h * req_dev : (h + 1) * req_dev] for h in range(heads)], axis=1
    ).astype(bf16)
    attended_ref[...] = attended
    rank = rank_ref[0]
    for k in range(kv_count):
        other = jnp.bitwise_xor(rank, k)
        at = pl.multiple_of(other * width, width)
        out_refs[k][...] = dot(attended, weight_ref[:, pl.ds(at, width)]).astype(bf16)


def combine(rank, got, query, fresh_key, fresh_value, out_weight, score_scale, heads, kv_count):
    req_dev = query.shape[0] // heads
    vmem = pl.BlockSpec(memory_space=pltpu.VMEM)
    smem = pl.BlockSpec(memory_space=pltpu.SMEM)
    width = out_weight.shape[1] // kv_count
    return pl.pallas_call(
        functools.partial(combine_kernel, heads, req_dev, score_scale, kv_count),
        in_specs=[smem] + [vmem] * 5,
        out_specs=[vmem] * (1 + kv_count),
        out_shape=[jax.ShapeDtypeStruct((req_dev, out_weight.shape[0]), bf16)]
        + [jax.ShapeDtypeStruct((req_dev, width), bf16)] * kv_count,
        compiler_params=pltpu.CompilerParams(vmem_limit_bytes=24 << 20),
        cost_estimate=pl.CostEstimate(
            flops=2 * req_dev * out_weight.size, bytes_accessed=2 * out_weight.size, transcendentals=0
        ),
        name="combine",
    )(rank, got, query, fresh_key, fresh_value, out_weight)


def exchange(x, axis, count, mask):
    return lax.ppermute(x, axis, [(i, i ^ mask) for i in range(count)])


def per_device(
    page_cache, keep_list, fold_weight, page_table, lengths, queries, fresh_entries, out_weight
):
    seq_count = lax.axis_size("seq")
    kv_count = lax.axis_size("kv")
    assert seq_count & (seq_count - 1) == 0 and kv_count & (kv_count - 1) == 0
    seq_rank = lax.axis_index("seq").astype(i32).reshape(1)
    kv_rank = lax.axis_index("kv").astype(i32).reshape(1)
    _, _, kv_local, slots, head_size = page_cache.shape
    req_dev, heads, _ = queries.shape
    groups = heads // kv_local
    score_scale = head_size ** (-0.5)

    others = [exchange(queries, "seq", seq_count, 2 * k) for k in range(1, seq_count // 2)]
    keys, own, mass, kept, fold_mass, position, count, share, fold_key, target, slot = prepare(
        seq_rank, page_table, lengths, keep_list, fold_weight, queries, page_cache, heads, req_dev
    )
    near = jnp.concatenate([own] + others, axis=0).reshape(-1, head_size)
    far = exchange(near, "seq", seq_count, 1)
    send, fold_value = attend(
        near, far, keys, kept, fold_mass, share, fold_key, target, slot, page_cache, score_scale,
        heads, req_dev,
    )
    got = lax.all_to_all(
        send.reshape(seq_count, -1, send.shape[1]), "seq", split_axis=0, concat_axis=0, tiled=True
    ).reshape(send.shape)
    packed = pack(1, page_cache, position, count, fold_value)
    got, packed = lax.optimization_barrier((got, packed))
    by_head = lambda x: x.transpose(1, 0, 2).reshape(heads * req_dev, head_size)
    fresh = jnp.repeat(fresh_entries, groups, axis=2)
    attended, *shares = combine(
        kv_rank, got, by_head(queries), by_head(fresh[:, 0]), by_head(fresh[:, 1]), out_weight,
        score_scale, heads, kv_count,
    )
    fold_key, *shares = lax.optimization_barrier((fold_key, *shares))
    total = shares[0].astype(f32)
    for k in range(1, kv_count):
        total = total + exchange(shares[k], "kv", kv_count, k).astype(f32)
    packed = pack(0, page_cache, position, count, fold_key, packed)
    return packed, mass, attended, total.astype(bf16)


def solution(mesh):
    placed = (
        P("seq", None, "kv", None, None),
        P("seq", None),
        P("seq", None),
        P(),
        P(),
        P("seq", "kv", None),
        P("seq", None, "kv", None),
        P("kv", None),
    )
    return jax.shard_map(
        per_device,
        mesh=mesh,
        in_specs=placed,
        out_specs=(
            P("seq", None, "kv", None, None),
            P("seq", None),
            P("seq", "kv"),
            P("seq", "kv"),
        ),
        check_vma=False,
    )
```

time: 55.7 us -> 37.7 us (0.68)
  local copies, waits for them, and re-layouts: 11.1 us -> 0.04 us
  waiting for transfers between devices: 10.7 us -> 5.31 us
  starting transfers between devices: 15 us -> 12.6 us
  Pallas kernels: 17.1 us -> 18 us
    unnamed x18 -> x7, local copies, waits for them, and re-layouts: 9.72 us -> 0.02 us
    all_to_all x1 -> x0, starting transfers between devices: 6.33 us -> none  [per_device(): lax.all_to_all(jnp.broadcast_to(rows[None], (seq_count,) + rows.shape), '...]
    ppermute x3 -> x7, starting transfers between devices: 3.54 us -> 9.24 us  [exchange(): return lax.ppermute(x, axis, [(i, i ^ mask) for i in range(count)])]
    all_to_all x1, waiting for transfers between devices: 6.72 us -> 2.19 us  [per_device(): lax.all_to_all(send.reshape(seq_count, -1, send.shape[1]), 'seq', split_a...]
    all_to_all x1, starting transfers between devices: 5.11 us -> 3.38 us  [per_device(): lax.all_to_all(send.reshape(seq_count, -1, send.shape[1]), 'seq', split_a...]
    broadcast_in_dim x1 -> x0, local copies, waits for them, and re-layouts: 1.34 us -> none  [per_device(): jnp.broadcast_to(rows[None], (seq_count,) + rows.shape)]
    pallas_call x2 -> x4, Pallas kernels: 15.6 us -> 16.7 us  [the longest x2 8.71 us: pack(): pl.pallas_call(functools.partial(pack_kernel, half, chunk), in_specs=[hbm...]
    ppermute x3 -> x7, waiting for transfers between devices: 3.96 us -> 3.12 us  [exchange(): return lax.ppermute(x, axis, [(i, i ^ mask) for i in range(count)])]
  transfers between devices with their start and end apart: 5 -> 8, of which waited for: 4 -> 3; matrix products, arithmetic and copies ran while one was open for 1% -> 0% of each run, Pallas kernels for 18% -> 33%
where the time goes in v2:
time: 37.7 us; the launch traced here: 37.4 us
  Pallas kernels  18 us (48%)
  starting transfers between devices  12.6 us (33%)
  waiting for transfers between devices  5.31 us (14%)
  between operations  0.8 us (2%)
  other arithmetic  0.64 us (2%)
    ppermute x7, starting transfers between devices, exchange(): return lax.ppermute(x, axis, [(i, i ^ mask) for i in range(count)])  9.24 us
    pallas_call x2, Pallas kernels, pack(): pl.pallas_call(functools.partial(pack_kernel, half, chunk), in_specs=[hbm...  8.71 us
    pallas_call x1, Pallas kernels, attend(): pl.pallas_call(functools.partial(attend_kernel, heads, req_dev, score_sca...  4.33 us
    pallas_call x1, Pallas kernels, prepare(): pl.pallas_call(functools.partial(prepare_kernel, heads, req_dev, chunk),...  3.69 us
    all_to_all x1, starting transfers between devices, per_device(): lax.all_to_all(send.reshape(seq_count, -1, send.shape[1]), 'seq', split_a...  3.38 us
    ppermute x7, waiting for transfers between devices, exchange(): return lax.ppermute(x, axis, [(i, i ^ mask) for i in range(count)])  3.12 us
    all_to_all x1, waiting for transfers between devices, per_device(): lax.all_to_all(send.reshape(seq_count, -1, send.shape[1]), 'seq', split_a...  2.19 us
    pallas_call x1, Pallas kernels, combine(): pl.pallas_call(functools.partial(combine_kernel, heads, req_dev, score_sc...  1.31 us
  transfers between devices with their start and end apart: 8, of which 3 were waited for; matrix products, arithmetic and copies ran while one was open for 0% of the time, Pallas kernels for 33%

profile of v2, /device:TPU:0, one launch (start us, length us, event | category | flops | bytes accessed | tf_op | source)
XLA Modules:
  0.0 37.4 jit_solution(17959272576065641357)
XLA Ops:
  0.6 3.1 %collective-permute-start = (bf16[8,4,128]{2,1,0:T(4,128)(2,1)}, bf16[8,4,128]{2,1,0:T(4,128)(2,1)S(1)}, u32[]{:S(2)}, u32[]{:S(2)}) collective-permute-start(bf16[8,4,128]{2,1,0:T(4,128)(2,1)} %query_hbm.1), channel_id=1, source_target_pairs={{0,2},{1,3},{2,0},{3,1},{4,6},{5,7},{6,4},{7,5},{8,10},{9,11},{10,... | collective-permute-start | bytes 24584 | tf_op jit(solution)/shard_map/ppermute | solution.py:445
  3.7 2.6 %collective-permute-start.1 = (bf16[8,4,128]{2,1,0:T(4,128)(2,1)}, bf16[8,4,128]{2,1,0:T(4,128)(2,1)S(1)}, u32[]{:S(2)}, u32[]{:S(2)}) collective-permute-start(bf16[8,4,128]{2,1,0:T(4,128)(2,1)} %query_hbm.1), channel_id=1, source_target_pairs={{0,4},{1,5},{2,6},{3,7},{4,0},{5,1},{6,2},{7,3},{8,12},{9,13},{10,... | collective-permute-start | bytes 24584 | tf_op jit(solution)/shard_map/ppermute | solution.py:445
  6.3 0.0 collective-permute-start.2
  6.3 3.7 %prepare.1 = (bf16[64,2,128,128]{3,2,1,0:T(8,128)(2,1)S(1)}, bf16[8,4,128]{2,1,0:T(4,128)(2,1)S(1)}, bf16[64,128]{1,0:T(8,128)(2,1)}, f32[64,128]{1,0:T(8,128)S(...) custom-call(s32[1]{0:T(128)} %bitcast.rank_ref, ...), custom_call_target="tpu_custom_call" | custom-call | tf_op jit(solution)/shard_map/prepare/pallas_call | solution.py:164
  10.0 0.0 copy-start.2
  10.0 0.0 copy-start.1
  10.0 0.0 collective-permute-done
  10.0 0.0 collective-permute-done.1
  10.1 1.9 %collective-permute-done.2 = bf16[8,4,128]{2,1,0:T(4,128)(2,1)S(1)} collective-permute-done((bf16[8,4,128]{2,1,0:T(4,128)(2,1)}, bf16[8,4,128]{2,1,0:T(4,128)(2,1)S(1)}, u32[]{:S(2)}, u32[]{:S(2)}) %collective-permute-start.2) | collective-permute-done | bytes 8224 | tf_op jit(solution)/shard_map/ppermute | solution.py:445
  12.0 0.1 collective-permute-start.3
  12.1 1.2 %collective-permute-done.3.far_ref = bf16[128,128]{1,0:T(8,128)(2,1)S(1)} collective-permute-done((bf16[128,128]{1,0:T(8,128)(2,1)S(1)}, bf16[128,128]{1,0:T(8,128)(2,1)S(1)}, u32[]{:S(2)}, u32[]{:S(2)}) %collective-permute-start.3) | collective-permute-done | bytes 32800 | tf_op jit(solution)/shard_map/ppermute | solution.py:445
  13.3 4.3 %attend.1 = (bf16[256,256]{1,0:T(8,128)(2,1)}, f32[2,64,128]{2,1,0:T(8,128)S(1)}) custom-call(bf16[128,128]{1,0:T(8,128)(2,1)S(1)} %bitcast.26, bf16[128,128]{1,0:T(8,128)(2,1)S(1)} %collective-permute-done.3.far_ref, bf16[64,2,128,128]{3,2,1,0:T(8,128)(2,1)S(1)} %get-tuple-element.33.keys, f32[64,128]{1,0:T(8,128)S(1)} %get-tuple-element.34.kept_ref, ...), custom_call_target="tpu_custom_call" | custom-call | tf_op jit(solution)/shard_map/attend/pallas_call | solution.py:360
  17.6 3.4 %all-to-all-start = ((bf16[8,32,256]{2,1,0:T(8,128)(2,1)}), bf16[8,32,256]{2,1,0:T(8,128)(2,1)S(1)}, u32[]{:S(2)}, u32[]{:S(2)}) async-start(bf16[8,32,256]{2,1,0:T(8,128)(2,1)} %bitcast.5), calls=%async_computation | async-start | bytes 262144 | tf_op jit(solution)/shard_map/all_to_all | solution.py:471
  21.1 0.0 copy-start
  21.1 4.4 %pack_values.1.refs_4_ = bf16[64,2,2,128,128]{4,3,2,1,0:T(8,128)(2,1)} custom-call(bf16[64,2,2,128,128]{4,3,2,1,0:T(8,128)(2,1)} %refs_0_.3, f32[64,128]{1,0:T(8,128)S(1)} %get-tuple-element.29.refs_1_, f32[64,128]{1,0:T(8,128)S(1)} %get-tuple-element.30.refs_2_, f32[2,64,128]{2,1,0:T(8,128)S(1)} %get-tuple-element.40.refs_3_), custom_call_target="tpu_custom_call" | custom-call | tf_op jit(solution)/shard_map/pack_values/pallas_call | solution.py:239
  25.5 2.2 %all-to-all-done = bf16[8,32,256]{2,1,0:T(8,128)(2,1)S(1)} async-done(((bf16[8,32,256]{2,1,0:T(8,128)(2,1)}), bf16[8,32,256]{2,1,0:T(8,128)(2,1)S(1)}, u32[]{:S(2)}, u32[]{:S(2)}) %all-to-all-start) | async-done | bytes 131104 | tf_op jit(solution)/shard_map/all_to_all | solution.py:471
  27.7 1.3 %combine.1 = (bf16[8,512]{1,0:T(8,128)(2,1)}, bf16[8,512]{1,0:T(8,128)(2,1)S(1)}, bf16[8,512]{1,0:T(8,128)(2,1)S(1)}, bf16[8,512]{1,0:T(8,128)(2,1)S(1)}, bf16[8,512]{1,0:T(8,128)(2,1)S(1)}) custom-call(s32[1]{0:T(128)} %bitcast.3.rank_ref, bf16[256,256]{1,0:T(8,128)(2,1)S(1)} %bitcast.24, bf16[32,128]{1,0:T(8,128)(2,1)S(1)} %bitcast.27, ...), custom_call_target="tpu_custom_call" | custom-call | flops 16777216 | bytes 2097152 | tf_op jit(solution)/shard_map/combine/pallas_call | solution.py:430
  29.0 1.5 %collective-permute-start.4 = (bf16[8,512]{1,0:T(8,128)(2,1)S(1)}, bf16[8,512]{1,0:T(8,128)(2,1)S(1)}, u32[]{:S(2)}, u32[]{:S(2)}) collective-permute-start(bf16[8,512]{1,0:T(8,128)(2,1)S(1)} %get-tuple-element.51), channel_id=1, source_target_pairs={{0,8},{8,0},{16,24},{24,16},{1,9},{9,1},{17,25},{25,17},{2,10},{10... | collective-permute-start | bytes 24584 | tf_op jit(solution)/shard_map/ppermute | solution.py:445
  30.5 1.5 %collective-permute-start.5 = (bf16[8,512]{1,0:T(8,128)(2,1)S(1)}, bf16[8,512]{1,0:T(8,128)(2,1)S(1)}, u32[]{:S(2)}, u32[]{:S(2)}) collective-permute-start(bf16[8,512]{1,0:T(8,128)(2,1)S(1)} %get-tuple-element.52), channel_id=1, source_target_pairs={{0,16},{8,24},{16,0},{24,8},{1,17},{9,25},{17,1},{25,9},{2,18},{10... | collective-permute-start | bytes 24584 | tf_op jit(solution)/shard_map/ppermute | solution.py:445
  32.0 0.5 %collective-permute-start.6 = (bf16[8,512]{1,0:T(8,128)(2,1)S(1)}, bf16[8,512]{1,0:T(8,128)(2,1)S(1)}, u32[]{:S(2)}, u32[]{:S(2)}) collective-permute-start(bf16[8,512]{1,0:T(8,128)(2,1)S(1)} %get-tuple-element.53), channel_id=1, source_target_pairs={{0,24},{8,16},{16,8},{24,0},{1,25},{9,17},{17,9},{25,1},{2,26},{10... | collective-permute-start | bytes 24584 | tf_op jit(solution)/shard_map/ppermute | solution.py:445
  32.5 4.3 %pack_keys.1 = bf16[64,2,2,128,128]{4,3,2,1,0:T(8,128)(2,1)} custom-call(bf16[64,2,2,128,128]{4,3,2,1,0:T(8,128)(2,1)} %refs_0_.3, f32[64,128]{1,0:T(8,128)S(1)} %get-tuple-element.29.refs_1_, f32[64,128]{1,0:T(8,128)S(1)} %get-tuple-element.30.refs_2_, f32[2,64,128]{2,1,0:T(8,128)S(1)} %get-tuple-element.46.fold_key_ref.refs_3_, ...), custom_call_target="tpu_custom_call", output_to_operand_aliasing={{}: (4, {})} | custom-call | tf_op jit(solution)/shard_map/pack_keys/pallas_call | solution.py:239
  36.8 0.0 collective-permute-done.4
  36.8 0.0 collective-permute-done.5
  36.8 0.6 %add_convert_fusion = bf16[8,512]{1,0:T(8,128)(2,1)} fusion(bf16[8,512]{1,0:T(8,128)(2,1)S(1)} %collective-permute-done.6, bf16[8,512]{1,0:T(8,128)(2,1)S(1)} %collective-permute-done.5, bf16[8,512]{1,0:T(8,128)(2,1)S(1)} %collective-permute-done.4, bf16[8,512]{1,0:T(8,128)(2,1)S(1)} %get-tuple-element.50), kind=kLoop, calls=%fused_computation.1 | loop fusion | flops 32768 | bytes 40960 | tf_op jit(solution)/shard_map/convert_element_type | solution.py:487
  (9 shorter events, 0.1 us)
Async XLA Ops:
  0.6 9.4 %collective-permute-start = (bf16[8,4,128]{2,1,0:T(4,128)(2,1)}, bf16[8,4,128]{2,1,0:T(4,128)(2,1)S(1)}, u32[]{:S(2)}, u32[]{:S(2)}) collective-permute-start(bf16[8,4,128]{2,1,0:T(4,128)(2,1)} %query_hbm.1), channel_id=1, source_target_pairs={{0,2},{1,3},{2,0},{3,1},{4,6},{5,7},{6,4},{7,5},{8,10},{9,11},{10,... | collective-permute-start | bytes 24584 | tf_op jit(solution)/shard_map/ppermute | solution.py:445
  3.7 6.3 %collective-permute-start.1 = (bf16[8,4,128]{2,1,0:T(4,128)(2,1)}, bf16[8,4,128]{2,1,0:T(4,128)(2,1)S(1)}, u32[]{:S(2)}, u32[]{:S(2)}) collective-permute-start(bf16[8,4,128]{2,1,0:T(4,128)(2,1)} %query_hbm.1), channel_id=1, source_target_pairs={{0,4},{1,5},{2,6},{3,7},{4,0},{5,1},{6,2},{7,3},{8,12},{9,13},{10,... | collective-permute-start | bytes 24584 | tf_op jit(solution)/shard_map/ppermute | solution.py:445
  6.3 5.7 %collective-permute-start.2 = (bf16[8,4,128]{2,1,0:T(4,128)(2,1)}, bf16[8,4,128]{2,1,0:T(4,128)(2,1)S(1)}, u32[]{:S(2)}, u32[]{:S(2)}) collective-permute-start(bf16[8,4,128]{2,1,0:T(4,128)(2,1)} %query_hbm.1), channel_id=1, source_target_pairs={{0,6},{1,7},{2,4},{3,5},{4,2},{5,3},{6,0},{7,1},{8,14},{9,15},{10,... | collective-permute-start | bytes 24584 | tf_op jit(solution)/shard_map/ppermute | solution.py:445
  10.0 11.0 %copy-start.2 = (bf16[8,2,2,128]{3,2,1,0:T(2,128)(2,1)S(1)}, bf16[8,2,2,128]{3,2,1,0:T(2,128)(2,1)}, u32[]{:S(2)}) copy-start(bf16[8,2,2,128]{3,2,1,0:T(2,128)(2,1)} %param.14) | copy-start | bytes 24580
  10.0 11.0 %copy-start.1 = (bf16[8,4,128]{2,1,0:T(4,128)(2,1)S(1)}, bf16[8,4,128]{2,1,0:T(4,128)(2,1)}, u32[]{:S(2)}) copy-start(bf16[8,4,128]{2,1,0:T(4,128)(2,1)} %query_hbm.1) | copy-start | bytes 24580
  12.0 1.3 %collective-permute-start.3 = (bf16[128,128]{1,0:T(8,128)(2,1)S(1)}, bf16[128,128]{1,0:T(8,128)(2,1)S(1)}, u32[]{:S(2)}, u32[]{:S(2)}) collective-permute-start(bf16[128,128]{1,0:T(8,128)(2,1)S(1)} %bitcast.25), channel_id=1, source_target_pairs={{0,1},{1,0},{2,3},{3,2},{4,5},{5,4},{6,7},{7,6},{8,9},{9,8},{10,11... | collective-permute-start | bytes 98312 | tf_op jit(solution)/shard_map/ppermute | solution.py:445
  17.6 10.1 %all-to-all-start = ((bf16[8,32,256]{2,1,0:T(8,128)(2,1)}), bf16[8,32,256]{2,1,0:T(8,128)(2,1)S(1)}, u32[]{:S(2)}, u32[]{:S(2)}) async-start(bf16[8,32,256]{2,1,0:T(8,128)(2,1)} %bitcast.5), calls=%async_computation | async-start | bytes 262144 | tf_op jit(solution)/shard_map/all_to_all | solution.py:471
  21.1 6.6 %copy-start = (bf16[512,2048]{1,0:T(8,128)(2,1)S(1)}, bf16[512,2048]{1,0:T(8,128)(2,1)}, u32[]{:S(2)}) copy-start(bf16[512,2048]{1,0:T(8,128)(2,1)} %weight_ref.1) | copy-start | bytes 6291460
  29.0 7.8 %collective-permute-start.4 = (bf16[8,512]{1,0:T(8,128)(2,1)S(1)}, bf16[8,512]{1,0:T(8,128)(2,1)S(1)}, u32[]{:S(2)}, u32[]{:S(2)}) collective-permute-start(bf16[8,512]{1,0:T(8,128)(2,1)S(1)} %get-tuple-element.51), channel_id=1, source_target_pairs={{0,8},{8,0},{16,24},{24,16},{1,9},{9,1},{17,25},{25,17},{2,10},{10... | collective-permute-start | bytes 24584 | tf_op jit(solution)/shard_map/ppermute | solution.py:445
  30.5 6.3 %collective-permute-start.5 = (bf16[8,512]{1,0:T(8,128)(2,1)S(1)}, bf16[8,512]{1,0:T(8,128)(2,1)S(1)}, u32[]{:S(2)}, u32[]{:S(2)}) collective-permute-start(bf16[8,512]{1,0:T(8,128)(2,1)S(1)} %get-tuple-element.52), channel_id=1, source_target_pairs={{0,16},{8,24},{16,0},{24,8},{1,17},{9,25},{17,1},{25,9},{2,18},{10... | collective-permute-start | bytes 24584 | tf_op jit(solution)/shard_map/ppermute | solution.py:445
  32.0 4.8 %collective-permute-start.6 = (bf16[8,512]{1,0:T(8,128)(2,1)S(1)}, bf16[8,512]{1,0:T(8,128)(2,1)S(1)}, u32[]{:S(2)}, u32[]{:S(2)}) collective-permute-start(bf16[8,512]{1,0:T(8,128)(2,1)S(1)} %get-tuple-element.53), channel_id=1, source_target_pairs={{0,24},{8,16},{16,8},{24,0},{1,25},{9,17},{17,9},{25,1},{2,26},{10... | collective-permute-start | bytes 24584 | tf_op jit(solution)/shard_map/ppermute | solution.py:445

commit v3 on v2

--- a/solution.py
+++ b/solution.py
@@ -64,8 +64,8 @@
 
 def prepare_kernel(
     heads, req_dev, chunk, rank_ref, table_hbm, lengths_hbm, keep_hbm, weight_hbm, query_hbm,
-    pages_hbm, keys, query_ref, mass_ref, kept_ref, fold_mass_ref, position_ref, count_ref, share_ref,
-    folded_ref, target_ref, slot_ref,
+    fresh_hbm, pages_hbm, keys, query_ref, fresh_ref, mass_ref, kept_ref, fold_mass_ref, position_ref, count_ref, share_ref,
+    target_ref, slot_ref,
     table_ref, lengths_ref, keep_ref, weight_ref, small_sem, in_sem,
 ):
     pages_dev, slots = keep_ref.shape
@@ -76,7 +76,7 @@
         pltpu.make_async_copy(a, b, small_sem.at[n])
         for n, (a, b) in enumerate(
             ((table_hbm, table_ref), (lengths_hbm, lengths_ref), (keep_hbm, keep_ref),
-             (weight_hbm, weight_ref), (query_hbm, query_ref))
+             (weight_hbm, weight_ref), (query_hbm, query_ref), (fresh_hbm, fresh_ref))
         )
     ]
     for copy in small:
@@ -128,7 +128,8 @@
 
     owner = request // req_dev
     chip, core = owner // 2, owner % 2
-    from_chip = jnp.bitwise_xor(chip, rank // 2)
+    chips = reqs // req_dev // 2
+    from_chip = lax.rem(rank // 2 - chip + chips, chips)
     from_core = jnp.where(core == rank % 2, 0, 1)
     at_hand = (from_core * (reqs // req_dev // 2) + from_chip) * req_dev + request % req_dev
     at_hand = jnp.broadcast_to(at_hand, (pages_dev, slots)).astype(f32)
@@ -144,16 +145,11 @@
     slot = jnp.broadcast_to(slot, (8, pages_dev)).astype(f32).astype(bf16)
     slot_ref[...] = dot(slot, spread, (1, 1))
 
-    for n in range(chunks):
-        loads[n].wait()
-        for page in range(n * chunk, (n + 1) * chunk):
-            result = dot(share_rows(page, share_ref), side_by_side(keys, page))
-            folded = rounded_fold(result[:8])
-            for g in range(kv_local):
-                folded_ref[g, page : page + 1, :] = folded[:, g * 128 : (g + 1) * 128]
-
-
-def prepare(rank, page_table, lengths, keep_list, fold_weight, queries, page_cache, heads, req_dev, chunk=16):
+    for copy in loads:
+        copy.wait()
+
+
+def prepare(rank, page_table, lengths, keep_list, fold_weight, queries, fresh_entries, page_cache, heads, req_dev, chunk=16):
     pages_dev, _, kv_local, slots, head_size = page_cache.shape
     reqs, max_pages = page_table.shape
     rows = pages_dev * heads
@@ -163,18 +159,18 @@
     small = (pages_dev, slots)
     return pl.pallas_call(
         functools.partial(prepare_kernel, heads, req_dev, chunk),
-        in_specs=[pl.BlockSpec(memory_space=pltpu.SMEM)] + [hbm] * 6,
+        in_specs=[pl.BlockSpec(memory_space=pltpu.SMEM)] + [hbm] * 7,
         out_specs=[vmem] * 11,
         out_shape=[
             pltpu.VMEM((pages_dev, kv_local, slots, head_size), bf16),
             pltpu.VMEM(queries.shape, bf16),
+            pltpu.VMEM(fresh_entries.shape, bf16),
             jax.ShapeDtypeStruct(small, bf16),
             jax.ShapeDtypeStruct(small, f32),
             jax.ShapeDtypeStruct(small, f32),
             jax.ShapeDtypeStruct(small, f32),
             jax.ShapeDtypeStruct(small, f32),
             jax.ShapeDtypeStruct((3,) + small, f32),
-            jax.ShapeDtypeStruct((kv_local, pages_dev, head_size), f32),
             jax.ShapeDtypeStruct((rows, slots), i32),
             jax.ShapeDtypeStruct((8, rows), f32),
         ],
@@ -183,7 +179,7 @@
             pltpu.VMEM((1, reqs), i32),
             pltpu.VMEM(small, i32),
             pltpu.VMEM(small, f32),
-            pltpu.SemaphoreType.DMA((5,)),
+            pltpu.SemaphoreType.DMA((6,)),
             pltpu.SemaphoreType.DMA((chunks,)),
         ],
         compiler_params=pltpu.CompilerParams(vmem_limit_bytes=24 << 20),
@@ -192,68 +188,100 @@
         rank, *(
             pltpu.with_memory_space_constraint(x, pltpu.HBM)
             for x in (
-                page_table.T, lengths.reshape(1, -1), keep_list, fold_weight, queries, page_cache
+                page_table.T, lengths.reshape(1, -1), keep_list, fold_weight, queries, fresh_entries,
+                page_cache,
             )
         )
     )
 
 
-def pack_kernel(half, chunk, *refs):
-    pages_hbm, position_ref, count_ref, folded_ref = refs[:4]
-    packed_hbm, raw, staged, in_sem, out_sem = refs[-5:]
-    pages_dev, slots = position_ref.shape
+def fold_kernel(keys, share_ref, folded_ref, _):
+    pages_dev, kv_local = keys.shape[:2]
+    for page in range(pages_dev):
+        result = dot(share_rows(page, share_ref), side_by_side(keys, page))
+        folded = rounded_fold(result[:8])
+        for g in range(kv_local):
+            folded_ref[g, page : page + 1, :] = folded[:, g * 128 : (g + 1) * 128]
+
+
+def fold_keys(keys, share):
+    pages_dev, kv_local, _, head_size = keys.shape
+    vmem = pl.BlockSpec(memory_space=pltpu.VMEM)
+    return pl.pallas_call(
+        fold_kernel,
+        in_specs=[vmem] * 2,
+        out_specs=[vmem] * 2,
+        out_shape=[
+            jax.ShapeDtypeStruct((kv_local, pages_dev, head_size), f32),
+            pltpu.VMEM(keys.shape, bf16),
+        ],
+        input_output_aliases={0: 1},
+        compiler_params=pltpu.CompilerParams(vmem_limit_bytes=24 << 20),
+        name="fold_keys",
+    )(keys, share)
+
+
+def pack_kernel(spans, chunk, pages_hbm, position_ref, count_ref, *rest):
+    folded_refs = rest[:2]
+    packed_hbm, raw, staged, in_sem, out_sem = rest[-5:]
+    slots = position_ref.shape[1]
     kv_local = raw.shape[1]
-    spans = [pl.ds(n * chunk, chunk) for n in range(pages_dev // chunk)]
-    loads = [
-        pltpu.make_async_copy(pages_hbm.at[span, half], raw.at[span], in_sem.at[n])
-        for n, span in enumerate(spans)
-    ]
-    stores = [
-        pltpu.make_async_copy(staged.at[span], packed_hbm.at[span, half], out_sem.at[n])
-        for n, span in enumerate(spans)
-    ]
+    parts = [(half, n) for half, first, end in spans for n in range(first, end, chunk)]
+    loads, stores = [], []
+    for i, (half, n) in enumerate(parts):
+        there, here = pl.ds(n, chunk), pl.ds(i * chunk, chunk)
+        loads.append(
+            pltpu.make_async_copy(pages_hbm.at[there, half], raw.at[here], in_sem.at[i])
+        )
+        stores.append(
+            pltpu.make_async_copy(staged.at[here], packed_hbm.at[there, half], out_sem.at[i])
+        )
     for copy in loads:
         copy.start()
-    for n in range(pages_dev // chunk):
-        loads[n].wait()
-        for page in range(n * chunk, (n + 1) * chunk):
+    for i, (half, n) in enumerate(parts):
+        loads[i].wait()
+        for j in range(chunk):
+            page, at = n + j, i * chunk + j
             selector, at_fold = select_left(page, position_ref, count_ref, slots)
-            result = dot(selector, side_by_side(raw, page))
+            result = dot(selector, side_by_side(raw, at))
             for g in range(kv_local):
-                staged[page, g] = jnp.where(
-                    at_fold, folded_ref[g, pl.ds(page, 1), :], result[:, g * 128 : (g + 1) * 128]
+                staged[at, g] = jnp.where(
+                    at_fold, folded_refs[half][g, pl.ds(page, 1), :],
+                    result[:, g * 128 : (g + 1) * 128],
                 ).astype(bf16)
-        stores[n].start()
+        stores[i].start()
     for copy in stores:
         copy.wait()
 
 
-def pack(half, page_cache, position, count, folded, packed=None, chunk=8):
-    pages_dev, _, kv_local, slots, head_size = page_cache.shape
+def pack(name, spans, page_cache, position, count, fold_key, fold_value, packed=None, chunk=8):
+    _, _, kv_local, slots, head_size = page_cache.shape
     hbm = pl.BlockSpec(memory_space=pltpu.HBM)
     vmem = pl.BlockSpec(memory_space=pltpu.VMEM)
-    there = [] if packed is None else [packed]
-    buffer = pltpu.VMEM((pages_dev, kv_local, slots, head_size), bf16)
-    chunks = pltpu.SemaphoreType.DMA((pages_dev // chunk,))
+    size = sum(end - first for _, first, end in spans)
+    buffer = pltpu.VMEM((size, kv_local, slots, head_size), bf16)
+    chunks = pltpu.SemaphoreType.DMA((size // chunk,))
     in_hbm = lambda x: pltpu.with_memory_space_constraint(x, pltpu.HBM)
+    there = [] if packed is None else [in_hbm(packed)]
     return pl.pallas_call(
-        functools.partial(pack_kernel, half, chunk),
-        in_specs=[hbm] + [vmem] * 3 + [hbm] * len(there),
+        functools.partial(pack_kernel, spans, chunk),
+        in_specs=[hbm] + [vmem] * 4 + [hbm] * len(there),
         out_specs=hbm,
         out_shape=jax.ShapeDtypeStruct(page_cache.shape, bf16),
-        input_output_aliases={4: 0} if there else {},
+        input_output_aliases={5: 0} if there else {},
         scratch_shapes=[buffer, buffer, chunks, chunks],
         compiler_params=pltpu.CompilerParams(vmem_limit_bytes=24 << 20),
-        name=("pack_keys", "pack_values")[half],
-    )(in_hbm(page_cache), position, count, folded, *map(in_hbm, there))
+        name=name,
+    )(in_hbm(page_cache), position, count, fold_key, fold_value, *there)
 
 
 def attend_kernel(
-    heads, req_dev, score_scale, chunk, near_ref, far_ref, keys, kept_ref, fold_mass_ref, share_ref,
-    fold_key_ref, target_ref, slot_ref, pages_hbm, out_ref, fold_value_ref, scores, parts, values,
-    value_sem,
+    heads, req_dev, score_scale, chunk, chips, keys, kept_ref, fold_mass_ref, share_ref,
+    fold_key_ref, target_ref, slot_ref, pages_hbm, *rest,
 ):
     pages_dev, slots = kept_ref.shape
+    query_refs = rest[: 2 * chips]
+    out_ref, fold_value_ref, values, scores, parts, value_sem = rest[2 * chips :]
     kv_local = keys.shape[1]
     loads = [
         pltpu.make_async_copy(
@@ -268,13 +296,13 @@
     rows = pages_dev * heads
     spread = spread_rows(pages_dev, heads)
 
-    half = near_ref.shape[0]
     query = jnp.zeros((rows, 128), f32)
-    for n, ref in enumerate((near_ref, far_ref)):
-        for m in range(half // slots):
-            first = n * half + m * slots
-            pick = ones_where(target_ref[...] == iota((rows, slots), 1) + first)
-            query = query + dot(pick, ref[m * slots : (m + 1) * slots])
+    per_slab = slots // query_refs[0].shape[0]
+    for n in range(0, 2 * chips, per_slab):
+        slab = jnp.concatenate([ref[...] for ref in query_refs[n : n + per_slab]], axis=0)
+        first = n * query_refs[0].shape[0]
+        pick = ones_where(target_ref[...] == iota((rows, slots), 1) + first)
+        query = query + dot(pick, slab)
     query_b = query.astype(bf16)
 
     tile = 16
@@ -352,41 +380,43 @@
 
 def attend(
     near, far, keys, kept, fold_mass, share, fold_key, target, slot, page_cache, score_scale, heads,
-    req_dev, chunk=16
+    req_dev, chips, chunk=16
 ):
     pages_dev, _, kv_local, slots, head_size = page_cache.shape
     rows = pages_dev * heads
     vmem = pl.BlockSpec(memory_space=pltpu.VMEM)
     return pl.pallas_call(
-        functools.partial(attend_kernel, heads, req_dev, score_scale, chunk),
-        in_specs=[vmem] * 9 + [pl.BlockSpec(memory_space=pltpu.HBM)],
+        functools.partial(attend_kernel, heads, req_dev, score_scale, chunk, chips),
+        in_specs=[vmem] * 7 + [pl.BlockSpec(memory_space=pltpu.HBM)] + [vmem] * (2 * chips),
         out_specs=[vmem] * 2,
         out_shape=[
             jax.ShapeDtypeStruct((rows, 2 * head_size), bf16),
             jax.ShapeDtypeStruct((kv_local, pages_dev, head_size), f32),
         ],
         scratch_shapes=[
+            pltpu.VMEM((pages_dev, kv_local, slots, head_size), bf16),
             pltpu.VMEM((rows, slots), f32),
             pltpu.VMEM((rows, head_size), f32),
-            pltpu.VMEM((pages_dev, kv_local, slots, head_size), bf16),
             pltpu.SemaphoreType.DMA((pages_dev // chunk,)),
         ],
         compiler_params=pltpu.CompilerParams(vmem_limit_bytes=24 << 20),
         name="attend",
     )(
-        near, far, keys, kept, fold_mass, share, fold_key, target, slot,
-        pltpu.with_memory_space_constraint(page_cache, pltpu.HBM),
+        keys, kept, fold_mass, share, fold_key, target, slot,
+        pltpu.with_memory_space_constraint(page_cache, pltpu.HBM), *near, *far,
     )
 
 
 def combine_kernel(
-    heads, req_dev, score_scale, kv_count, rank_ref, got_ref, query_ref, fresh_key_ref,
-    fresh_value_ref, weight_ref, attended_ref, *out_refs
+    heads, kv_local, req_dev, score_scale, kv_count, rank_ref, query_ref, fresh_ref,
+    weight_ref, *rest
 ):
-    rows = got_ref.shape[0]
+    got_ref, attended_ref, *out_refs = rest
+    got = got_ref[...]
+    rows = got.shape[0]
     cols = heads * req_dev
     width = weight_ref.shape[1] // kv_count
-    stats = got_ref[:, 128:].astype(f32)
+    stats = got[:, 128:].astype(f32)
     top = stats[:, 0:1] + stats[:, 1:2] + stats[:, 2:3]
     request = stats[:, 6:7]
     row_head = (iota((rows, cols), 0) % heads).astype(f32)
@@ -394,8 +424,15 @@
     match = jnp.logical_and(
         request == (col % req_dev).astype(f32), row_head == (col // req_dev).astype(f32)
     )
+    head, request = iota((cols, 1), 0) // req_dev, iota((cols, 1), 0) % req_dev
+
+    def rows_of(ref, index):
+        return dot(ones_where(iota((cols, ref.shape[0]), 1) == index), ref[...])
+
+    fresh_row = request * (2 * kv_local) + head // (heads // kv_local)
     own = jnp.sum(
-        query_ref[...].astype(f32) * fresh_key_ref[...].astype(f32), axis=1, keepdims=True
+        rows_of(query_ref, request * heads + head) * rows_of(fresh_ref, fresh_row),
+        axis=1, keepdims=True,
     ) * score_scale
     diagonal = iota((cols, cols), 0) == iota((cols, cols), 1)
     own_row = jnp.sum(jnp.where(diagonal, own, 0.0), axis=0, keepdims=True)
@@ -405,11 +442,10 @@
     best_col = jnp.sum(jnp.where(diagonal, best, 0.0), axis=1, keepdims=True)
     factor = jnp.where(match, jnp.exp(top - best), 0.0)
     high, middle, low = pieces(factor)
-    got = got_ref[...]
     sums = dot(high, got, (0, 0)) + dot(middle, got, (0, 0)) + dot(low, got, (0, 0))
     own_factor = jnp.exp(own - best_col)
     denominator = sums[:, 131:132] + sums[:, 132:133] + sums[:, 133:134] + own_factor
-    numerator = sums[:, :128] + own_factor * fresh_value_ref[...].astype(f32)
+    numerator = sums[:, :128] + own_factor * rows_of(fresh_ref, fresh_row + kv_local)
     attended = numerator / denominator
     attended = jnp.concatenate(
         [attended[h * req_dev : (h + 1) * req_dev] for h in range(heads)], axis=1
@@ -422,14 +458,14 @@
         out_refs[k][...] = dot(attended, weight_ref[:, pl.ds(at, width)]).astype(bf16)
 
 
-def combine(rank, got, query, fresh_key, fresh_value, out_weight, score_scale, heads, kv_count):
+def combine(rank, got, query, fresh, out_weight, score_scale, heads, kv_local, kv_count):
     req_dev = query.shape[0] // heads
     vmem = pl.BlockSpec(memory_space=pltpu.VMEM)
     smem = pl.BlockSpec(memory_space=pltpu.SMEM)
     width = out_weight.shape[1] // kv_count
     return pl.pallas_call(
-        functools.partial(combine_kernel, heads, req_dev, score_scale, kv_count),
-        in_specs=[smem] + [vmem] * 5,
+        functools.partial(combine_kernel, heads, kv_local, req_dev, score_scale, kv_count),
+        in_specs=[smem] + [vmem] * 4,
         out_specs=[vmem] * (1 + kv_count),
         out_shape=[jax.ShapeDtypeStruct((req_dev, out_weight.shape[0]), bf16)]
         + [jax.ShapeDtypeStruct((req_dev, width), bf16)] * kv_count,
@@ -438,11 +474,15 @@
             flops=2 * req_dev * out_weight.size, bytes_accessed=2 * out_weight.size, transcendentals=0
         ),
         name="combine",
-    )(rank, got, query, fresh_key, fresh_value, out_weight)
+    )(rank, query, fresh, out_weight, got)
 
 
 def exchange(x, axis, count, mask):
     return lax.ppermute(x, axis, [(i, i ^ mask) for i in range(count)])
+
+
+def shift(x, axis, count, step):
+    return lax.ppermute(x, axis, [(i, (i + step) % count) for i in range(count)])
 
 
 def per_device(
@@ -455,35 +495,44 @@
     kv_rank = lax.axis_index("kv").astype(i32).reshape(1)
     _, _, kv_local, slots, head_size = page_cache.shape
     req_dev, heads, _ = queries.shape
-    groups = heads // kv_local
     score_scale = head_size ** (-0.5)
 
-    others = [exchange(queries, "seq", seq_count, 2 * k) for k in range(1, seq_count // 2)]
-    keys, own, mass, kept, fold_mass, position, count, share, fold_key, target, slot = prepare(
-        seq_rank, page_table, lengths, keep_list, fold_weight, queries, page_cache, heads, req_dev
-    )
-    near = jnp.concatenate([own] + others, axis=0).reshape(-1, head_size)
-    far = exchange(near, "seq", seq_count, 1)
+    others = {k: shift(queries, "seq", seq_count, 2 * k) for k in [2] + [k for k in range(seq_count // 2 - 1, 0, -1) if k != 2]}
+    others = [others[k] for k in range(1, seq_count // 2)]
+    keys, own, fresh, mass, kept, fold_mass, position, count, share, target, slot = prepare(
+        seq_rank, page_table, lengths, keep_list, fold_weight, queries, fresh_entries, page_cache,
+        heads, req_dev,
+    )
+    flat = lambda x: x.reshape(-1, head_size)
+    near = [flat(x) for x in [own] + others]
+    far = [exchange(x, "seq", seq_count, 1) for x in near]
+    fold_key, keys = fold_keys(keys, share)
+    fold_key, *far = lax.optimization_barrier((fold_key, *far))
     send, fold_value = attend(
         near, far, keys, kept, fold_mass, share, fold_key, target, slot, page_cache, score_scale,
-        heads, req_dev,
+        heads, req_dev, seq_count // 2,
     )
     got = lax.all_to_all(
         send.reshape(seq_count, -1, send.shape[1]), "seq", split_axis=0, concat_axis=0, tiled=True
     ).reshape(send.shape)
-    packed = pack(1, page_cache, position, count, fold_value)
+    pages_dev = page_cache.shape[0]
+    fold_key, fold_value = lax.optimization_barrier((fold_key, fold_value))
+    middle = pages_dev // 2
+    packed = pack(
+        "pack_first", [(0, 0, pages_dev), (1, 0, middle)], page_cache, position, count, fold_key,
+        fold_value,
+    )
     got, packed = lax.optimization_barrier((got, packed))
-    by_head = lambda x: x.transpose(1, 0, 2).reshape(heads * req_dev, head_size)
-    fresh = jnp.repeat(fresh_entries, groups, axis=2)
     attended, *shares = combine(
-        kv_rank, got, by_head(queries), by_head(fresh[:, 0]), by_head(fresh[:, 1]), out_weight,
-        score_scale, heads, kv_count,
-    )
-    fold_key, *shares = lax.optimization_barrier((fold_key, *shares))
+        kv_rank, got, flat(own), flat(fresh), out_weight, score_scale, heads, kv_local, kv_count,
+    )
+    packed, *shares = lax.optimization_barrier((packed, *shares))
+    packed = pack(
+        "pack_rest", [(1, middle, pages_dev)], page_cache, position, count, fold_key, fold_value, packed
+    )
     total = shares[0].astype(f32)
-    for k in range(1, kv_count):
+    for k in range(kv_count - 1, 0, -1):
         total = total + exchange(shares[k], "kv", kv_count, k).astype(f32)
-    packed = pack(0, page_cache, position, count, fold_key, packed)
     return packed, mass, attended, total.astype(bf16)
 
 

time: 37.7 us -> 35.8 us (0.950)
  waiting for transfers between devices: 5.31 us -> 1.19 us
  starting transfers between devices: 12.6 us -> 15 us
    ppermute x0 -> x3, starting transfers between devices: none -> 7.01 us  [shift(): lax.ppermute(x, axis, [(i, (i + step) % count) for i in range(count)])]
    ppermute x7, starting transfers between devices: 9.24 us -> 4.56 us  [exchange(): return lax.ppermute(x, axis, [(i, i ^ mask) for i in range(count)])]
    ppermute x7, waiting for transfers between devices: 3.12 us -> 0.15 us  [exchange(): return lax.ppermute(x, axis, [(i, i ^ mask) for i in range(count)])]
    all_to_all x1, waiting for transfers between devices: 2.19 us -> 1.03 us  [per_device(): lax.all_to_all(send.reshape(seq_count, -1, send.shape[1]), 'seq', split_a...]
    pallas_call x1, Pallas kernels: 3.69 us -> 2.95 us  [prepare(): pl.pallas_call(functools.partial(prepare_kernel, heads, req_dev, chunk),...]
    pallas_call x3 -> x4, Pallas kernels: 10 us -> 10.7 us  [the longest x2 8.71 us: pack(): pl.pallas_call(functools.partial(pack_kernel, spans, chunk), in_specs=[hb...]
  transfers between devices with their start and end apart: 8 -> 11, of which waited for: 3 -> 2; matrix products, arithmetic and copies ran while one was open for 0% -> 0% of each run, Pallas kernels for 33% -> 35%
where the time goes in v3:
time: 35.8 us; the launch traced here: 35.5 us
  Pallas kernels  18 us (50%)
  starting transfers between devices  15 us (42%)
  waiting for transfers between devices  1.19 us (3%)
  between operations  0.76 us (2%)
  other arithmetic  0.61 us (2%)
    pallas_call x2, Pallas kernels, pack(): pl.pallas_call(functools.partial(pack_kernel, spans, chunk), in_specs=[hb...  8.71 us
    ppermute x3, starting transfers between devices, shift(): lax.ppermute(x, axis, [(i, (i + step) % count) for i in range(count)])  7.01 us
    ppermute x7, starting transfers between devices, exchange(): return lax.ppermute(x, axis, [(i, i ^ mask) for i in range(count)])  4.56 us
    pallas_call x1, Pallas kernels, attend(): pl.pallas_call(functools.partial(attend_kernel, heads, req_dev, score_sca...  4.33 us
    all_to_all x1, starting transfers between devices, per_device(): lax.all_to_all(send.reshape(seq_count, -1, send.shape[1]), 'seq', split_a...  3.38 us
    pallas_call x1, Pallas kernels, prepare(): pl.pallas_call(functools.partial(prepare_kernel, heads, req_dev, chunk),...  2.95 us
    pallas_call x1, Pallas kernels, combine(): pl.pallas_call(functools.partial(combine_kernel, heads, kv_local, req_dev...  1.32 us
    all_to_all x1, waiting for transfers between devices, per_device(): lax.all_to_all(send.reshape(seq_count, -1, send.shape[1]), 'seq', split_a...  1.03 us
  transfers between devices with their start and end apart: 11, of which 2 were waited for; matrix products, arithmetic and copies ran while one was open for 0% of the time, Pallas kernels for 35%

profile of v3, /device:TPU:0, one launch (start us, length us, event | category | flops | bytes accessed | tf_op | source)
XLA Modules:
  0.0 35.5 jit_solution(3281046063464708732)
XLA Ops:
  0.6 3.1 %collective-permute-start.1 = (bf16[8,4,128]{2,1,0:T(4,128)(2,1)}, bf16[8,4,128]{2,1,0:T(4,128)(2,1)S(1)}, u32[]{:S(2)}, u32[]{:S(2)}) collective-permute-start(bf16[8,4,128]{2,1,0:T(4,128)(2,1)} %query_hbm.1), channel_id=1, source_target_pairs={{0,2},{1,3},{2,4},{3,5},{4,6},{5,7},{6,0},{7,1},{8,10},{9,11},{10,... | collective-permute-start | bytes 24584 | tf_op jit(solution)/shard_map/ppermute | solution.py:485
  3.7 2.6 %collective-permute-start.3 = (bf16[8,4,128]{2,1,0:T(4,128)(2,1)}, bf16[8,4,128]{2,1,0:T(4,128)(2,1)S(1)}, u32[]{:S(2)}, u32[]{:S(2)}) collective-permute-start(bf16[8,4,128]{2,1,0:T(4,128)(2,1)} %query_hbm.1), channel_id=1, source_target_pairs={{0,4},{1,5},{2,6},{3,7},{4,0},{5,1},{6,2},{7,3},{8,12},{9,13},{10,... | collective-permute-start | bytes 24584 | tf_op jit(solution)/shard_map/ppermute | solution.py:485
  6.3 1.3 %collective-permute-start.5 = (bf16[8,4,128]{2,1,0:T(4,128)(2,1)}, bf16[8,4,128]{2,1,0:T(4,128)(2,1)S(1)}, u32[]{:S(2)}, u32[]{:S(2)}) collective-permute-start(bf16[8,4,128]{2,1,0:T(4,128)(2,1)} %query_hbm.1), channel_id=1, source_target_pairs={{0,6},{1,7},{2,0},{3,1},{4,2},{5,3},{6,4},{7,5},{8,14},{9,15},{10,... | collective-permute-start | bytes 24584 | tf_op jit(solution)/shard_map/ppermute | solution.py:485
  7.6 2.9 %prepare.1 = (bf16[64,2,128,128]{3,2,1,0:T(8,128)(2,1)S(1)}, bf16[8,4,128]{2,1,0:T(4,128)(2,1)S(1)}, bf16[8,2,2,128]{3,2,1,0:T(2,128)(2,1)S(1)}, bf16[64,128]{1,...) custom-call(s32[1]{0:T(128)} %bitcast.rank_ref, ...), custom_call_target="tpu_custom_call" | custom-call | tf_op jit(solution)/shard_map/prepare/pallas_call | solution.py:160
  10.6 0.1 collective-permute-start
  10.7 0.5 %collective-permute-start.2 = (bf16[32,128]{1,0:T(8,128)(2,1)S(1)}, bf16[32,128]{1,0:T(8,128)(2,1)S(1)}, u32[]{:S(2)}, u32[]{:S(2)}) collective-permute-start(bf16[32,128]{1,0:T(8,128)(2,1)S(1)} %bitcast.16), channel_id=1, source_target_pairs={{0,1},{1,0},{2,3},{3,2},{4,5},{5,4},{6,7},{7,6},{8,9},{9,8},{10,11... | collective-permute-start | bytes 24584 | tf_op jit(solution)/shard_map/ppermute | solution.py:481
  11.2 0.0 collective-permute-done.3
  11.2 0.1 collective-permute-start.4
  11.3 0.0 collective-permute-done.5
  11.3 0.4 %collective-permute-start.6 = (bf16[32,128]{1,0:T(8,128)(2,1)S(1)}, bf16[32,128]{1,0:T(8,128)(2,1)S(1)}, u32[]{:S(2)}, u32[]{:S(2)}) collective-permute-start(bf16[32,128]{1,0:T(8,128)(2,1)S(1)} %bitcast.20), channel_id=1, source_target_pairs={{0,1},{1,0},{2,3},{3,2},{4,5},{5,4},{6,7},{7,6},{8,9},{9,8},{10,11... | collective-permute-start | bytes 24584 | tf_op jit(solution)/shard_map/ppermute | solution.py:481
  11.7 0.7 %fold_keys.1 = (f32[2,64,128]{2,1,0:T(8,128)S(1)}, bf16[64,2,128,128]{3,2,1,0:T(8,128)(2,1)S(1)}) custom-call(bf16[64,2,128,128]{3,2,1,0:T(8,128)(2,1)S(1)} %get-tuple-element.40.keys, f32[3,64,128]{2,1,0:T(8,128)S(1)} %get-tuple-element.41.share_ref), custom_call_target="tpu_custom_call", output_to_operand_aliasing={{1}: (0, {})} | custom-call | tf_op jit(solution)/shard_map/fold_keys/pallas_call | solution.py:210
  12.4 0.1 collective-permute-done.6.rest_7_
  12.5 4.3 %attend.1 = (bf16[256,256]{1,0:T(8,128)(2,1)}, f32[2,64,128]{2,1,0:T(8,128)S(1)}) custom-call(bf16[64,2,128,128]{3,2,1,0:T(8,128)(2,1)S(1)} %get-tuple-element.45.keys, f32[64,128]{1,0:T(8,128)S(1)} %get-tuple-element.46.kept_ref, f32[64,128]{1,0:T(8,128)S(1)} %get-tuple-element.47.fold_mass_ref, f32[3,64,128]{2,1,0:T(8,128)S(1)} %get-tuple-element.41.share_ref, ...), custom_call_target="tpu_custom_call" | custom-call | tf_op jit(solution)/shard_map/attend/pallas_call | solution.py:388
  16.9 3.4 %all-to-all-start = ((bf16[8,32,256]{2,1,0:T(8,128)(2,1)}), bf16[8,32,256]{2,1,0:T(8,128)(2,1)S(1)}, u32[]{:S(2)}, u32[]{:S(2)}) async-start(bf16[8,32,256]{2,1,0:T(8,128)(2,1)} %bitcast.7), calls=%async_computation | async-start | bytes 262144 | tf_op jit(solution)/shard_map/all_to_all | solution.py:515
  20.3 0.0 copy-start
  20.3 5.7 %pack_first.1.rest_2_ = bf16[64,2,2,128,128]{4,3,2,1,0:T(8,128)(2,1)} custom-call(bf16[64,2,2,128,128]{4,3,2,1,0:T(8,128)(2,1)} %pages_hbm.7, f32[64,128]{1,0:T(8,128)S(1)} %get-tuple-element.38.position_ref, f32[64,128]{1,0:T(8,128)S(1)} %get-tuple-element.39.count_ref, f32[2,64,128]{2,1,0:T(8,128)S(1)} %get-tuple-element.55.fold_key_ref.rest_0_, ...), custom_call_target="tpu_custom_call" | custom-call | tf_op jit(solution)/shard_map/pack_first/pallas_call | solution.py:266
  25.9 1.0 %all-to-all-done = bf16[8,32,256]{2,1,0:T(8,128)(2,1)S(1)} async-done(((bf16[8,32,256]{2,1,0:T(8,128)(2,1)}), bf16[8,32,256]{2,1,0:T(8,128)(2,1)S(1)}, u32[]{:S(2)}, u32[]{:S(2)}) %all-to-all-start) | async-done | bytes 131104 | tf_op jit(solution)/shard_map/all_to_all | solution.py:515
  27.0 1.3 %combine.1 = (bf16[8,512]{1,0:T(8,128)(2,1)}, bf16[8,512]{1,0:T(8,128)(2,1)S(1)}, bf16[8,512]{1,0:T(8,128)(2,1)S(1)}, bf16[8,512]{1,0:T(8,128)(2,1)S(1)}, bf16[8,512]{1,0:T(8,128)(2,1)S(1)}) custom-call(s32[1]{0:T(128)} %bitcast.9.rank_ref, bf16[32,128]{1,0:T(8,128)(2,1)S(1)} %bitcast.14, bf16[32,128]{1,0:T(8,128)(2,1)S(1)} %bitcast.15, ...), custom_call_target="tpu_custom_call" | custom-call | flops 16777216 | bytes 2097152 | tf_op jit(solution)/shard_map/combine/pallas_call | solution.py:466
  28.3 2.4 %collective-permute-start.7 = (bf16[8,512]{1,0:T(8,128)(2,1)S(1)}, bf16[8,512]{1,0:T(8,128)(2,1)S(1)}, u32[]{:S(2)}, u32[]{:S(2)}) collective-permute-start(bf16[8,512]{1,0:T(8,128)(2,1)S(1)} %get-tuple-element.69), channel_id=1, source_target_pairs={{0,24},{8,16},{16,8},{24,0},{1,25},{9,17},{17,9},{25,1},{2,26},{10... | collective-permute-start | bytes 24584 | tf_op jit(solution)/shard_map/ppermute | solution.py:481
  30.7 0.5 %collective-permute-start.8 = (bf16[8,512]{1,0:T(8,128)(2,1)S(1)}, bf16[8,512]{1,0:T(8,128)(2,1)S(1)}, u32[]{:S(2)}, u32[]{:S(2)}) collective-permute-start(bf16[8,512]{1,0:T(8,128)(2,1)S(1)} %get-tuple-element.70), channel_id=1, source_target_pairs={{0,16},{8,24},{16,0},{24,8},{1,17},{9,25},{17,1},{25,9},{2,18},{10... | collective-permute-start | bytes 24584 | tf_op jit(solution)/shard_map/ppermute | solution.py:481
  31.2 0.5 %collective-permute-start.9 = (bf16[8,512]{1,0:T(8,128)(2,1)S(1)}, bf16[8,512]{1,0:T(8,128)(2,1)S(1)}, u32[]{:S(2)}, u32[]{:S(2)}) collective-permute-start(bf16[8,512]{1,0:T(8,128)(2,1)S(1)} %get-tuple-element.71), channel_id=1, source_target_pairs={{0,8},{8,0},{16,24},{24,16},{1,9},{9,1},{17,25},{25,17},{2,10},{10... | collective-permute-start | bytes 24584 | tf_op jit(solution)/shard_map/ppermute | solution.py:481
  31.8 3.1 %pack_rest.1 = bf16[64,2,2,128,128]{4,3,2,1,0:T(8,128)(2,1)} custom-call(bf16[64,2,2,128,128]{4,3,2,1,0:T(8,128)(2,1)} %pages_hbm.7, f32[64,128]{1,0:T(8,128)S(1)} %get-tuple-element.38.position_ref, f32[64,128]{1,0:T(8,128)S(1)} %get-tuple-element.39.count_ref, ...), custom_call_target="tpu_custom_call", output_to_operand_aliasing={{}: (5, {})} | custom-call | tf_op jit(solution)/shard_map/pack_rest/pallas_call | solution.py:266
  34.9 0.0 collective-permute-done.9
  34.9 0.6 %add_convert_fusion = bf16[8,512]{1,0:T(8,128)(2,1)} fusion(bf16[8,512]{1,0:T(8,128)(2,1)S(1)} %collective-permute-done.9, bf16[8,512]{1,0:T(8,128)(2,1)S(1)} %collective-permute-done.8, bf16[8,512]{1,0:T(8,128)(2,1)S(1)} %collective-permute-done.7, bf16[8,512]{1,0:T(8,128)(2,1)S(1)} %get-tuple-element.68), kind=kLoop, calls=%fused_computation | loop fusion | flops 32768 | bytes 40960 | tf_op jit(solution)/shard_map/convert_element_type | solution.py:536
  (7 shorter events, 0.0 us)
Async XLA Ops:
  0.6 10.1 %collective-permute-start.1 = (bf16[8,4,128]{2,1,0:T(4,128)(2,1)}, bf16[8,4,128]{2,1,0:T(4,128)(2,1)S(1)}, u32[]{:S(2)}, u32[]{:S(2)}) collective-permute-start(bf16[8,4,128]{2,1,0:T(4,128)(2,1)} %query_hbm.1), channel_id=1, source_target_pairs={{0,2},{1,3},{2,4},{3,5},{4,6},{5,7},{6,0},{7,1},{8,10},{9,11},{10,... | collective-permute-start | bytes 24584 | tf_op jit(solution)/shard_map/ppermute | solution.py:485
  3.7 7.5 %collective-permute-start.3 = (bf16[8,4,128]{2,1,0:T(4,128)(2,1)}, bf16[8,4,128]{2,1,0:T(4,128)(2,1)S(1)}, u32[]{:S(2)}, u32[]{:S(2)}) collective-permute-start(bf16[8,4,128]{2,1,0:T(4,128)(2,1)} %query_hbm.1), channel_id=1, source_target_pairs={{0,4},{1,5},{2,6},{3,7},{4,0},{5,1},{6,2},{7,3},{8,12},{9,13},{10,... | collective-permute-start | bytes 24584 | tf_op jit(solution)/shard_map/ppermute | solution.py:485
  6.3 5.0 %collective-permute-start.5 = (bf16[8,4,128]{2,1,0:T(4,128)(2,1)}, bf16[8,4,128]{2,1,0:T(4,128)(2,1)S(1)}, u32[]{:S(2)}, u32[]{:S(2)}) collective-permute-start(bf16[8,4,128]{2,1,0:T(4,128)(2,1)} %query_hbm.1), channel_id=1, source_target_pairs={{0,6},{1,7},{2,0},{3,1},{4,2},{5,3},{6,4},{7,5},{8,14},{9,15},{10,... | collective-permute-start | bytes 24584 | tf_op jit(solution)/shard_map/ppermute | solution.py:485
  10.6 1.8 %collective-permute-start = (bf16[32,128]{1,0:T(8,128)(2,1)S(1)}, bf16[32,128]{1,0:T(8,128)(2,1)S(1)}, u32[]{:S(2)}, u32[]{:S(2)}) collective-permute-start(bf16[32,128]{1,0:T(8,128)(2,1)S(1)} %bitcast.12), channel_id=1, source_target_pairs={{0,1},{1,0},{2,3},{3,2},{4,5},{5,4},{6,7},{7,6},{8,9},{9,8},{10,11... | collective-permute-start | bytes 24584 | tf_op jit(solution)/shard_map/ppermute | solution.py:481
  10.7 1.7 %collective-permute-start.2 = (bf16[32,128]{1,0:T(8,128)(2,1)S(1)}, bf16[32,128]{1,0:T(8,128)(2,1)S(1)}, u32[]{:S(2)}, u32[]{:S(2)}) collective-permute-start(bf16[32,128]{1,0:T(8,128)(2,1)S(1)} %bitcast.16), channel_id=1, source_target_pairs={{0,1},{1,0},{2,3},{3,2},{4,5},{5,4},{6,7},{7,6},{8,9},{9,8},{10,11... | collective-permute-start | bytes 24584 | tf_op jit(solution)/shard_map/ppermute | solution.py:481
  11.2 1.2 %collective-permute-start.4 = (bf16[32,128]{1,0:T(8,128)(2,1)S(1)}, bf16[32,128]{1,0:T(8,128)(2,1)S(1)}, u32[]{:S(2)}, u32[]{:S(2)}) collective-permute-start(bf16[32,128]{1,0:T(8,128)(2,1)S(1)} %bitcast.18), channel_id=1, source_target_pairs={{0,1},{1,0},{2,3},{3,2},{4,5},{5,4},{6,7},{7,6},{8,9},{9,8},{10,11... | collective-permute-start | bytes 24584 | tf_op jit(solution)/shard_map/ppermute | solution.py:481
  11.3 1.3 %collective-permute-start.6 = (bf16[32,128]{1,0:T(8,128)(2,1)S(1)}, bf16[32,128]{1,0:T(8,128)(2,1)S(1)}, u32[]{:S(2)}, u32[]{:S(2)}) collective-permute-start(bf16[32,128]{1,0:T(8,128)(2,1)S(1)} %bitcast.20), channel_id=1, source_target_pairs={{0,1},{1,0},{2,3},{3,2},{4,5},{5,4},{6,7},{7,6},{8,9},{9,8},{10,11... | collective-permute-start | bytes 24584 | tf_op jit(solution)/shard_map/ppermute | solution.py:481
  16.9 10.1 %all-to-all-start = ((bf16[8,32,256]{2,1,0:T(8,128)(2,1)}), bf16[8,32,256]{2,1,0:T(8,128)(2,1)S(1)}, u32[]{:S(2)}, u32[]{:S(2)}) async-start(bf16[8,32,256]{2,1,0:T(8,128)(2,1)} %bitcast.7), calls=%async_computation | async-start | bytes 262144 | tf_op jit(solution)/shard_map/all_to_all | solution.py:515
  20.3 6.7 %copy-start = (bf16[512,2048]{1,0:T(8,128)(2,1)S(1)}, bf16[512,2048]{1,0:T(8,128)(2,1)}, u32[]{:S(2)}) copy-start(bf16[512,2048]{1,0:T(8,128)(2,1)} %weight_ref.1) | copy-start | bytes 6291460
  28.3 6.6 %collective-permute-start.7 = (bf16[8,512]{1,0:T(8,128)(2,1)S(1)}, bf16[8,512]{1,0:T(8,128)(2,1)S(1)}, u32[]{:S(2)}, u32[]{:S(2)}) collective-permute-start(bf16[8,512]{1,0:T(8,128)(2,1)S(1)} %get-tuple-element.69), channel_id=1, source_target_pairs={{0,24},{8,16},{16,8},{24,0},{1,25},{9,17},{17,9},{25,1},{2,26},{10... | collective-permute-start | bytes 24584 | tf_op jit(solution)/shard_map/ppermute | solution.py:481
  30.7 4.1 %collective-permute-start.8 = (bf16[8,512]{1,0:T(8,128)(2,1)S(1)}, bf16[8,512]{1,0:T(8,128)(2,1)S(1)}, u32[]{:S(2)}, u32[]{:S(2)}) collective-permute-start(bf16[8,512]{1,0:T(8,128)(2,1)S(1)} %get-tuple-element.70), channel_id=1, source_target_pairs={{0,16},{8,24},{16,0},{24,8},{1,17},{9,25},{17,1},{25,9},{2,18},{10... | collective-permute-start | bytes 24584 | tf_op jit(solution)/shard_map/ppermute | solution.py:481
  31.2 3.7 %collective-permute-start.9 = (bf16[8,512]{1,0:T(8,128)(2,1)S(1)}, bf16[8,512]{1,0:T(8,128)(2,1)S(1)}, u32[]{:S(2)}, u32[]{:S(2)}) collective-permute-start(bf16[8,512]{1,0:T(8,128)(2,1)S(1)} %get-tuple-element.71), channel_id=1, source_target_pairs={{0,8},{8,0},{16,24},{24,16},{1,9},{9,1},{17,25},{25,17},{2,10},{10... | collective-permute-start | bytes 24584 | tf_op jit(solution)/shard_map/ppermute | solution.py:481

commit v4 on v3

--- a/solution.py
+++ b/solution.py
@@ -64,7 +64,7 @@
 
 def prepare_kernel(
     heads, req_dev, chunk, rank_ref, table_hbm, lengths_hbm, keep_hbm, weight_hbm, query_hbm,
-    fresh_hbm, pages_hbm, keys, query_ref, fresh_ref, mass_ref, kept_ref, fold_mass_ref, position_ref, count_ref, share_ref,
+    fresh_hbm, pages_hbm, keys, values, query_ref, fresh_ref, mass_ref, kept_ref, fold_mass_ref, position_ref, count_ref, share_ref,
     target_ref, slot_ref,
     table_ref, lengths_ref, keep_ref, weight_ref, small_sem, in_sem,
 ):
@@ -83,8 +83,10 @@
         copy.start()
     loads = [
         pltpu.make_async_copy(
-            pages_hbm.at[pl.ds(n * chunk, chunk), 0], keys.at[pl.ds(n * chunk, chunk)], in_sem.at[n]
+            pages_hbm.at[pl.ds(n * chunk, chunk), half], held.at[pl.ds(n * chunk, chunk)],
+            in_sem.at[half, n],
         )
+        for half, held in enumerate((keys, values))
         for n in range(chunks)
     ]
     for copy in loads:
@@ -160,8 +162,9 @@
     return pl.pallas_call(
         functools.partial(prepare_kernel, heads, req_dev, chunk),
         in_specs=[pl.BlockSpec(memory_space=pltpu.SMEM)] + [hbm] * 7,
-        out_specs=[vmem] * 11,
+        out_specs=[vmem] * 12,
         out_shape=[
+            pltpu.VMEM((pages_dev, kv_local, slots, head_size), bf16),
             pltpu.VMEM((pages_dev, kv_local, slots, head_size), bf16),
             pltpu.VMEM(queries.shape, bf16),
             pltpu.VMEM(fresh_entries.shape, bf16),
@@ -180,7 +183,7 @@
             pltpu.VMEM(small, i32),
             pltpu.VMEM(small, f32),
             pltpu.SemaphoreType.DMA((6,)),
-            pltpu.SemaphoreType.DMA((chunks,)),
+            pltpu.SemaphoreType.DMA((2, chunks)),
         ],
         compiler_params=pltpu.CompilerParams(vmem_limit_bytes=24 << 20),
         name="prepare",
@@ -275,34 +278,28 @@
     )(in_hbm(page_cache), position, count, fold_key, fold_value, *there)
 
 
+def message(rows, peers):
+    each = rows // peers
+    return (peers * (each + each // 4), 128) if each % 32 == 0 else (rows, 256)
+
+
 def attend_kernel(
-    heads, req_dev, score_scale, chunk, chips, keys, kept_ref, fold_mass_ref, share_ref,
-    fold_key_ref, target_ref, slot_ref, pages_hbm, *rest,
+    heads, req_dev, score_scale, peers, keys, kept_ref, fold_mass_ref, share_ref,
+    fold_key_ref, target_ref, slot_ref, values, *rest,
 ):
     pages_dev, slots = kept_ref.shape
-    query_refs = rest[: 2 * chips]
-    out_ref, fold_value_ref, values, scores, parts, value_sem = rest[2 * chips :]
+    query_refs = rest[:2]
+    out_ref, fold_value_ref, scores, parts = rest[2:]
     kv_local = keys.shape[1]
-    loads = [
-        pltpu.make_async_copy(
-            pages_hbm.at[pl.ds(n * chunk, chunk), 1], values.at[pl.ds(n * chunk, chunk)],
-            value_sem.at[n],
-        )
-        for n in range(pages_dev // chunk)
-    ]
-    for copy in loads:
-        copy.start()
     groups = heads // kv_local
     rows = pages_dev * heads
     spread = spread_rows(pages_dev, heads)
 
     query = jnp.zeros((rows, 128), f32)
-    per_slab = slots // query_refs[0].shape[0]
-    for n in range(0, 2 * chips, per_slab):
-        slab = jnp.concatenate([ref[...] for ref in query_refs[n : n + per_slab]], axis=0)
-        first = n * query_refs[0].shape[0]
+    held = jnp.concatenate([ref[...] for ref in query_refs], axis=0)
+    for first in range(0, held.shape[0], slots):
         pick = ones_where(target_ref[...] == iota((rows, slots), 1) + first)
-        query = query + dot(pick, slab)
+        query = query + dot(pick, held[first : first + slots])
     query_b = query.astype(bf16)
 
     tile = 16
@@ -351,8 +348,6 @@
     weight_b = weight.astype(bf16)
 
     for first in range(0, pages_dev, tile_pages):
-        if first % chunk == 0:
-            loads[first // chunk].wait()
         at = first * heads
         results = []
         for i in range(tile_pages):
@@ -375,44 +370,70 @@
     send = jnp.concatenate([part.astype(bf16), stats.astype(bf16)], axis=1)
     place = slot_ref[:1] * heads + (iota((1, rows), 1) % heads).astype(f32)
     move = ones_where(iota((rows, rows), 0).astype(f32) == place)
-    out_ref[...] = dot(move, send).astype(bf16)
+    placed = dot(move, send)
+    each = rows // peers
+    if out_ref.shape[1] == 256:
+        out_ref[...] = placed.astype(bf16)
+    else:
+        quarter = each // 4
+        message_rows = []
+        for n in range(peers):
+            mine = placed[n * each : (n + 1) * each]
+            message_rows.append(mine[:, :128])
+            message_rows.append(
+                mine[:quarter, 128:]
+                + sum(
+                    jnp.roll(mine[k * quarter : (k + 1) * quarter, 128:], 32 * k, axis=1)
+                    for k in range(1, 4)
+                )
+            )
+        out_ref[...] = jnp.concatenate(message_rows, axis=0).astype(bf16)
 
 
 def attend(
-    near, far, keys, kept, fold_mass, share, fold_key, target, slot, page_cache, score_scale, heads,
-    req_dev, chips, chunk=16
+    near, far, keys, kept, fold_mass, share, fold_key, target, slot, values, score_scale, heads,
+    req_dev, peers
 ):
-    pages_dev, _, kv_local, slots, head_size = page_cache.shape
+    pages_dev, kv_local, slots, head_size = values.shape
     rows = pages_dev * heads
     vmem = pl.BlockSpec(memory_space=pltpu.VMEM)
     return pl.pallas_call(
-        functools.partial(attend_kernel, heads, req_dev, score_scale, chunk, chips),
-        in_specs=[vmem] * 7 + [pl.BlockSpec(memory_space=pltpu.HBM)] + [vmem] * (2 * chips),
+        functools.partial(attend_kernel, heads, req_dev, score_scale, peers),
+        in_specs=[vmem] * 10,
         out_specs=[vmem] * 2,
         out_shape=[
-            jax.ShapeDtypeStruct((rows, 2 * head_size), bf16),
+            jax.ShapeDtypeStruct(message(rows, peers), bf16),
             jax.ShapeDtypeStruct((kv_local, pages_dev, head_size), f32),
         ],
         scratch_shapes=[
-            pltpu.VMEM((pages_dev, kv_local, slots, head_size), bf16),
             pltpu.VMEM((rows, slots), f32),
             pltpu.VMEM((rows, head_size), f32),
-            pltpu.SemaphoreType.DMA((pages_dev // chunk,)),
         ],
         compiler_params=pltpu.CompilerParams(vmem_limit_bytes=24 << 20),
         name="attend",
     )(
-        keys, kept, fold_mass, share, fold_key, target, slot,
-        pltpu.with_memory_space_constraint(page_cache, pltpu.HBM), *near, *far,
+        keys, kept, fold_mass, share, fold_key, target, slot, values, *near, *far,
     )
 
 
 def combine_kernel(
-    heads, kv_local, req_dev, score_scale, kv_count, rank_ref, query_ref, fresh_ref,
+    heads, kv_local, req_dev, score_scale, kv_count, peers, rank_ref, query_ref, fresh_ref,
     weight_ref, *rest
 ):
     got_ref, attended_ref, *out_refs = rest
     got = got_ref[...]
+    if got.shape[1] == 128:
+        size = got.shape[0] // peers
+        each = size * 4 // 5
+        got = got.astype(f32)
+        own_rows, stat_rows = [], []
+        for n in range(peers):
+            own_rows.append(got[n * size : n * size + each])
+            together = got[n * size + each : (n + 1) * size]
+            stat_rows += [together] + [jnp.roll(together, 128 - 32 * k, axis=1) for k in range(1, 4)]
+        got = jnp.concatenate(
+            [jnp.concatenate(own_rows, axis=0), jnp.concatenate(stat_rows, axis=0)], axis=1
+        ).astype(bf16)
     rows = got.shape[0]
     cols = heads * req_dev
     width = weight_ref.shape[1] // kv_count
@@ -458,13 +479,13 @@
         out_refs[k][...] = dot(attended, weight_ref[:, pl.ds(at, width)]).astype(bf16)
 
 
-def combine(rank, got, query, fresh, out_weight, score_scale, heads, kv_local, kv_count):
+def combine(rank, got, query, fresh, out_weight, score_scale, heads, kv_local, kv_count, peers):
     req_dev = query.shape[0] // heads
     vmem = pl.BlockSpec(memory_space=pltpu.VMEM)
     smem = pl.BlockSpec(memory_space=pltpu.SMEM)
     width = out_weight.shape[1] // kv_count
     return pl.pallas_call(
-        functools.partial(combine_kernel, heads, kv_local, req_dev, score_scale, kv_count),
+        functools.partial(combine_kernel, heads, kv_local, req_dev, score_scale, kv_count, peers),
         in_specs=[smem] + [vmem] * 4,
         out_specs=[vmem] * (1 + kv_count),
         out_shape=[jax.ShapeDtypeStruct((req_dev, out_weight.shape[0]), bf16)]
@@ -499,18 +520,19 @@
 
     others = {k: shift(queries, "seq", seq_count, 2 * k) for k in [2] + [k for k in range(seq_count // 2 - 1, 0, -1) if k != 2]}
     others = [others[k] for k in range(1, seq_count // 2)]
-    keys, own, fresh, mass, kept, fold_mass, position, count, share, target, slot = prepare(
+    keys, values, own, fresh, mass, kept, fold_mass, position, count, share, target, slot = prepare(
         seq_rank, page_table, lengths, keep_list, fold_weight, queries, fresh_entries, page_cache,
         heads, req_dev,
     )
     flat = lambda x: x.reshape(-1, head_size)
-    near = [flat(x) for x in [own] + others]
-    far = [exchange(x, "seq", seq_count, 1) for x in near]
+    own, *others = lax.optimization_barrier((own, *others))
+    near = [jnp.concatenate([flat(x) for x in [own] + others])]
+    far = [exchange(near[0], "seq", seq_count, 1)]
     fold_key, keys = fold_keys(keys, share)
     fold_key, *far = lax.optimization_barrier((fold_key, *far))
     send, fold_value = attend(
-        near, far, keys, kept, fold_mass, share, fold_key, target, slot, page_cache, score_scale,
-        heads, req_dev, seq_count // 2,
+        near, far, keys, kept, fold_mass, share, fold_key, target, slot, values, score_scale,
+        heads, req_dev, seq_count,
     )
     got = lax.all_to_all(
         send.reshape(seq_count, -1, send.shape[1]), "seq", split_axis=0, concat_axis=0, tiled=True
@@ -525,6 +547,7 @@
     got, packed = lax.optimization_barrier((got, packed))
     attended, *shares = combine(
         kv_rank, got, flat(own), flat(fresh), out_weight, score_scale, heads, kv_local, kv_count,
+        seq_count,
     )
     packed, *shares = lax.optimization_barrier((packed, *shares))
     packed = pack(

time: 35.8 us -> 35.1 us (0.980)
  starting transfers between devices: 15 us -> 13.9 us
  Pallas kernels: 18 us -> 18.7 us
    pallas_call x1, Pallas kernels: 2.95 us -> 4.19 us  [prepare(): pl.pallas_call(functools.partial(prepare_kernel, heads, req_dev, chunk),...]
    ppermute x7 -> x4, starting transfers between devices: 4.56 us -> 3.56 us  [exchange(): return lax.ppermute(x, axis, [(i, i ^ mask) for i in range(count)])]
    all_to_all x1, waiting for transfers between devices: 1.03 us -> 0.37 us  [per_device(): lax.all_to_all(send.reshape(seq_count, -1, send.shape[1]), 'seq', split_a...]
    pallas_call x1, Pallas kernels: 4.33 us -> 3.73 us  [attend(): pl.pallas_call(functools.partial(attend_kernel, heads, req_dev, score_sca...]
    ppermute x7 -> x4, waiting for transfers between devices: 0.15 us -> 0.53 us  [exchange(): return lax.ppermute(x, axis, [(i, i ^ mask) for i in range(count)])]
  transfers between devices with their start and end apart: 11 -> 8, of which waited for: 2 -> 2; matrix products, arithmetic and copies ran while one was open for 0% -> 0% of each run, Pallas kernels for 35% -> 39%
where the time goes in v4:
time: 35.1 us; the launch traced here: 34.9 us
  Pallas kernels  18.7 us (53%)
  starting transfers between devices  13.9 us (40%)
  waiting for transfers between devices  0.91 us (3%)
  between operations  0.75 us (2%)
  other arithmetic  0.61 us (2%)
    pallas_call x2, Pallas kernels, pack(): pl.pallas_call(functools.partial(pack_kernel, spans, chunk), in_specs=[hb...  8.71 us
    ppermute x3, starting transfers between devices, shift(): lax.ppermute(x, axis, [(i, (i + step) % count) for i in range(count)])  7.01 us
    pallas_call x1, Pallas kernels, prepare(): pl.pallas_call(functools.partial(prepare_kernel, heads, req_dev, chunk),...  4.19 us
    pallas_call x1, Pallas kernels, attend(): pl.pallas_call(functools.partial(attend_kernel, heads, req_dev, score_sca...  3.73 us
    ppermute x4, starting transfers between devices, exchange(): return lax.ppermute(x, axis, [(i, i ^ mask) for i in range(count)])  3.56 us
    all_to_all x1, starting transfers between devices, per_device(): lax.all_to_all(send.reshape(seq_count, -1, send.shape[1]), 'seq', split_a...  3.36 us
    pallas_call x1, Pallas kernels, combine(): pl.pallas_call(functools.partial(combine_kernel, heads, kv_local, req_dev...  1.38 us
  transfers between devices with their start and end apart: 8, of which 2 were waited for; matrix products, arithmetic and copies ran while one was open for 0% of the time, Pallas kernels for 39%

profile of v4, /device:TPU:0, one launch (start us, length us, event | category | flops | bytes accessed | tf_op | source)
XLA Modules:
  0.0 34.9 jit_solution(17792614338117283009)
XLA Ops:
  0.6 3.1 %collective-permute-start = (bf16[8,4,128]{2,1,0:T(4,128)(2,1)}, bf16[8,4,128]{2,1,0:T(4,128)(2,1)S(1)}, u32[]{:S(2)}, u32[]{:S(2)}) collective-permute-start(bf16[8,4,128]{2,1,0:T(4,128)(2,1)} %query_hbm.1), channel_id=1, source_target_pairs={{0,2},{1,3},{2,4},{3,5},{4,6},{5,7},{6,0},{7,1},{8,10},{9,11},{10,... | collective-permute-start | bytes 24584 | tf_op jit(solution)/shard_map/ppermute | solution.py:506
  3.7 2.6 %collective-permute-start.1 = (bf16[8,4,128]{2,1,0:T(4,128)(2,1)}, bf16[8,4,128]{2,1,0:T(4,128)(2,1)S(1)}, u32[]{:S(2)}, u32[]{:S(2)}) collective-permute-start(bf16[8,4,128]{2,1,0:T(4,128)(2,1)} %query_hbm.1), channel_id=1, source_target_pairs={{0,4},{1,5},{2,6},{3,7},{4,0},{5,1},{6,2},{7,3},{8,12},{9,13},{10,... | collective-permute-start | bytes 24584 | tf_op jit(solution)/shard_map/ppermute | solution.py:506
  6.3 1.3 %collective-permute-start.2 = (bf16[8,4,128]{2,1,0:T(4,128)(2,1)}, bf16[8,4,128]{2,1,0:T(4,128)(2,1)S(1)}, u32[]{:S(2)}, u32[]{:S(2)}) collective-permute-start(bf16[8,4,128]{2,1,0:T(4,128)(2,1)} %query_hbm.1), channel_id=1, source_target_pairs={{0,6},{1,7},{2,0},{3,1},{4,2},{5,3},{6,4},{7,5},{8,14},{9,15},{10,... | collective-permute-start | bytes 24584 | tf_op jit(solution)/shard_map/ppermute | solution.py:506
  7.6 4.2 %prepare.1 = (bf16[64,2,128,128]{3,2,1,0:T(8,128)(2,1)S(1)}, bf16[64,2,128,128]{3,2,1,0:T(8,128)(2,1)S(1)}, bf16[8,4,128]{2,1,0:T(4,128)(2,1)S(1)}, bf16[8,2,2,1...) custom-call(s32[1]{0:T(128)} %bitcast.rank_ref, ...), custom_call_target="tpu_custom_call" | custom-call | tf_op jit(solution)/shard_map/prepare/pallas_call | solution.py:162
  11.8 0.0 collective-permute-done
  11.9 0.0 collective-permute-done.1
  11.9 0.0 collective-permute-done.2
  11.9 0.1 collective-permute-start.3
  12.0 0.7 %fold_keys.1 = (f32[2,64,128]{2,1,0:T(8,128)S(1)}, bf16[64,2,128,128]{3,2,1,0:T(8,128)(2,1)S(1)}) custom-call(bf16[64,2,128,128]{3,2,1,0:T(8,128)(2,1)S(1)} %get-tuple-element.42.keys, f32[3,64,128]{2,1,0:T(8,128)S(1)} %get-tuple-element.43.share_ref), custom_call_target="tpu_custom_call", output_to_operand_aliasing={{1}: (0, {})} | custom-call | tf_op jit(solution)/shard_map/fold_keys/pallas_call | solution.py:213
  12.7 0.5 %collective-permute-done.3.rest_1_ = bf16[128,128]{1,0:T(8,128)(2,1)S(1)} collective-permute-done((bf16[128,128]{1,0:T(8,128)(2,1)S(1)}, bf16[128,128]{1,0:T(8,128)(2,1)S(1)}, u32[]{:S(2)}, u32[]{:S(2)}) %collective-permute-start.3) | collective-permute-done | bytes 32800 | tf_op jit(solution)/shard_map/ppermute | solution.py:502
  13.2 3.7 %attend.1 = (bf16[320,128]{1,0:T(8,128)(2,1)}, f32[2,64,128]{2,1,0:T(8,128)S(1)}) custom-call(bf16[64,2,128,128]{3,2,1,0:T(8,128)(2,1)S(1)} %get-tuple-element.51.keys, f32[64,128]{1,0:T(8,128)S(1)} %get-tuple-element.52.kept_ref, f32[64,128]{1,0:T(8,128)S(1)} %get-tuple-element.53.fold_mass_ref, f32[3,64,128]{2,1,0:T(8,128)S(1)} %get-tuple-element.43.share_ref, ...), custom_call_target="tpu_custom_call" | custom-call | tf_op jit(solution)/shard_map/attend/pallas_call | solution.py:400
  16.9 3.4 %all-to-all-start = ((bf16[8,40,128]{2,1,0:T(8,128)(2,1)}), bf16[8,40,128]{2,1,0:T(8,128)(2,1)S(1)}, u32[]{:S(2)}, u32[]{:S(2)}) async-start(bf16[8,40,128]{2,1,0:T(8,128)(2,1)} %bitcast.7), calls=%async_computation | async-start | bytes 163840 | tf_op jit(solution)/shard_map/all_to_all | solution.py:537
  20.3 0.0 copy-start
  20.3 5.7 %pack_first.1.rest_2_ = bf16[64,2,2,128,128]{4,3,2,1,0:T(8,128)(2,1)} custom-call(bf16[64,2,2,128,128]{4,3,2,1,0:T(8,128)(2,1)} %pages_hbm.5, f32[64,128]{1,0:T(8,128)S(1)} %get-tuple-element.40.position_ref, f32[64,128]{1,0:T(8,128)S(1)} %get-tuple-element.41.count_ref, f32[2,64,128]{2,1,0:T(8,128)S(1)} %get-tuple-element.59.fold_key_ref.rest_0_, ...), custom_call_target="tpu_custom_call" | custom-call | tf_op jit(solution)/shard_map/pack_first/pallas_call | solution.py:269
  25.9 0.4 %all-to-all-done = bf16[8,40,128]{2,1,0:T(8,128)(2,1)S(1)} async-done(((bf16[8,40,128]{2,1,0:T(8,128)(2,1)}), bf16[8,40,128]{2,1,0:T(8,128)(2,1)S(1)}, u32[]{:S(2)}, u32[]{:S(2)}) %all-to-all-start) | async-done | bytes 81952 | tf_op jit(solution)/shard_map/all_to_all | solution.py:537
  26.3 1.4 %combine.1 = (bf16[8,512]{1,0:T(8,128)(2,1)}, bf16[8,512]{1,0:T(8,128)(2,1)S(1)}, bf16[8,512]{1,0:T(8,128)(2,1)S(1)}, bf16[8,512]{1,0:T(8,128)(2,1)S(1)}, bf16[8,512]{1,0:T(8,128)(2,1)S(1)}) custom-call(s32[1]{0:T(128)} %bitcast.9.rank_ref, bf16[32,128]{1,0:T(8,128)(2,1)S(1)} %bitcast.13, bf16[32,128]{1,0:T(8,128)(2,1)S(1)} %bitcast.14, ...), custom_call_target="tpu_custom_call" | custom-call | flops 16777216 | bytes 2097152 | tf_op jit(solution)/shard_map/combine/pallas_call | solution.py:487
  27.7 2.4 %collective-permute-start.4 = (bf16[8,512]{1,0:T(8,128)(2,1)S(1)}, bf16[8,512]{1,0:T(8,128)(2,1)S(1)}, u32[]{:S(2)}, u32[]{:S(2)}) collective-permute-start(bf16[8,512]{1,0:T(8,128)(2,1)S(1)} %get-tuple-element.73), channel_id=1, source_target_pairs={{0,24},{8,16},{16,8},{24,0},{1,25},{9,17},{17,9},{25,1},{2,26},{10... | collective-permute-start | bytes 24584 | tf_op jit(solution)/shard_map/ppermute | solution.py:502
  30.1 0.5 %collective-permute-start.5 = (bf16[8,512]{1,0:T(8,128)(2,1)S(1)}, bf16[8,512]{1,0:T(8,128)(2,1)S(1)}, u32[]{:S(2)}, u32[]{:S(2)}) collective-permute-start(bf16[8,512]{1,0:T(8,128)(2,1)S(1)} %get-tuple-element.74), channel_id=1, source_target_pairs={{0,16},{8,24},{16,0},{24,8},{1,17},{9,25},{17,1},{25,9},{2,18},{10... | collective-permute-start | bytes 24584 | tf_op jit(solution)/shard_map/ppermute | solution.py:502
  30.6 0.5 %collective-permute-start.6 = (bf16[8,512]{1,0:T(8,128)(2,1)S(1)}, bf16[8,512]{1,0:T(8,128)(2,1)S(1)}, u32[]{:S(2)}, u32[]{:S(2)}) collective-permute-start(bf16[8,512]{1,0:T(8,128)(2,1)S(1)} %get-tuple-element.75), channel_id=1, source_target_pairs={{0,8},{8,0},{16,24},{24,16},{1,9},{9,1},{17,25},{25,17},{2,10},{10... | collective-permute-start | bytes 24584 | tf_op jit(solution)/shard_map/ppermute | solution.py:502
  31.2 3.1 %pack_rest.1 = bf16[64,2,2,128,128]{4,3,2,1,0:T(8,128)(2,1)} custom-call(bf16[64,2,2,128,128]{4,3,2,1,0:T(8,128)(2,1)} %pages_hbm.5, f32[64,128]{1,0:T(8,128)S(1)} %get-tuple-element.40.position_ref, f32[64,128]{1,0:T(8,128)S(1)} %get-tuple-element.41.count_ref, ...), custom_call_target="tpu_custom_call", output_to_operand_aliasing={{}: (5, {})} | custom-call | tf_op jit(solution)/shard_map/pack_rest/pallas_call | solution.py:269
  34.2 0.0 collective-permute-done.4
  34.3 0.0 collective-permute-done.5
  34.3 0.0 collective-permute-done.6
  34.3 0.6 %add_convert_fusion = bf16[8,512]{1,0:T(8,128)(2,1)} fusion(bf16[8,512]{1,0:T(8,128)(2,1)S(1)} %collective-permute-done.6, bf16[8,512]{1,0:T(8,128)(2,1)S(1)} %collective-permute-done.5, bf16[8,512]{1,0:T(8,128)(2,1)S(1)} %collective-permute-done.4, bf16[8,512]{1,0:T(8,128)(2,1)S(1)} %get-tuple-element.72), kind=kLoop, calls=%fused_computation.1 | loop fusion | flops 32768 | bytes 40960 | tf_op jit(solution)/shard_map/convert_element_type | solution.py:559
  (2 shorter events, 0.0 us)
Async XLA Ops:
  0.6 11.2 %collective-permute-start = (bf16[8,4,128]{2,1,0:T(4,128)(2,1)}, bf16[8,4,128]{2,1,0:T(4,128)(2,1)S(1)}, u32[]{:S(2)}, u32[]{:S(2)}) collective-permute-start(bf16[8,4,128]{2,1,0:T(4,128)(2,1)} %query_hbm.1), channel_id=1, source_target_pairs={{0,2},{1,3},{2,4},{3,5},{4,6},{5,7},{6,0},{7,1},{8,10},{9,11},{10,... | collective-permute-start | bytes 24584 | tf_op jit(solution)/shard_map/ppermute | solution.py:506
  3.7 8.2 %collective-permute-start.1 = (bf16[8,4,128]{2,1,0:T(4,128)(2,1)}, bf16[8,4,128]{2,1,0:T(4,128)(2,1)S(1)}, u32[]{:S(2)}, u32[]{:S(2)}) collective-permute-start(bf16[8,4,128]{2,1,0:T(4,128)(2,1)} %query_hbm.1), channel_id=1, source_target_pairs={{0,4},{1,5},{2,6},{3,7},{4,0},{5,1},{6,2},{7,3},{8,12},{9,13},{10,... | collective-permute-start | bytes 24584 | tf_op jit(solution)/shard_map/ppermute | solution.py:506
  6.3 5.6 %collective-permute-start.2 = (bf16[8,4,128]{2,1,0:T(4,128)(2,1)}, bf16[8,4,128]{2,1,0:T(4,128)(2,1)S(1)}, u32[]{:S(2)}, u32[]{:S(2)}) collective-permute-start(bf16[8,4,128]{2,1,0:T(4,128)(2,1)} %query_hbm.1), channel_id=1, source_target_pairs={{0,6},{1,7},{2,0},{3,1},{4,2},{5,3},{6,4},{7,5},{8,14},{9,15},{10,... | collective-permute-start | bytes 24584 | tf_op jit(solution)/shard_map/ppermute | solution.py:506
  11.9 1.3 %collective-permute-start.3 = (bf16[128,128]{1,0:T(8,128)(2,1)S(1)}, bf16[128,128]{1,0:T(8,128)(2,1)S(1)}, u32[]{:S(2)}, u32[]{:S(2)}) collective-permute-start(bf16[128,128]{1,0:T(8,128)(2,1)S(1)} %pad_maximum_fusion.rest_0_), channel_id=1, source_target_pairs={{0,1},{1,0},{2,3},{3,2},{4,5},{5,4},{6,7},{7,6},{8,9},{9,8},{10,11... | collective-permute-start | bytes 98312 | tf_op jit(solution)/shard_map/ppermute | solution.py:502
  16.9 9.4 %all-to-all-start = ((bf16[8,40,128]{2,1,0:T(8,128)(2,1)}), bf16[8,40,128]{2,1,0:T(8,128)(2,1)S(1)}, u32[]{:S(2)}, u32[]{:S(2)}) async-start(bf16[8,40,128]{2,1,0:T(8,128)(2,1)} %bitcast.7), calls=%async_computation | async-start | bytes 163840 | tf_op jit(solution)/shard_map/all_to_all | solution.py:537
  20.3 6.1 %copy-start = (bf16[512,2048]{1,0:T(8,128)(2,1)S(1)}, bf16[512,2048]{1,0:T(8,128)(2,1)}, u32[]{:S(2)}) copy-start(bf16[512,2048]{1,0:T(8,128)(2,1)} %weight_ref.1) | copy-start | bytes 6291460
  27.7 6.6 %collective-permute-start.4 = (bf16[8,512]{1,0:T(8,128)(2,1)S(1)}, bf16[8,512]{1,0:T(8,128)(2,1)S(1)}, u32[]{:S(2)}, u32[]{:S(2)}) collective-permute-start(bf16[8,512]{1,0:T(8,128)(2,1)S(1)} %get-tuple-element.73), channel_id=1, source_target_pairs={{0,24},{8,16},{16,8},{24,0},{1,25},{9,17},{17,9},{25,1},{2,26},{10... | collective-permute-start | bytes 24584 | tf_op jit(solution)/shard_map/ppermute | solution.py:502
  30.1 4.1 %collective-permute-start.5 = (bf16[8,512]{1,0:T(8,128)(2,1)S(1)}, bf16[8,512]{1,0:T(8,128)(2,1)S(1)}, u32[]{:S(2)}, u32[]{:S(2)}) collective-permute-start(bf16[8,512]{1,0:T(8,128)(2,1)S(1)} %get-tuple-element.74), channel_id=1, source_target_pairs={{0,16},{8,24},{16,0},{24,8},{1,17},{9,25},{17,1},{25,9},{2,18},{10... | collective-permute-start | bytes 24584 | tf_op jit(solution)/shard_map/ppermute | solution.py:502
  30.6 3.7 %collective-permute-start.6 = (bf16[8,512]{1,0:T(8,128)(2,1)S(1)}, bf16[8,512]{1,0:T(8,128)(2,1)S(1)}, u32[]{:S(2)}, u32[]{:S(2)}) collective-permute-start(bf16[8,512]{1,0:T(8,128)(2,1)S(1)} %get-tuple-element.75), channel_id=1, source_target_pairs={{0,8},{8,0},{16,24},{24,16},{1,9},{9,1},{17,25},{25,17},{2,10},{10... | collective-permute-start | bytes 24584 | tf_op jit(solution)/shard_map/ppermute | solution.py:502

commit v5 on v4

--- a/solution.py
+++ b/solution.py
@@ -87,7 +87,7 @@
             in_sem.at[half, n],
         )
         for half, held in enumerate((keys, values))
-        for n in range(chunks)
+        for n in range(held.shape[0] // chunk)
     ]
     for copy in loads:
         copy.start()
@@ -198,30 +198,36 @@
     )
 
 
-def fold_kernel(keys, share_ref, folded_ref, _):
-    pages_dev, kv_local = keys.shape[:2]
-    for page in range(pages_dev):
-        result = dot(share_rows(page, share_ref), side_by_side(keys, page))
-        folded = rounded_fold(result[:8])
-        for g in range(kv_local):
-            folded_ref[g, page : page + 1, :] = folded[:, g * 128 : (g + 1) * 128]
-
-
-def fold_keys(keys, share):
-    pages_dev, kv_local, _, head_size = keys.shape
+def fold_page(page, held, share_ref, folded_ref):
+    result = dot(share_rows(page, share_ref), side_by_side(held, page))
+    folded = rounded_fold(result[:8])
+    for g in range(held.shape[1]):
+        folded_ref[g, page : page + 1, :] = folded[:, g * 128 : (g + 1) * 128]
+
+
+def fold_kernel(keys, values, share_ref, fold_key_ref, fold_value_ref, *_):
+    for held, folded_ref in ((keys, fold_key_ref), (values, fold_value_ref)):
+        for page in range(held.shape[0]):
+            fold_page(page, held, share_ref, folded_ref)
+
+
+def fold(keys, values, share):
+    kv_local, head_size = keys.shape[1], keys.shape[3]
     vmem = pl.BlockSpec(memory_space=pltpu.VMEM)
     return pl.pallas_call(
         fold_kernel,
-        in_specs=[vmem] * 2,
-        out_specs=[vmem] * 2,
+        in_specs=[vmem] * 3,
+        out_specs=[vmem] * 4,
         out_shape=[
-            jax.ShapeDtypeStruct((kv_local, pages_dev, head_size), f32),
+            jax.ShapeDtypeStruct((kv_local, keys.shape[0], head_size), f32),
+            jax.ShapeDtypeStruct((kv_local, values.shape[0], head_size), f32),
             pltpu.VMEM(keys.shape, bf16),
+            pltpu.VMEM(values.shape, bf16),
         ],
-        input_output_aliases={0: 1},
+        input_output_aliases={0: 2, 1: 3},
         compiler_params=pltpu.CompilerParams(vmem_limit_bytes=24 << 20),
-        name="fold_keys",
-    )(keys, share)
+        name="fold",
+    )(keys, values, share)
 
 
 def pack_kernel(spans, chunk, pages_hbm, position_ref, count_ref, *rest):
@@ -284,12 +290,12 @@
 
 
 def attend_kernel(
-    heads, req_dev, score_scale, peers, keys, kept_ref, fold_mass_ref, share_ref,
-    fold_key_ref, target_ref, slot_ref, values, *rest,
+    heads, req_dev, score_scale, peers, keys, kept_ref, fold_mass_ref,
+    fold_key_ref, target_ref, slot_ref, values, fold_value_ref, *rest,
 ):
     pages_dev, slots = kept_ref.shape
     query_refs = rest[:2]
-    out_ref, fold_value_ref, scores, parts = rest[2:]
+    out_ref, scores, parts = rest[2:]
     kv_local = keys.shape[1]
     groups = heads // kv_local
     rows = pages_dev * heads
@@ -349,16 +355,8 @@
 
     for first in range(0, pages_dev, tile_pages):
         at = first * heads
-        results = []
-        for i in range(tile_pages):
-            left = jnp.concatenate(
-                [weight_b[at : at + tile], share_rows(first + i, share_ref)], axis=0
-            )
-            result = dot(left, side_by_side(values, first + i))
-            results.append(result)
-            folded = rounded_fold(result[tile : tile + 8])
-            for g in range(kv_local):
-                fold_value_ref[g, first + i : first + i + 1, :] = folded[:, g * 128 : (g + 1) * 128]
+        left = weight_b[at : at + tile]
+        results = [dot(left, side_by_side(values, first + i)) for i in range(tile_pages)]
         parts[at : at + tile, :] = choose(results)
 
     part = parts[...] + fold_weight.astype(bf16).astype(f32) * spread_fold(fold_value_ref)
@@ -391,20 +389,17 @@
 
 
 def attend(
-    near, far, keys, kept, fold_mass, share, fold_key, target, slot, values, score_scale, heads,
-    req_dev, peers
+    near, far, keys, kept, fold_mass, fold_key, target, slot, values, fold_value, score_scale,
+    heads, req_dev, peers
 ):
-    pages_dev, kv_local, slots, head_size = values.shape
+    pages_dev, _, slots, head_size = keys.shape
     rows = pages_dev * heads
     vmem = pl.BlockSpec(memory_space=pltpu.VMEM)
     return pl.pallas_call(
         functools.partial(attend_kernel, heads, req_dev, score_scale, peers),
         in_specs=[vmem] * 10,
-        out_specs=[vmem] * 2,
-        out_shape=[
-            jax.ShapeDtypeStruct(message(rows, peers), bf16),
-            jax.ShapeDtypeStruct((kv_local, pages_dev, head_size), f32),
-        ],
+        out_specs=vmem,
+        out_shape=jax.ShapeDtypeStruct(message(rows, peers), bf16),
         scratch_shapes=[
             pltpu.VMEM((rows, slots), f32),
             pltpu.VMEM((rows, head_size), f32),
@@ -412,7 +407,7 @@
         compiler_params=pltpu.CompilerParams(vmem_limit_bytes=24 << 20),
         name="attend",
     )(
-        keys, kept, fold_mass, share, fold_key, target, slot, values, *near, *far,
+        keys, kept, fold_mass, fold_key, target, slot, values, fold_value, *near, *far,
     )
 
 
@@ -528,17 +523,17 @@
     own, *others = lax.optimization_barrier((own, *others))
     near = [jnp.concatenate([flat(x) for x in [own] + others])]
     far = [exchange(near[0], "seq", seq_count, 1)]
-    fold_key, keys = fold_keys(keys, share)
+    fold_key, fold_value, keys, values = fold(keys, values, share)
     fold_key, *far = lax.optimization_barrier((fold_key, *far))
-    send, fold_value = attend(
-        near, far, keys, kept, fold_mass, share, fold_key, target, slot, values, score_scale,
+    send = attend(
+        near, far, keys, kept, fold_mass, fold_key, target, slot, values, fold_value, score_scale,
         heads, req_dev, seq_count,
     )
     got = lax.all_to_all(
         send.reshape(seq_count, -1, send.shape[1]), "seq", split_axis=0, concat_axis=0, tiled=True
     ).reshape(send.shape)
     pages_dev = page_cache.shape[0]
-    fold_key, fold_value = lax.optimization_barrier((fold_key, fold_value))
+    fold_key, send = lax.optimization_barrier((fold_key, send))
     middle = pages_dev // 2
     packed = pack(
         "pack_first", [(0, 0, pages_dev), (1, 0, middle)], page_cache, position, count, fold_key,
@@ -554,7 +549,7 @@
         "pack_rest", [(1, middle, pages_dev)], page_cache, position, count, fold_key, fold_value, packed
     )
     total = shares[0].astype(f32)
-    for k in range(kv_count - 1, 0, -1):
+    for k in range(1, kv_count):
         total = total + exchange(shares[k], "kv", kv_count, k).astype(f32)
     return packed, mass, attended, total.astype(bf16)
 

time: 35.1 us -> 35 us (level)
  waiting for transfers between devices: 0.91 us -> 0.42 us
    pallas_call x1, Pallas kernels: 0.69 us -> 1.25 us  [fold(): pl.pallas_call(fold_kernel, in_specs=[vmem] * 3, out_specs=[vmem] * 4, ou...]
    ppermute x4, waiting for transfers between devices: 0.53 us -> 0.04 us  [exchange(): return lax.ppermute(x, axis, [(i, i ^ mask) for i in range(count)])]
  transfers between devices with their start and end apart: 8 -> 8, of which waited for: 2 -> 1; matrix products, arithmetic and copies ran while one was open for 0% -> 0% of each run, Pallas kernels for 39% -> 41%
where the time goes in v5:
time: 35 us; the launch traced here: 34.7 us
  Pallas kernels  19 us (54%)
  starting transfers between devices  13.9 us (40%)
  between operations  0.75 us (2%)
  other arithmetic  0.61 us (2%)
  waiting for transfers between devices  0.42 us (1%)
    pallas_call x2, Pallas kernels, pack(): pl.pallas_call(functools.partial(pack_kernel, spans, chunk), in_specs=[hb...  8.71 us
    ppermute x3, starting transfers between devices, shift(): lax.ppermute(x, axis, [(i, (i + step) % count) for i in range(count)])  7.01 us
    pallas_call x1, Pallas kernels, prepare(): pl.pallas_call(functools.partial(prepare_kernel, heads, req_dev, chunk),...  4.19 us
    ppermute x4, starting transfers between devices, exchange(): return lax.ppermute(x, axis, [(i, i ^ mask) for i in range(count)])  3.56 us
    pallas_call x1, Pallas kernels, attend(): pl.pallas_call(functools.partial(attend_kernel, heads, req_dev, score_sca...  3.49 us
    all_to_all x1, starting transfers between devices, per_device(): lax.all_to_all(send.reshape(seq_count, -1, send.shape[1]), 'seq', split_a...  3.36 us
    pallas_call x1, Pallas kernels, combine(): pl.pallas_call(functools.partial(combine_kernel, heads, kv_local, req_dev...  1.38 us
    pallas_call x1, Pallas kernels, fold(): pl.pallas_call(fold_kernel, in_specs=[vmem] * 3, out_specs=[vmem] * 4, ou...  1.25 us
  transfers between devices with their start and end apart: 8, of which 1 were waited for; matrix products, arithmetic and copies ran while one was open for 0% of the time, Pallas kernels for 41%

profile of v5, /device:TPU:0, one launch (start us, length us, event | category | flops | bytes accessed | tf_op | source)
XLA Modules:
  0.0 34.7 jit_solution(1501127780631977237)
XLA Ops:
  0.6 3.1 %collective-permute-start = (bf16[8,4,128]{2,1,0:T(4,128)(2,1)}, bf16[8,4,128]{2,1,0:T(4,128)(2,1)S(1)}, u32[]{:S(2)}, u32[]{:S(2)}) collective-permute-start(bf16[8,4,128]{2,1,0:T(4,128)(2,1)} %query_hbm.1), channel_id=1, source_target_pairs={{0,2},{1,3},{2,4},{3,5},{4,6},{5,7},{6,0},{7,1},{8,10},{9,11},{10,... | collective-permute-start | bytes 24584 | tf_op jit(solution)/shard_map/ppermute | solution.py:501
  3.7 2.6 %collective-permute-start.1 = (bf16[8,4,128]{2,1,0:T(4,128)(2,1)}, bf16[8,4,128]{2,1,0:T(4,128)(2,1)S(1)}, u32[]{:S(2)}, u32[]{:S(2)}) collective-permute-start(bf16[8,4,128]{2,1,0:T(4,128)(2,1)} %query_hbm.1), channel_id=1, source_target_pairs={{0,4},{1,5},{2,6},{3,7},{4,0},{5,1},{6,2},{7,3},{8,12},{9,13},{10,... | collective-permute-start | bytes 24584 | tf_op jit(solution)/shard_map/ppermute | solution.py:501
  6.3 1.3 %collective-permute-start.2 = (bf16[8,4,128]{2,1,0:T(4,128)(2,1)}, bf16[8,4,128]{2,1,0:T(4,128)(2,1)S(1)}, u32[]{:S(2)}, u32[]{:S(2)}) collective-permute-start(bf16[8,4,128]{2,1,0:T(4,128)(2,1)} %query_hbm.1), channel_id=1, source_target_pairs={{0,6},{1,7},{2,0},{3,1},{4,2},{5,3},{6,4},{7,5},{8,14},{9,15},{10,... | collective-permute-start | bytes 24584 | tf_op jit(solution)/shard_map/ppermute | solution.py:501
  7.6 4.2 %prepare.1 = (bf16[64,2,128,128]{3,2,1,0:T(8,128)(2,1)S(1)}, bf16[64,2,128,128]{3,2,1,0:T(8,128)(2,1)S(1)}, bf16[8,4,128]{2,1,0:T(4,128)(2,1)S(1)}, bf16[8,2,2,1...) custom-call(s32[1]{0:T(128)} %bitcast.rank_ref, ...), custom_call_target="tpu_custom_call" | custom-call | tf_op jit(solution)/shard_map/prepare/pallas_call | solution.py:162
  11.8 0.0 collective-permute-done
  11.9 0.0 collective-permute-done.1
  11.9 0.0 collective-permute-done.2
  11.9 0.1 collective-permute-start.3
  12.0 1.3 %fold.1 = (f32[2,64,128]{2,1,0:T(8,128)S(1)}, f32[2,64,128]{2,1,0:T(8,128)S(1)}, bf16[64,2,128,128]{3,2,1,0:T(8,128)(2,1)S(1)}, bf16[64,2,128,128]{3,2,1,0:T(8,128)(2,1)S(1)}) custom-call(bf16[64,2,128,128]{3,2,1,0:T(8,128)(2,1)S(1)} %get-tuple-element.41.keys, ...), custom_call_target="tpu_custom_call", output_to_operand_aliasing={{2}: (0, {}), {3}: (1, {})} | custom-call | tf_op jit(solution)/shard_map/fold/pallas_call | solution.py:217
  13.2 0.0 collective-permute-done.3.rest_1_
  13.2 3.5 %attend.1 = bf16[320,128]{1,0:T(8,128)(2,1)} custom-call(bf16[64,2,128,128]{3,2,1,0:T(8,128)(2,1)S(1)} %get-tuple-element.51.keys, f32[64,128]{1,0:T(8,128)S(1)} %get-tuple-element.52.kept_ref, f32[64,128]{1,0:T(8,128)S(1)} %get-tuple-element.53.fold_mass_ref, f32[2,64,128]{2,1,0:T(8,128)S(1)} %get-tuple-element.59.fold_key_ref.rest_0_, ...), custom_call_target="tpu_custom_call" | custom-call | tf_op jit(solution)/shard_map/attend/pallas_call | solution.py:398
  16.7 3.4 %all-to-all-start = ((bf16[8,40,128]{2,1,0:T(8,128)(2,1)}), bf16[8,40,128]{2,1,0:T(8,128)(2,1)S(1)}, u32[]{:S(2)}, u32[]{:S(2)}) async-start(bf16[8,40,128]{2,1,0:T(8,128)(2,1)} %bitcast.7), calls=%async_computation | async-start | bytes 163840 | tf_op jit(solution)/shard_map/all_to_all | solution.py:532
  20.1 0.0 copy-start
  20.1 5.7 %pack_first.1.rest_2_ = bf16[64,2,2,128,128]{4,3,2,1,0:T(8,128)(2,1)} custom-call(bf16[64,2,2,128,128]{4,3,2,1,0:T(8,128)(2,1)} %pages_hbm.5, f32[64,128]{1,0:T(8,128)S(1)} %get-tuple-element.39.position_ref, f32[64,128]{1,0:T(8,128)S(1)} %get-tuple-element.40.count_ref, f32[2,64,128]{2,1,0:T(8,128)S(1)} %get-tuple-element.59.fold_key_ref.rest_0_, ...), custom_call_target="tpu_custom_call" | custom-call | tf_op jit(solution)/shard_map/pack_first/pallas_call | solution.py:275
  25.8 0.4 %all-to-all-done = bf16[8,40,128]{2,1,0:T(8,128)(2,1)S(1)} async-done(((bf16[8,40,128]{2,1,0:T(8,128)(2,1)}), bf16[8,40,128]{2,1,0:T(8,128)(2,1)S(1)}, u32[]{:S(2)}, u32[]{:S(2)}) %all-to-all-start) | async-done | bytes 81952 | tf_op jit(solution)/shard_map/all_to_all | solution.py:532
  26.2 1.4 %combine.1 = (bf16[8,512]{1,0:T(8,128)(2,1)}, bf16[8,512]{1,0:T(8,128)(2,1)S(1)}, bf16[8,512]{1,0:T(8,128)(2,1)S(1)}, bf16[8,512]{1,0:T(8,128)(2,1)S(1)}, bf16[8,512]{1,0:T(8,128)(2,1)S(1)}) custom-call(s32[1]{0:T(128)} %bitcast.9.rank_ref, bf16[32,128]{1,0:T(8,128)(2,1)S(1)} %bitcast.13, bf16[32,128]{1,0:T(8,128)(2,1)S(1)} %bitcast.14, ...), custom_call_target="tpu_custom_call" | custom-call | flops 16777216 | bytes 2097152 | tf_op jit(solution)/shard_map/combine/pallas_call | solution.py:482
  27.5 2.4 %collective-permute-start.6 = (bf16[8,512]{1,0:T(8,128)(2,1)S(1)}, bf16[8,512]{1,0:T(8,128)(2,1)S(1)}, u32[]{:S(2)}, u32[]{:S(2)}) collective-permute-start(bf16[8,512]{1,0:T(8,128)(2,1)S(1)} %get-tuple-element.73), channel_id=1, source_target_pairs={{0,24},{8,16},{16,8},{24,0},{1,25},{9,17},{17,9},{25,1},{2,26},{10... | collective-permute-start | bytes 24584 | tf_op jit(solution)/shard_map/ppermute | solution.py:497
  30.0 0.5 %collective-permute-start.5 = (bf16[8,512]{1,0:T(8,128)(2,1)S(1)}, bf16[8,512]{1,0:T(8,128)(2,1)S(1)}, u32[]{:S(2)}, u32[]{:S(2)}) collective-permute-start(bf16[8,512]{1,0:T(8,128)(2,1)S(1)} %get-tuple-element.72), channel_id=1, source_target_pairs={{0,16},{8,24},{16,0},{24,8},{1,17},{9,25},{17,1},{25,9},{2,18},{10... | collective-permute-start | bytes 24584 | tf_op jit(solution)/shard_map/ppermute | solution.py:497
  30.5 0.5 %collective-permute-start.4 = (bf16[8,512]{1,0:T(8,128)(2,1)S(1)}, bf16[8,512]{1,0:T(8,128)(2,1)S(1)}, u32[]{:S(2)}, u32[]{:S(2)}) collective-permute-start(bf16[8,512]{1,0:T(8,128)(2,1)S(1)} %get-tuple-element.71), channel_id=1, source_target_pairs={{0,8},{8,0},{16,24},{24,16},{1,9},{9,1},{17,25},{25,17},{2,10},{10... | collective-permute-start | bytes 24584 | tf_op jit(solution)/shard_map/ppermute | solution.py:497
  31.0 3.1 %pack_rest.1 = bf16[64,2,2,128,128]{4,3,2,1,0:T(8,128)(2,1)} custom-call(bf16[64,2,2,128,128]{4,3,2,1,0:T(8,128)(2,1)} %pages_hbm.5, f32[64,128]{1,0:T(8,128)S(1)} %get-tuple-element.39.position_ref, f32[64,128]{1,0:T(8,128)S(1)} %get-tuple-element.40.count_ref, ...), custom_call_target="tpu_custom_call", output_to_operand_aliasing={{}: (5, {})} | custom-call | tf_op jit(solution)/shard_map/pack_rest/pallas_call | solution.py:275
  34.1 0.0 collective-permute-done.6
  34.1 0.0 collective-permute-done.5
  34.1 0.0 collective-permute-done.4
  34.1 0.6 %add_convert_fusion = bf16[8,512]{1,0:T(8,128)(2,1)} fusion(bf16[8,512]{1,0:T(8,128)(2,1)S(1)} %collective-permute-done.6, bf16[8,512]{1,0:T(8,128)(2,1)S(1)} %collective-permute-done.5, bf16[8,512]{1,0:T(8,128)(2,1)S(1)} %collective-permute-done.4, bf16[8,512]{1,0:T(8,128)(2,1)S(1)} %get-tuple-element.70), kind=kLoop, calls=%fused_computation.1 | loop fusion | flops 32768 | bytes 40960 | tf_op jit(solution)/shard_map/convert_element_type | solution.py:554
  (2 shorter events, 0.0 us)
Async XLA Ops:
  0.6 11.2 %collective-permute-start = (bf16[8,4,128]{2,1,0:T(4,128)(2,1)}, bf16[8,4,128]{2,1,0:T(4,128)(2,1)S(1)}, u32[]{:S(2)}, u32[]{:S(2)}) collective-permute-start(bf16[8,4,128]{2,1,0:T(4,128)(2,1)} %query_hbm.1), channel_id=1, source_target_pairs={{0,2},{1,3},{2,4},{3,5},{4,6},{5,7},{6,0},{7,1},{8,10},{9,11},{10,... | collective-permute-start | bytes 24584 | tf_op jit(solution)/shard_map/ppermute | solution.py:501
  3.7 8.2 %collective-permute-start.1 = (bf16[8,4,128]{2,1,0:T(4,128)(2,1)}, bf16[8,4,128]{2,1,0:T(4,128)(2,1)S(1)}, u32[]{:S(2)}, u32[]{:S(2)}) collective-permute-start(bf16[8,4,128]{2,1,0:T(4,128)(2,1)} %query_hbm.1), channel_id=1, source_target_pairs={{0,4},{1,5},{2,6},{3,7},{4,0},{5,1},{6,2},{7,3},{8,12},{9,13},{10,... | collective-permute-start | bytes 24584 | tf_op jit(solution)/shard_map/ppermute | solution.py:501
  6.3 5.6 %collective-permute-start.2 = (bf16[8,4,128]{2,1,0:T(4,128)(2,1)}, bf16[8,4,128]{2,1,0:T(4,128)(2,1)S(1)}, u32[]{:S(2)}, u32[]{:S(2)}) collective-permute-start(bf16[8,4,128]{2,1,0:T(4,128)(2,1)} %query_hbm.1), channel_id=1, source_target_pairs={{0,6},{1,7},{2,0},{3,1},{4,2},{5,3},{6,4},{7,5},{8,14},{9,15},{10,... | collective-permute-start | bytes 24584 | tf_op jit(solution)/shard_map/ppermute | solution.py:501
  11.9 1.3 %collective-permute-start.3 = (bf16[128,128]{1,0:T(8,128)(2,1)S(1)}, bf16[128,128]{1,0:T(8,128)(2,1)S(1)}, u32[]{:S(2)}, u32[]{:S(2)}) collective-permute-start(bf16[128,128]{1,0:T(8,128)(2,1)S(1)} %pad_maximum_fusion.rest_0_), channel_id=1, source_target_pairs={{0,1},{1,0},{2,3},{3,2},{4,5},{5,4},{6,7},{7,6},{8,9},{9,8},{10,11... | collective-permute-start | bytes 98312 | tf_op jit(solution)/shard_map/ppermute | solution.py:497
  16.7 9.4 %all-to-all-start = ((bf16[8,40,128]{2,1,0:T(8,128)(2,1)}), bf16[8,40,128]{2,1,0:T(8,128)(2,1)S(1)}, u32[]{:S(2)}, u32[]{:S(2)}) async-start(bf16[8,40,128]{2,1,0:T(8,128)(2,1)} %bitcast.7), calls=%async_computation | async-start | bytes 163840 | tf_op jit(solution)/shard_map/all_to_all | solution.py:532
  20.1 6.1 %copy-start = (bf16[512,2048]{1,0:T(8,128)(2,1)S(1)}, bf16[512,2048]{1,0:T(8,128)(2,1)}, u32[]{:S(2)}) copy-start(bf16[512,2048]{1,0:T(8,128)(2,1)} %weight_ref.1) | copy-start | bytes 6291460
  27.5 6.6 %collective-permute-start.6 = (bf16[8,512]{1,0:T(8,128)(2,1)S(1)}, bf16[8,512]{1,0:T(8,128)(2,1)S(1)}, u32[]{:S(2)}, u32[]{:S(2)}) collective-permute-start(bf16[8,512]{1,0:T(8,128)(2,1)S(1)} %get-tuple-element.73), channel_id=1, source_target_pairs={{0,24},{8,16},{16,8},{24,0},{1,25},{9,17},{17,9},{25,1},{2,26},{10... | collective-permute-start | bytes 24584 | tf_op jit(solution)/shard_map/ppermute | solution.py:497
  30.0 4.1 %collective-permute-start.5 = (bf16[8,512]{1,0:T(8,128)(2,1)S(1)}, bf16[8,512]{1,0:T(8,128)(2,1)S(1)}, u32[]{:S(2)}, u32[]{:S(2)}) collective-permute-start(bf16[8,512]{1,0:T(8,128)(2,1)S(1)} %get-tuple-element.72), channel_id=1, source_target_pairs={{0,16},{8,24},{16,0},{24,8},{1,17},{9,25},{17,1},{25,9},{2,18},{10... | collective-permute-start | bytes 24584 | tf_op jit(solution)/shard_map/ppermute | solution.py:497
  30.5 3.7 %collective-permute-start.4 = (bf16[8,512]{1,0:T(8,128)(2,1)S(1)}, bf16[8,512]{1,0:T(8,128)(2,1)S(1)}, u32[]{:S(2)}, u32[]{:S(2)}) collective-permute-start(bf16[8,512]{1,0:T(8,128)(2,1)S(1)} %get-tuple-element.71), channel_id=1, source_target_pairs={{0,8},{8,0},{16,24},{24,16},{1,9},{9,1},{17,25},{25,17},{2,10},{10... | collective-permute-start | bytes 24584 | tf_op jit(solution)/shard_map/ppermute | solution.py:497

commit v6 on v5

--- a/solution.py
+++ b/solution.py
@@ -457,8 +457,8 @@
     )
     best_col = jnp.sum(jnp.where(diagonal, best, 0.0), axis=1, keepdims=True)
     factor = jnp.where(match, jnp.exp(top - best), 0.0)
-    high, middle, low = pieces(factor)
-    sums = dot(high, got, (0, 0)) + dot(middle, got, (0, 0)) + dot(low, got, (0, 0))
+    high, middle, _ = pieces(factor)
+    sums = dot(high, got, (0, 0)) + dot(middle, got, (0, 0))
     own_factor = jnp.exp(own - best_col)
     denominator = sums[:, 131:132] + sums[:, 132:133] + sums[:, 133:134] + own_factor
     numerator = sums[:, :128] + own_factor * rows_of(fresh_ref, fresh_row + kv_local)

time: 35 us -> 34.9 us (level)
  no operation moved by 1% of the time
where the time goes in v6:
time: 34.9 us; the launch traced here: 34.7 us
  Pallas kernels  19 us (54%)
  starting transfers between devices  13.9 us (40%)
  between operations  0.75 us (2%)
  other arithmetic  0.61 us (2%)
  waiting for transfers between devices  0.42 us (1%)
    pallas_call x2, Pallas kernels, pack(): pl.pallas_call(functools.partial(pack_kernel, spans, chunk), in_specs=[hb...  8.71 us
    ppermute x3, starting transfers between devices, shift(): lax.ppermute(x, axis, [(i, (i + step) % count) for i in range(count)])  7.01 us
    pallas_call x1, Pallas kernels, prepare(): pl.pallas_call(functools.partial(prepare_kernel, heads, req_dev, chunk),...  4.19 us
    ppermute x4, starting transfers between devices, exchange(): return lax.ppermute(x, axis, [(i, i ^ mask) for i in range(count)])  3.56 us
    pallas_call x1, Pallas kernels, attend(): pl.pallas_call(functools.partial(attend_kernel, heads, req_dev, score_sca...  3.49 us
    all_to_all x1, starting transfers between devices, per_device(): lax.all_to_all(send.reshape(seq_count, -1, send.shape[1]), 'seq', split_a...  3.36 us
    pallas_call x1, Pallas kernels, combine(): pl.pallas_call(functools.partial(combine_kernel, heads, kv_local, req_dev...  1.34 us
    pallas_call x1, Pallas kernels, fold(): pl.pallas_call(fold_kernel, in_specs=[vmem] * 3, out_specs=[vmem] * 4, ou...  1.25 us
  transfers between devices with their start and end apart: 8, of which 1 were waited for; matrix products, arithmetic and copies ran while one was open for 0% of the time, Pallas kernels for 41%

profile of v6, /device:TPU:0, one launch (start us, length us, event | category | flops | bytes accessed | tf_op | source)
XLA Modules:
  0.0 34.7 jit_solution(10059746040971838045)
XLA Ops:
  0.6 3.1 %collective-permute-start = (bf16[8,4,128]{2,1,0:T(4,128)(2,1)}, bf16[8,4,128]{2,1,0:T(4,128)(2,1)S(1)}, u32[]{:S(2)}, u32[]{:S(2)}) collective-permute-start(bf16[8,4,128]{2,1,0:T(4,128)(2,1)} %query_hbm.1), channel_id=1, source_target_pairs={{0,2},{1,3},{2,4},{3,5},{4,6},{5,7},{6,0},{7,1},{8,10},{9,11},{10,... | collective-permute-start | bytes 24584 | tf_op jit(solution)/shard_map/ppermute | solution.py:501
  3.7 2.6 %collective-permute-start.1 = (bf16[8,4,128]{2,1,0:T(4,128)(2,1)}, bf16[8,4,128]{2,1,0:T(4,128)(2,1)S(1)}, u32[]{:S(2)}, u32[]{:S(2)}) collective-permute-start(bf16[8,4,128]{2,1,0:T(4,128)(2,1)} %query_hbm.1), channel_id=1, source_target_pairs={{0,4},{1,5},{2,6},{3,7},{4,0},{5,1},{6,2},{7,3},{8,12},{9,13},{10,... | collective-permute-start | bytes 24584 | tf_op jit(solution)/shard_map/ppermute | solution.py:501
  6.3 1.3 %collective-permute-start.2 = (bf16[8,4,128]{2,1,0:T(4,128)(2,1)}, bf16[8,4,128]{2,1,0:T(4,128)(2,1)S(1)}, u32[]{:S(2)}, u32[]{:S(2)}) collective-permute-start(bf16[8,4,128]{2,1,0:T(4,128)(2,1)} %query_hbm.1), channel_id=1, source_target_pairs={{0,6},{1,7},{2,0},{3,1},{4,2},{5,3},{6,4},{7,5},{8,14},{9,15},{10,... | collective-permute-start | bytes 24584 | tf_op jit(solution)/shard_map/ppermute | solution.py:501
  7.6 4.2 %prepare.1 = (bf16[64,2,128,128]{3,2,1,0:T(8,128)(2,1)S(1)}, bf16[64,2,128,128]{3,2,1,0:T(8,128)(2,1)S(1)}, bf16[8,4,128]{2,1,0:T(4,128)(2,1)S(1)}, bf16[8,2,2,1...) custom-call(s32[1]{0:T(128)} %bitcast.rank_ref, ...), custom_call_target="tpu_custom_call" | custom-call | tf_op jit(solution)/shard_map/prepare/pallas_call | solution.py:162
  11.8 0.0 collective-permute-done
  11.9 0.0 collective-permute-done.1
  11.9 0.0 collective-permute-done.2
  11.9 0.1 collective-permute-start.3
  12.0 1.3 %fold.1 = (f32[2,64,128]{2,1,0:T(8,128)S(1)}, f32[2,64,128]{2,1,0:T(8,128)S(1)}, bf16[64,2,128,128]{3,2,1,0:T(8,128)(2,1)S(1)}, bf16[64,2,128,128]{3,2,1,0:T(8,128)(2,1)S(1)}) custom-call(bf16[64,2,128,128]{3,2,1,0:T(8,128)(2,1)S(1)} %get-tuple-element.41.keys, ...), custom_call_target="tpu_custom_call", output_to_operand_aliasing={{2}: (0, {}), {3}: (1, {})} | custom-call | tf_op jit(solution)/shard_map/fold/pallas_call | solution.py:217
  13.2 0.0 collective-permute-done.3.rest_1_
  13.2 3.5 %attend.1 = bf16[320,128]{1,0:T(8,128)(2,1)} custom-call(bf16[64,2,128,128]{3,2,1,0:T(8,128)(2,1)S(1)} %get-tuple-element.51.keys, f32[64,128]{1,0:T(8,128)S(1)} %get-tuple-element.52.kept_ref, f32[64,128]{1,0:T(8,128)S(1)} %get-tuple-element.53.fold_mass_ref, f32[2,64,128]{2,1,0:T(8,128)S(1)} %get-tuple-element.59.fold_key_ref.rest_0_, ...), custom_call_target="tpu_custom_call" | custom-call | tf_op jit(solution)/shard_map/attend/pallas_call | solution.py:398
  16.7 3.4 %all-to-all-start = ((bf16[8,40,128]{2,1,0:T(8,128)(2,1)}), bf16[8,40,128]{2,1,0:T(8,128)(2,1)S(1)}, u32[]{:S(2)}, u32[]{:S(2)}) async-start(bf16[8,40,128]{2,1,0:T(8,128)(2,1)} %bitcast.7), calls=%async_computation | async-start | bytes 163840 | tf_op jit(solution)/shard_map/all_to_all | solution.py:532
  20.1 0.0 copy-start
  20.1 5.7 %pack_first.1.rest_2_ = bf16[64,2,2,128,128]{4,3,2,1,0:T(8,128)(2,1)} custom-call(bf16[64,2,2,128,128]{4,3,2,1,0:T(8,128)(2,1)} %pages_hbm.5, f32[64,128]{1,0:T(8,128)S(1)} %get-tuple-element.39.position_ref, f32[64,128]{1,0:T(8,128)S(1)} %get-tuple-element.40.count_ref, f32[2,64,128]{2,1,0:T(8,128)S(1)} %get-tuple-element.59.fold_key_ref.rest_0_, ...), custom_call_target="tpu_custom_call" | custom-call | tf_op jit(solution)/shard_map/pack_first/pallas_call | solution.py:275
  25.8 0.4 %all-to-all-done = bf16[8,40,128]{2,1,0:T(8,128)(2,1)S(1)} async-done(((bf16[8,40,128]{2,1,0:T(8,128)(2,1)}), bf16[8,40,128]{2,1,0:T(8,128)(2,1)S(1)}, u32[]{:S(2)}, u32[]{:S(2)}) %all-to-all-start) | async-done | bytes 81952 | tf_op jit(solution)/shard_map/all_to_all | solution.py:532
  26.2 1.3 %combine.1 = (bf16[8,512]{1,0:T(8,128)(2,1)}, bf16[8,512]{1,0:T(8,128)(2,1)S(1)}, bf16[8,512]{1,0:T(8,128)(2,1)S(1)}, bf16[8,512]{1,0:T(8,128)(2,1)S(1)}, bf16[8,512]{1,0:T(8,128)(2,1)S(1)}) custom-call(s32[1]{0:T(128)} %bitcast.9.rank_ref, bf16[32,128]{1,0:T(8,128)(2,1)S(1)} %bitcast.13, bf16[32,128]{1,0:T(8,128)(2,1)S(1)} %bitcast.14, ...), custom_call_target="tpu_custom_call" | custom-call | flops 16777216 | bytes 2097152 | tf_op jit(solution)/shard_map/combine/pallas_call | solution.py:482
  27.5 2.4 %collective-permute-start.6 = (bf16[8,512]{1,0:T(8,128)(2,1)S(1)}, bf16[8,512]{1,0:T(8,128)(2,1)S(1)}, u32[]{:S(2)}, u32[]{:S(2)}) collective-permute-start(bf16[8,512]{1,0:T(8,128)(2,1)S(1)} %get-tuple-element.73), channel_id=1, source_target_pairs={{0,24},{8,16},{16,8},{24,0},{1,25},{9,17},{17,9},{25,1},{2,26},{10... | collective-permute-start | bytes 24584 | tf_op jit(solution)/shard_map/ppermute | solution.py:497
  29.9 0.5 %collective-permute-start.5 = (bf16[8,512]{1,0:T(8,128)(2,1)S(1)}, bf16[8,512]{1,0:T(8,128)(2,1)S(1)}, u32[]{:S(2)}, u32[]{:S(2)}) collective-permute-start(bf16[8,512]{1,0:T(8,128)(2,1)S(1)} %get-tuple-element.72), channel_id=1, source_target_pairs={{0,16},{8,24},{16,0},{24,8},{1,17},{9,25},{17,1},{25,9},{2,18},{10... | collective-permute-start | bytes 24584 | tf_op jit(solution)/shard_map/ppermute | solution.py:497
  30.4 0.5 %collective-permute-start.4 = (bf16[8,512]{1,0:T(8,128)(2,1)S(1)}, bf16[8,512]{1,0:T(8,128)(2,1)S(1)}, u32[]{:S(2)}, u32[]{:S(2)}) collective-permute-start(bf16[8,512]{1,0:T(8,128)(2,1)S(1)} %get-tuple-element.71), channel_id=1, source_target_pairs={{0,8},{8,0},{16,24},{24,16},{1,9},{9,1},{17,25},{25,17},{2,10},{10... | collective-permute-start | bytes 24584 | tf_op jit(solution)/shard_map/ppermute | solution.py:497
  31.0 3.1 %pack_rest.1 = bf16[64,2,2,128,128]{4,3,2,1,0:T(8,128)(2,1)} custom-call(bf16[64,2,2,128,128]{4,3,2,1,0:T(8,128)(2,1)} %pages_hbm.5, f32[64,128]{1,0:T(8,128)S(1)} %get-tuple-element.39.position_ref, f32[64,128]{1,0:T(8,128)S(1)} %get-tuple-element.40.count_ref, ...), custom_call_target="tpu_custom_call", output_to_operand_aliasing={{}: (5, {})} | custom-call | tf_op jit(solution)/shard_map/pack_rest/pallas_call | solution.py:275
  34.0 0.0 collective-permute-done.6
  34.1 0.0 collective-permute-done.5
  34.1 0.0 collective-permute-done.4
  34.1 0.6 %add_convert_fusion = bf16[8,512]{1,0:T(8,128)(2,1)} fusion(bf16[8,512]{1,0:T(8,128)(2,1)S(1)} %collective-permute-done.6, bf16[8,512]{1,0:T(8,128)(2,1)S(1)} %collective-permute-done.5, bf16[8,512]{1,0:T(8,128)(2,1)S(1)} %collective-permute-done.4, bf16[8,512]{1,0:T(8,128)(2,1)S(1)} %get-tuple-element.70), kind=kLoop, calls=%fused_computation.1 | loop fusion | flops 32768 | bytes 40960 | tf_op jit(solution)/shard_map/convert_element_type | solution.py:554
  (2 shorter events, 0.0 us)
Async XLA Ops:
  0.6 11.2 %collective-permute-start = (bf16[8,4,128]{2,1,0:T(4,128)(2,1)}, bf16[8,4,128]{2,1,0:T(4,128)(2,1)S(1)}, u32[]{:S(2)}, u32[]{:S(2)}) collective-permute-start(bf16[8,4,128]{2,1,0:T(4,128)(2,1)} %query_hbm.1), channel_id=1, source_target_pairs={{0,2},{1,3},{2,4},{3,5},{4,6},{5,7},{6,0},{7,1},{8,10},{9,11},{10,... | collective-permute-start | bytes 24584 | tf_op jit(solution)/shard_map/ppermute | solution.py:501
  3.7 8.2 %collective-permute-start.1 = (bf16[8,4,128]{2,1,0:T(4,128)(2,1)}, bf16[8,4,128]{2,1,0:T(4,128)(2,1)S(1)}, u32[]{:S(2)}, u32[]{:S(2)}) collective-permute-start(bf16[8,4,128]{2,1,0:T(4,128)(2,1)} %query_hbm.1), channel_id=1, source_target_pairs={{0,4},{1,5},{2,6},{3,7},{4,0},{5,1},{6,2},{7,3},{8,12},{9,13},{10,... | collective-permute-start | bytes 24584 | tf_op jit(solution)/shard_map/ppermute | solution.py:501
  6.3 5.6 %collective-permute-start.2 = (bf16[8,4,128]{2,1,0:T(4,128)(2,1)}, bf16[8,4,128]{2,1,0:T(4,128)(2,1)S(1)}, u32[]{:S(2)}, u32[]{:S(2)}) collective-permute-start(bf16[8,4,128]{2,1,0:T(4,128)(2,1)} %query_hbm.1), channel_id=1, source_target_pairs={{0,6},{1,7},{2,0},{3,1},{4,2},{5,3},{6,4},{7,5},{8,14},{9,15},{10,... | collective-permute-start | bytes 24584 | tf_op jit(solution)/shard_map/ppermute | solution.py:501
  11.9 1.3 %collective-permute-start.3 = (bf16[128,128]{1,0:T(8,128)(2,1)S(1)}, bf16[128,128]{1,0:T(8,128)(2,1)S(1)}, u32[]{:S(2)}, u32[]{:S(2)}) collective-permute-start(bf16[128,128]{1,0:T(8,128)(2,1)S(1)} %pad_maximum_fusion.rest_0_), channel_id=1, source_target_pairs={{0,1},{1,0},{2,3},{3,2},{4,5},{5,4},{6,7},{7,6},{8,9},{9,8},{10,11... | collective-permute-start | bytes 98312 | tf_op jit(solution)/shard_map/ppermute | solution.py:497
  16.7 9.4 %all-to-all-start = ((bf16[8,40,128]{2,1,0:T(8,128)(2,1)}), bf16[8,40,128]{2,1,0:T(8,128)(2,1)S(1)}, u32[]{:S(2)}, u32[]{:S(2)}) async-start(bf16[8,40,128]{2,1,0:T(8,128)(2,1)} %bitcast.7), calls=%async_computation | async-start | bytes 163840 | tf_op jit(solution)/shard_map/all_to_all | solution.py:532
  20.1 6.1 %copy-start = (bf16[512,2048]{1,0:T(8,128)(2,1)S(1)}, bf16[512,2048]{1,0:T(8,128)(2,1)}, u32[]{:S(2)}) copy-start(bf16[512,2048]{1,0:T(8,128)(2,1)} %weight_ref.1) | copy-start | bytes 6291460
  27.5 6.6 %collective-permute-start.6 = (bf16[8,512]{1,0:T(8,128)(2,1)S(1)}, bf16[8,512]{1,0:T(8,128)(2,1)S(1)}, u32[]{:S(2)}, u32[]{:S(2)}) collective-permute-start(bf16[8,512]{1,0:T(8,128)(2,1)S(1)} %get-tuple-element.73), channel_id=1, source_target_pairs={{0,24},{8,16},{16,8},{24,0},{1,25},{9,17},{17,9},{25,1},{2,26},{10... | collective-permute-start | bytes 24584 | tf_op jit(solution)/shard_map/ppermute | solution.py:497
  29.9 4.1 %collective-permute-start.5 = (bf16[8,512]{1,0:T(8,128)(2,1)S(1)}, bf16[8,512]{1,0:T(8,128)(2,1)S(1)}, u32[]{:S(2)}, u32[]{:S(2)}) collective-permute-start(bf16[8,512]{1,0:T(8,128)(2,1)S(1)} %get-tuple-element.72), channel_id=1, source_target_pairs={{0,16},{8,24},{16,0},{24,8},{1,17},{9,25},{17,1},{25,9},{2,18},{10... | collective-permute-start | bytes 24584 | tf_op jit(solution)/shard_map/ppermute | solution.py:497
  30.4 3.7 %collective-permute-start.4 = (bf16[8,512]{1,0:T(8,128)(2,1)S(1)}, bf16[8,512]{1,0:T(8,128)(2,1)S(1)}, u32[]{:S(2)}, u32[]{:S(2)}) collective-permute-start(bf16[8,512]{1,0:T(8,128)(2,1)S(1)} %get-tuple-element.71), channel_id=1, source_target_pairs={{0,8},{8,0},{16,24},{24,16},{1,9},{9,1},{17,25},{25,17},{2,10},{10... | collective-permute-start | bytes 24584 | tf_op jit(solution)/shard_map/ppermute | solution.py:497
